TPU v7x, 32 devices: a whole 2x2x4 slice. The times are simulated.
32 devices in a mesh: groups: 2 (over x), src: 16 (over z, y, core).
Axes of the slice: x: 2, y: 2, z: 4, core: 2. Of those that a mesh axis runs over, the one named last changes fastest.
Arguments:
- src_emb: bfloat16 [8192, 256], P(('groups', 'src')), parts along dimension 0, may hold values from -64 to 64
- dst_emb: bfloat16 [8192, 256], P(('groups', 'src')), parts along dimension 0, may hold values from -64 to 64
- tile_dst: int32 [32, 16], P(('groups', 'src')), parts along dimension 0, may hold values from 0 to 15, as said below
- tile_count: int32 [32], P(('groups', 'src')), parts along dimension 0, may hold values from 1 to 16, 128 in all
- beliefs: bfloat16 [64, 4096], P('groups', 'src'), parts along dimension 0, may hold values from 0.019897461 to 1
- grad_next: bfloat16 [64, 4096], P('groups', 'src'), parts along dimension 0, may hold values from -6 to 6
Outputs:
- next_belief: float32 [64, 4096], P('groups', 'src'), parts along dimension 0
- grad_belief: bfloat16 [64, 4096], P('groups', 'src'), parts along dimension 0
- grad_src: float32 [8192, 256], P(('groups', 'src')), parts along dimension 0
- grad_dst: float32 [8192, 256], P(('groups', 'src')), parts along dimension 0
There are 2 independent parts, one for each index of `groups`. A program takes and returns all parts, laid end to end along the dimension named above; each array names one. Nothing has to cross between parts.
Inputs may be any that keep to these rules, and one draw needn't show every extreme that they name: `tile_dst`: each row holds every destination block exactly once; only its first tile_count entries are listed.
All inputs are finite; a program needn't handle non-finite values. No bound on the sum of `tile_count` on one device may be relied on, other than what follows from the above.
Results may differ from a plain program's by a relative error of at most 0.0057.
Values may be sent and summed in bfloat16 or wider, within the bound.
No kernel may reach another device: no remote copies, remote signals or barrier semaphores. Data moves between devices by JAX's collectives and lax.ppermute only.
A program may use at most 128 MiB of HBM per device.

v0:
```python
import functools

import jax
import jax.numpy as jnp
from jax import lax
from jax.experimental import pallas as pl
from jax.experimental.pallas import tpu as pltpu
from jax.sharding import PartitionSpec as P

f32 = jnp.float32
bf16 = jnp.bfloat16
unlisted = 1e30
mib = 1 << 20


class Grid:
    def __init__(self, n, rows, width, batch):
        bits = n.bit_length() - 1
        row_bits = max(1, bits // 2 - 1)
        self.n, self.rows, self.width, self.batch = n, rows, width, batch
        self.n_row = 1 << row_bits
        self.n_col = n // self.n_row
        self.span = self.n_row * rows
        self.packet = rows + batch
        self.head = (3 * self.n_row + 7) // 8 * 8
        even = range(0, self.n_col, 2)
        self.early = [t for t in even if t & (t - 1) == 0]
        self.late = [t for t in even if t & (t - 1)]
        self.groups = [self.early[2:], [2], [0], self.late]
        both = [group + [t + 1 for t in group] for group in self.groups]
        self.parts = [both[0] + both[1] + both[2], both[3]]
        self.spots = {t: (2 * k + (t & 1), group.index(t & ~1)) for k, group in enumerate(self.groups) for t in both[k]}
        top = self.n_col // 2
        self.far = [t for t in range(top, self.n_col, 2)]
        self.near = [t for t in range(0, top, 2)]

    def row_flip(self, s):
        return s * self.n_col

    def where(self, t):
        part = 0 if t in self.parts[0] else 1
        return part, self.parts[part].index(t)


def low_bit(t):
    return t & -t


def dot(a, b, dims):
    return lax.dot_general(a, b, (dims, ((), ())), preferred_element_type=f32)


NN = ((1,), (0,))
NT = ((1,), (1,))
TN = ((0,), (0,))


def in_vmem():
    return pl.BlockSpec(memory_space=pltpu.VMEM)


def anywhere():
    return pl.BlockSpec(memory_space=pl.ANY)


def in_smem():
    return pl.BlockSpec(memory_space=pltpu.SMEM)


shape = jax.ShapeDtypeStruct


def call(name, kernel, out_shape, operands, after=(), scratch=(), limit=8 * mib):
    many = isinstance(out_shape, tuple)
    return pl.pallas_call(
        kernel,
        out_shape=out_shape,
        in_specs=[in_vmem()] * len(operands) + [anywhere()] * len(after),
        out_specs=(in_vmem(),) * len(out_shape) if many else in_vmem(),
        scratch_shapes=list(scratch),
        compiler_params=pltpu.CompilerParams(vmem_limit_bytes=limit),
        name=name,
    )(*operands, *after)


def pack_kernel(g, tile_ref, count_ref, src_ref, bel_ref, dst_ref, grad_ref, src_pack, dst_pack, flags):
    rows, batch = g.rows, g.batch
    me = lax.axis_index("src")
    count = jnp.broadcast_to(count_ref[...], (1, g.width))
    for k in range(g.n):
        flags[pl.ds(tile_ref[0, k] ^ me, 1), :] = jnp.where(count > k, 1.0, 0.0).astype(f32)
    src_pack[:rows] = src_ref[...]
    src_pack[rows : rows + batch] = bel_ref[...]
    src_pack[rows + batch :] = flags[...].astype(bf16)
    dst_pack[:rows] = dst_ref[...]
    dst_pack[rows:] = grad_ref[...]


def pack(g, tile_dst, tile_count, src_emb, beliefs, dst_emb, grad_next):
    return pl.pallas_call(
        functools.partial(pack_kernel, g),
        out_shape=(
            shape((g.rows + g.batch + g.n, g.width), bf16),
            shape((g.rows + g.batch, g.width), bf16),
        ),
        in_specs=[in_smem()] + [in_vmem()] * 5,
        out_specs=(in_vmem(),) * 2,
        scratch_shapes=[pltpu.VMEM((g.n, g.width), f32)],
        compiler_params=pltpu.CompilerParams(vmem_limit_bytes=60 * mib),
        name="pack",
    )(tile_dst, tile_count.reshape(1, 1), src_emb, beliefs, dst_emb, grad_next)


def keep(src_pack, dst_pack, *after):
    def kernel(src_ref, dst_ref, *refs):
        refs[-2][...] = src_ref[...]
        refs[-1][...] = dst_ref[...]

    outs = (shape(src_pack.shape, bf16), shape(dst_pack.shape, bf16))
    return call("keep", kernel, outs, [src_pack, dst_pack], after, limit=2 * mib)


def hand(one, *after):
    def kernel(one_ref, *refs):
        refs[-1][...] = one_ref[...]

    return call("hand", kernel, shape(one.shape, one.dtype), [one], after, limit=2 * mib)


def paired(block, small, *after):
    def kernel(block_ref, small_ref, *refs):
        refs[-1][: block.shape[0]] = block_ref[...]
        refs[-1][block.shape[0] :] = small_ref[...]

    out = shape((block.shape[0] + small.shape[0], block.shape[1]), bf16)
    return call("paired", kernel, out, [block, small], after, limit=2 * mib)


def stack(packs, *after):
    def kernel(*refs):
        for i in range(len(packs)):
            refs[-1][i] = refs[i][...]

    out = shape((len(packs),) + packs[0].shape, packs[0].dtype)
    return call("stack", kernel, out, packs, after)


def score_kernel(g, row_slots, slots, *refs):
    rows, batch, span = g.rows, g.batch, len(row_slots) * g.rows
    src_packs, stacks = refs[: len(row_slots)], refs[len(row_slots) :]
    prob_ref, grad_sum, stats, src_all, bel_all = refs[-5:]
    first = g.spots[slots[0]][0]
    listed = []
    for p, one in enumerate(src_packs):
        lanes = slice(p * rows, (p + 1) * rows)
        src_all[lanes] = one[:rows]
        bel_all[:, lanes] = one[rows : rows + batch]
        listed.append((one[rows + batch :].astype(f32) - 1.0) * unlisted)

    def packet(t):
        stack, place = g.spots[t]
        return stacks[stack - first].at[place]

    top = jnp.full((8, span), -unlisted, f32)
    for i, t in enumerate(slots):
        flips = [g.row_flip(s) | t for s in row_slots]
        bias = jnp.concatenate([one[v : v + 1] for one, v in zip(listed, flips)], axis=1)
        logits = dot(packet(t)[:rows], src_all[...], NT) + bias
        prob_ref[i * rows : (i + 1) * rows] = logits
        top = jnp.maximum(top, jnp.max(logits.reshape(rows // 8, 8, span), axis=0))
    top = jnp.max(top, axis=0, keepdims=True)
    total = jnp.zeros((8, span), f32)
    grad_sum[...] = jnp.zeros(grad_sum.shape, f32)
    for i, t in enumerate(slots):
        here = slice(i * rows, (i + 1) * rows)
        prob = jnp.exp(prob_ref[here] - top)
        prob_ref[here] = prob
        grad_sum[...] += dot(packet(t)[rows:], prob.astype(bf16), NN)
        total = total + jnp.sum(prob.reshape(rows // 8, 8, span), axis=0)
    stats[0:1] = top
    stats[1:2] = jnp.sum(total, axis=0, keepdims=True)
    stats[2:3] = jnp.sum(bel_all[...].astype(f32) * grad_sum[...], axis=0, keepdims=True)


def scores(g, row_slots, slots, src_packs, stacks, *after):
    tall, span = len(slots) * g.rows, len(row_slots) * g.rows
    outs = (shape((tall, span), f32), shape((g.batch, span), f32), shape((3, span), f32))
    scratch = [pltpu.VMEM((span, g.width), bf16), pltpu.VMEM((g.batch, span), bf16)]
    kernel = functools.partial(score_kernel, g, row_slots, slots)
    operands = [*[src_packs[s] for s in row_slots], *stacks]
    return call("scores", kernel, outs, operands, after, scratch, tall * span * 8 + 6 * mib)


def flat(parts):
    return [one for part in parts for one in part]


def unflat(refs, parts):
    out = []
    for part in parts:
        out.append(refs[: len(part)])
        refs = refs[len(part) :]
    return out, refs


def wide(refs, here=slice(None)):
    return jnp.concatenate([one[here] for one in refs], axis=1)


def merged(stats):
    tops = [one[0:1] for one in stats]
    top = functools.reduce(jnp.maximum, tops)
    factors = [jnp.exp(one - top) for one in tops]
    total = sum(factor * one[1:2] for factor, one in zip(factors, stats))
    dots = sum(factor * one[2:3] for factor, one in zip(factors, stats))
    return top, total, dots


def join(g, stats):
    def kernel(*refs):
        out = refs[-1]
        parts, _ = unflat(refs, stats)
        for kind, value in enumerate(merged([wide(one) for one in parts])):
            for s in range(g.n_row):
                at = kind * g.n_row + s
                out[at : at + 1] = value[:, s * g.rows : (s + 1) * g.rows]
        if g.head > 3 * g.n_row:
            out[3 * g.n_row :] = jnp.zeros((g.head - 3 * g.n_row, g.rows), f32)

    return call("join", kernel, shape((g.head, g.rows), f32), flat(stats), limit=2 * mib)


def stage(g, src_packs, stacks):
    rows, batch = g.rows, g.batch

    def kernel(*refs):
        src_refs, stack_refs = refs[: g.n_row], refs[g.n_row : -4]
        src_all, bel_all, *prob_grads = refs[-4:]
        for s, one in enumerate(src_refs):
            lanes = slice(s * rows, (s + 1) * rows)
            src_all[lanes] = one[:rows]
            bel_all[:, lanes] = one[rows : rows + batch]
        for slots, out in zip(g.parts, prob_grads):
            for i, t in enumerate(slots):
                stack, place = g.spots[t]
                out[i * rows : (i + 1) * rows] = dot(stack_refs[stack][place, rows:], bel_all[...], TN)

    outs = (
        shape((g.span, g.width), bf16),
        shape((batch, g.span), bf16),
        *[shape((len(part) * rows, g.span), f32) for part in g.parts],
    )
    limit = g.n * rows * rows * 4 + 8 * mib
    return call("stage", kernel, outs, [*src_packs, *stacks], limit=limit)


def norms(g, stats, grad_sums, messages):
    def kernel(*refs):
        part_stats, refs = unflat(refs, stats)
        part_sums, refs = unflat(refs, grad_sums)
        everyone, (factors, belief_sum) = refs[: g.n_row], refs[-2:]
        part_stats = [wide(one) for one in part_stats]
        for s in range(g.n_row):
            lanes = slice(s * g.rows, (s + 1) * g.rows)

            def row(u, kind):
                at = kind * g.n_row + (s ^ u)
                return everyone[u][at : at + 1]

            tops = [row(u, 0) for u in range(g.n_row)]
            top = functools.reduce(jnp.maximum, tops)
            shares = [jnp.exp(one - top) for one in tops]
            inverse = 1.0 / sum(share * row(u, 1) for u, share in enumerate(shares))
            for part, one in enumerate(part_stats):
                factors[part : part + 1, lanes] = jnp.exp(one[0:1, lanes] - top) * inverse
            dots = sum(share * row(u, 2) for u, share in enumerate(shares))
            factors[2:3, lanes] = dots * inverse
        belief_sum[...] = wide(part_sums[0]) * factors[0:1] + wide(part_sums[1]) * factors[1:2]

    outs = (shape((8, g.span), f32), shape((g.batch, g.span), f32))
    return call("norms", kernel, outs, [*flat(stats), *flat(grad_sums), *messages], limit=4 * mib)


def column_shares(g, slots, kind, factors, probs, prob_grads, src_all, bel_all, *after):
    rows = g.rows

    def kernel(factors, *refs):
        prob_refs, refs = unflat(refs, probs)
        prob_grads, (src_all, bel_all), (change_ref, share_ref) = refs[:2], refs[2:4], refs[-2:]
        for i, t in enumerate(slots):
            part, place = g.where(t)
            here = slice(place * rows, (place + 1) * rows)
            prob = wide(prob_refs[part], here) * factors[part : part + 1]
            change = (prob * (prob_grads[part][here] - factors[2:3])).astype(bf16)
            change_ref[i * rows : (i + 1) * rows] = change
            share_ref[i, :rows] = dot(change, src_all[...], NN).astype(kind)
            share_ref[i, rows:] = dot(bel_all[...], prob.astype(bf16), NT).astype(kind)

    outs = (
        shape((len(slots) * rows, g.span), bf16),
        shape((len(slots), g.packet, g.width), kind),
    )
    operands = [factors, *flat(probs), *prob_grads, src_all, bel_all]
    return call("column_shares", kernel, outs, operands, after, limit=g.n * rows * rows * 8 + 6 * mib)


def row_shares(g, slots, kind, changes, order, stacks, belief_sum, *after):
    rows = g.rows

    def kernel(*refs):
        changes = refs[: len(order)]
        stack_refs = refs[len(order) : len(order) + len(stacks)]
        belief_sum = refs[len(order) + len(stacks)]
        for s, out in zip(slots, refs[-len(slots) :]):
            lanes = slice(s * rows, (s + 1) * rows)
            total = 0.0
            for change, columns in zip(changes, order):
                for i, t in enumerate(columns):
                    stack, place = g.spots[t]
                    packet = stack_refs[stack][place, :rows]
                    total = total + dot(change[i * rows : (i + 1) * rows, lanes], packet, TN)
            out[:rows] = total.astype(kind)
            out[rows:] = belief_sum[:, lanes].astype(kind)

    outs = (shape((g.packet, g.width), kind),) * len(slots)
    operands = [*changes, *stacks, belief_sum]
    return call("row_shares", kernel, outs, operands, after, limit=g.n * rows * rows * 4 + 6 * mib)


def fold(own, near, i, others, *after):
    def kernel(own_ref, near_ref, *refs):
        total = own_ref[i] + near_ref[i].astype(f32)
        for one in refs[: len(others)]:
            total = total + one[...].astype(f32)
        refs[-1][...] = total.astype(bf16)

    return call("fold", kernel, shape(own.shape[1:], bf16), [own, near, *others], after)


def totals(g, src_own, src_others, dst_own, dst_near, dst_others):
    def kernel(*refs):
        src_out, belief_out, dst_out, next_out = refs[-4:]
        src_refs, dst_refs = refs[: 1 + len(src_others)], refs[1 + len(src_others) : -4]

        def added(out, here, own, others):
            total = own[here] + sum(one[here].astype(f32) for one in others)
            out[...] = total.astype(out.dtype)

        big, small = slice(0, g.rows), slice(g.rows, g.packet)
        dst_refs = [dst_refs[0].at[0], dst_refs[1].at[0], *dst_refs[2:]]
        added(src_out, big, src_refs[0], src_refs[1:])
        added(belief_out, small, src_refs[0], src_refs[1:])
        added(dst_out, big, dst_refs[0], dst_refs[1:])
        added(next_out, small, dst_refs[0], dst_refs[1:])

    outs = (
        shape((g.rows, g.width), f32),
        shape((g.batch, g.rows), bf16),
        shape((g.rows, g.width), f32),
        shape((g.batch, g.rows), f32),
    )
    operands = [src_own, *src_others, dst_own, dst_near, *dst_others]
    return call("totals", kernel, outs, operands, limit=12 * mib)


def per_device(n, src_emb, dst_emb, tile_dst, tile_count, beliefs, grad_next):
    g = Grid(n, *src_emb.shape, beliefs.shape[0])

    def swap(array, flip):
        return lax.ppermute(array, "src", [(i, i ^ flip) for i in range(n)])

    raw = {t: (swap(dst_emb, t), swap(grad_next, t)) for t in g.early[2:]}
    src_pack, dst_pack = pack(g, tile_dst, tile_count, src_emb, beliefs, dst_emb, grad_next)
    src_others = [swap(src_pack, g.row_flip(s)) for s in range(1, g.n_row)]
    packets = {2: swap(dst_pack, 2)}
    for t, (block, small) in raw.items():
        packets[t] = paired(block, small)
    src_kept, packets[0] = keep(src_pack, dst_pack, *[packets[t] for t in raw])
    src_packs = [src_kept] + src_others
    for t in sorted(g.late, key=lambda t: bin(t).count("1")):
        packets[t] = swap(packets[t ^ low_bit(t)], low_bit(t))
    stacks = []
    for slots in g.groups:
        pile = stack([packets[t] for t in slots], *(src_others if slots is g.late else ()))
        stacks += [pile, swap(pile, 1)]

    everyone = list(range(g.n_row))
    scored = [scores(g, everyone, g.parts[0], src_packs, stacks[:-2])]
    scored.append(scores(g, everyone, g.parts[1], src_packs, stacks[-2:], scored[0][2]))
    probs, grad_sums, stats = ([[one] for one in each] for each in zip(*scored))
    message = join(g, stats)
    messages = [message] + [swap(message, g.row_flip(s)) for s in range(1, g.n_row)]
    src_all, bel_all, *prob_grads = stage(g, src_packs, stacks)
    factors, belief_sum = norms(g, stats, grad_sums, messages)

    def columns(slots, kind, *after):
        return column_shares(g, slots, kind, factors, probs, prob_grads, src_all, bel_all, *after)

    odd_far, odd_near = ([t + 1 for t in slots] for slots in (g.far, g.near))
    change_of_far_odd, far_send = columns(odd_far, bf16)
    far_got = swap(far_send, 1)
    change_of_far, far_own = columns(g.far, f32, far_send)
    change_of_near_odd, near_send = columns(odd_near, bf16, far_own)
    near_got = swap(near_send, 1)
    change_of_near, near_own = columns(g.near, f32, near_send)
    changes = [change_of_far_odd, change_of_far, change_of_near_odd, change_of_near]
    order = [odd_far, g.far, odd_near, g.near]

    got = {t: [] for t in range(0, g.n_col, 2)}
    last = near_send
    for t in reversed(range(2, g.n_col, 2)):
        own, near, slots = (far_own, far_got, g.far) if t in g.far else (near_own, near_got, g.near)
        send = fold(own, near, slots.index(t), got[t], last)
        one = swap(send, low_bit(t))
        got[t ^ low_bit(t)].append(hand(one) if low_bit(t) > 2 else one)
        if t == g.n_col - 2:
            rest = list(range(1, g.n_row))
            src_send = row_shares(g, rest, bf16, changes, order, stacks, belief_sum, send)
            src_got = [swap(one, g.row_flip(s)) for one, s in zip(src_send, rest)]
        elif t == 4:
            (src_own,) = row_shares(g, [0], f32, changes, order, stacks, belief_sum, send)
            send = src_own
        last = send
    grad_src, grad_belief, grad_dst, next_belief = totals(
        g, src_own, src_got, near_own, near_got, got[0]
    )
    return (next_belief, grad_belief, grad_src, grad_dst)


def solution(mesh):
    placed = (
        P(("groups", "src"), None),
        P(("groups", "src"), None),
        P(("groups", "src"), None),
        P(("groups", "src")),
        P("groups", "src"),
        P("groups", "src"),
    )
    return jax.shard_map(
        functools.partial(per_device, mesh.shape["src"]),
        mesh=mesh,
        in_specs=placed,
        out_specs=(
            P("groups", "src"),
            P("groups", "src"),
            P(("groups", "src"), None),
            P(("groups", "src"), None),
        ),
        check_vma=False,
    )
```

profile of v0, /device:TPU:0, one launch (start us, length us, event | category | flops | bytes accessed | tf_op | source)
XLA Modules:
  0.0 40.7 jit_solution(6052878033306512283)
XLA Ops:
  0.6 3.1 %collective-permute-start = (bf16[256,256]{1,0:T(8,128)(2,1)}, bf16[256,256]{1,0:T(8,128)(2,1)S(1)}, u32[]{:S(2)}, u32[]{:S(2)}) collective-permute-start(bf16[256,256]{1,0:T(8,128)(2,1)} %dst_ref.1), channel_id=1, source_target_pairs={{0,4},{1,5},{2,6},{3,7},{4,0},{5,1},{6,2},{7,3},{8,12},{9,13},{10,... | collective-permute-start | bytes 393224 | tf_op jit(solution)/shard_map/ppermute | solution.py:370
  4.5 1.8 %pack.1 = (bf16[304,256]{1,0:T(8,128)(2,1)}, bf16[288,256]{1,0:T(8,128)(2,1)}) custom-call(s32[1,16]{1,0:T(1,128)} %tile_ref.1, s32[1,1]{1,0:T(1,128)} %bitcast.1.count_ref, bf16[256,256]{1,0:T(8,128)(2,1)} %src_ref.1, bf16[32,256]{1,0:T(8,128)(2,1)} %bel_ref.1, bf16[256,256]{1,0:T(8,128)(2,1)} %dst_ref.1, bf16[32,256]{1,0:T(8,128)(2,1)} %grad_ref.1), custom_call_target="tpu_custom_call" | custom-call | tf_op jit(solution)/shard_map/pack/pallas_call | solution.py:100
  6.2 3.0 %collective-permute-start.2 = (bf16[304,256]{1,0:T(8,128)(2,1)}, bf16[304,256]{1,0:T(8,128)(2,1)S(1)}, u32[]{:S(2)}, u32[]{:S(2)}) collective-permute-start(bf16[304,256]{1,0:T(8,128)(2,1)} %get-tuple-element.32.src_ref), channel_id=1, source_target_pairs={{0,8},{1,9},{2,10},{3,11},{4,12},{5,13},{6,14},{7,15},{8,0},{9,1},... | collective-permute-start | bytes 466952 | tf_op jit(solution)/shard_map/ppermute | solution.py:370
  9.2 1.5 %collective-permute-start.4 = (bf16[288,256]{1,0:T(8,128)(2,1)}, bf16[288,256]{1,0:T(8,128)(2,1)S(1)}, u32[]{:S(2)}, u32[]{:S(2)}) collective-permute-start(bf16[288,256]{1,0:T(8,128)(2,1)} %get-tuple-element.33.dst_ref), channel_id=1, source_target_pairs={{0,2},{1,3},{2,0},{3,1},{4,6},{5,7},{6,4},{7,5},{8,10},{9,11},{10,... | collective-permute-start | bytes 442376 | tf_op jit(solution)/shard_map/ppermute | solution.py:370
  10.7 0.6 %collective-permute-start.7 = (bf16[288,256]{1,0:T(8,128)(2,1)S(1)}, bf16[288,256]{1,0:T(8,128)(2,1)S(1)}, u32[]{:S(2)}, u32[]{:S(2)}) collective-permute-start(bf16[288,256]{1,0:T(8,128)(2,1)S(1)} %paired.1.refs_0_), channel_id=1, source_target_pairs={{0,2},{1,3},{2,0},{3,1},{4,6},{5,7},{6,4},{7,5},{8,10},{9,11},{10,... | collective-permute-start | bytes 442376 | tf_op jit(solution)/shard_map/ppermute | solution.py:370
  11.3 0.9 %copy-done = bf16[304,256]{1,0:T(8,128)(2,1)S(1)} copy-done((bf16[304,256]{1,0:T(8,128)(2,1)S(1)}, bf16[304,256]{1,0:T(8,128)(2,1)}, u32[]{:S(2)}) %copy-start) | copy-done | bytes 155672
  12.2 0.9 %copy-done.1 = bf16[288,256]{1,0:T(8,128)(2,1)S(1)} copy-done((bf16[288,256]{1,0:T(8,128)(2,1)S(1)}, bf16[288,256]{1,0:T(8,128)(2,1)}, u32[]{:S(2)}) %copy-start.1) | copy-done | bytes 147480
  13.2 0.5 %collective-permute-start.3 = (bf16[1,288,256]{2,1,0:T(8,128)(2,1)S(1)}, bf16[1,288,256]{2,1,0:T(8,128)(2,1)S(1)}, u32[]{:S(2)}, u32[]{:S(2)}) collective-permute-start(bf16[1,288,256]{2,1,0:T(8,128)(2,1)S(1)} %stack.4.refs_2_.refs_4_), channel_id=1, source_target_pairs={{0,1},{1,0},{2,3},{3,2},{4,5},{5,4},{6,7},{7,6},{8,9},{9,8},{10,11... | collective-permute-start | bytes 442376 | tf_op jit(solution)/shard_map/ppermute | solution.py:370
  13.7 2.0 %collective-permute-done.4.refs_0_ = bf16[288,256]{1,0:T(8,128)(2,1)S(1)} collective-permute-done((bf16[288,256]{1,0:T(8,128)(2,1)}, bf16[288,256]{1,0:T(8,128)(2,1)S(1)}, u32[]{:S(2)}, u32[]{:S(2)}) %collective-permute-start.4) | collective-permute-done | bytes 147488 | tf_op jit(solution)/shard_map/ppermute | solution.py:370
  16.2 1.1 %collective-permute-done.7.refs_0_ = bf16[288,256]{1,0:T(8,128)(2,1)S(1)} collective-permute-done((bf16[288,256]{1,0:T(8,128)(2,1)S(1)}, bf16[288,256]{1,0:T(8,128)(2,1)S(1)}, u32[]{:S(2)}, u32[]{:S(2)}) %collective-permute-start.7) | collective-permute-done | bytes 147488 | tf_op jit(solution)/shard_map/ppermute | solution.py:370
  17.4 1.6 %scores.2 = (f32[1536,512]{1,0:T(8,128)S(1)}, f32[32,512]{1,0:T(8,128)S(1)}, f32[3,512]{1,0:T(4,128)S(1)}) custom-call(bf16[304,256]{1,0:T(8,128)(2,1)S(1)} %get-tuple-element.34.refs_0_, bf16[304,256]{1,0:T(8,128)(2,1)S(1)} %collective-permute-done.2.refs_1_, bf16[1,288,256]{2,1,0:T(8,128)(2,1)S(1)} %stack.4.refs_2_.refs_4_, ...), custom_call_target="tpu_custom_call" | custom-call | tf_op jit(solution)/shard_map/scores/pallas_call | solution.py:75
  19.0 0.7 %scores.3 = (f32[512,512]{1,0:T(8,128)S(1)}, f32[32,512]{1,0:T(8,128)S(1)}, f32[3,512]{1,0:T(4,128)S(1)}) custom-call(bf16[304,256]{1,0:T(8,128)(2,1)S(1)} %get-tuple-element.34.refs_0_, bf16[304,256]{1,0:T(8,128)(2,1)S(1)} %collective-permute-done.2.refs_1_, bf16[1,288,256]{2,1,0:T(8,128)(2,1)S(1)} %stack.7.refs_2_.refs_8_.refs_10_, ...), custom_call_target="tpu_custom_call" | custom-call | tf_op jit(solution)/shard_map/scores/pallas_call | solution.py:75
  20.1 0.7 %stage.1 = (bf16[512,256]{1,0:T(8,128)(2,1)S(1)}, bf16[32,512]{1,0:T(8,128)(2,1)S(1)}, f32[1536,512]{1,0:T(8,128)S(1)}, f32[512,512]{1,0:T(8,128)S(1)}) custom-call(bf16[304,256]{1,0:T(8,128)(2,1)S(1)} %get-tuple-element.34.refs_0_, bf16[304,256]{1,0:T(8,128)(2,1)S(1)} %collective-permute-done.2.refs_1_, bf16[1,288,256]{2,1,0:T(8,128)(2,1)S(1)} %stack.4.refs_2_.refs_4_, ...), custom_call_target="tpu_custom_call" | custom-call | tf_op jit(solution)/shard_map/stage/pallas_call | solution.py:75
  20.8 3.5 %collective-permute-done.9.refs_5_ = f32[8,256]{1,0:T(8,128)S(1)} collective-permute-done((f32[8,256]{1,0:T(8,128)S(1)}, f32[8,256]{1,0:T(8,128)S(1)}, u32[]{:S(2)}, u32[]{:S(2)}) %collective-permute-start.9) | collective-permute-done | bytes 8224 | tf_op jit(solution)/shard_map/ppermute | solution.py:370
  25.3 0.4 %column_shares.6 = (bf16[512,512]{1,0:T(8,128)(2,1)S(1)}, bf16[2,288,256]{2,1,0:T(8,128)(2,1)S(1)}) custom-call(f32[8,512]{1,0:T(8,128)S(1)} %get-tuple-element.40.factors, f32[1536,512]{1,0:T(8,128)S(1)} %get-tuple-element.41.refs_0_, f32[512,512]{1,0:T(8,128)S(1)} %get-tuple-element.42.refs_1_, f32[1536,512]{1,0:T(8,128)S(1)} %get-tuple-element.43.refs_2_, ...), custom_call_target="tpu_custom_call" | custom-call | tf_op jit(solution)/shard_map/column_shares/pallas_call | solution.py:75
  25.8 0.6 %collective-permute-start.13 = (bf16[2,288,256]{2,1,0:T(8,128)(2,1)S(1)}, bf16[2,288,256]{2,1,0:T(8,128)(2,1)S(1)}, u32[]{:S(2)}, u32[]{:S(2)}) collective-permute-start(bf16[2,288,256]{2,1,0:T(8,128)(2,1)S(1)} %get-tuple-element.52.refs_6_.refs_0_), channel_id=1, source_target_pairs={{0,1},{1,0},{2,3},{3,2},{4,5},{5,4},{6,7},{7,6},{8,9},{9,8},{10,11... | collective-permute-start | bytes 884744 | tf_op jit(solution)/shard_map/ppermute | solution.py:370
  26.5 1.6 %collective-permute-start.11 = (bf16[288,256]{1,0:T(8,128)(2,1)S(1)}, bf16[288,256]{1,0:T(8,128)(2,1)S(1)}, u32[]{:S(2)}, u32[]{:S(2)}) collective-permute-start(bf16[288,256]{1,0:T(8,128)(2,1)S(1)} %fold.3.refs_1_.refs_13_), channel_id=1, source_target_pairs={{0,2},{1,3},{2,0},{3,1},{4,6},{5,7},{6,4},{7,5},{8,10},{9,11},{10,... | collective-permute-start | bytes 442376 | tf_op jit(solution)/shard_map/ppermute | solution.py:370
  28.5 0.5 %row_shares.3 = bf16[288,256]{1,0:T(8,128)(2,1)S(1)} custom-call(bf16[512,512]{1,0:T(8,128)(2,1)S(1)} %get-tuple-element.47.refs_0_, bf16[512,512]{1,0:T(8,128)(2,1)S(1)} %get-tuple-element.49.refs_1_, bf16[512,512]{1,0:T(8,128)(2,1)S(1)} %get-tuple-element.51.refs_2_, bf16[512,512]{1,0:T(8,128)(2,1)S(1)} %get-tuple-element.53.refs_3_, ...), custom_call_target="tpu_custom_call" | custom-call | tf_op jit(solution)/shard_map/row_shares/pallas_call | solution.py:75
  29.4 3.0 %collective-permute-done.11.refs_0_ = bf16[288,256]{1,0:T(8,128)(2,1)S(1)} collective-permute-done((bf16[288,256]{1,0:T(8,128)(2,1)S(1)}, bf16[288,256]{1,0:T(8,128)(2,1)S(1)}, u32[]{:S(2)}, u32[]{:S(2)}) %collective-permute-start.11) | collective-permute-done | bytes 147488 | tf_op jit(solution)/shard_map/ppermute | solution.py:370
  32.5 1.6 %collective-permute-start.14 = (bf16[288,256]{1,0:T(8,128)(2,1)S(1)}, bf16[288,256]{1,0:T(8,128)(2,1)S(1)}, u32[]{:S(2)}, u32[]{:S(2)}) collective-permute-start(bf16[288,256]{1,0:T(8,128)(2,1)S(1)} %fold.4.refs_13_), channel_id=1, source_target_pairs={{0,4},{1,5},{2,6},{3,7},{4,0},{5,1},{6,2},{7,3},{8,12},{9,13},{10,... | collective-permute-start | bytes 442376 | tf_op jit(solution)/shard_map/ppermute | solution.py:370
  34.2 0.5 %row_shares.2.refs_0_ = f32[288,256]{1,0:T(8,128)S(1)} custom-call(bf16[512,512]{1,0:T(8,128)(2,1)S(1)} %get-tuple-element.47.refs_0_, bf16[512,512]{1,0:T(8,128)(2,1)S(1)} %get-tuple-element.49.refs_1_, bf16[512,512]{1,0:T(8,128)(2,1)S(1)} %get-tuple-element.51.refs_2_, bf16[512,512]{1,0:T(8,128)(2,1)S(1)} %get-tuple-element.53.refs_3_, ...), custom_call_target="tpu_custom_call" | custom-call | tf_op jit(solution)/shard_map/row_shares/pallas_call | solution.py:75
  34.7 1.6 %collective-permute-start.15 = (bf16[288,256]{1,0:T(8,128)(2,1)S(1)}, bf16[288,256]{1,0:T(8,128)(2,1)S(1)}, u32[]{:S(2)}, u32[]{:S(2)}) collective-permute-start(bf16[288,256]{1,0:T(8,128)(2,1)S(1)} %fold.5), channel_id=1, source_target_pairs={{0,2},{1,3},{2,0},{3,1},{4,6},{5,7},{6,4},{7,5},{8,10},{9,11},{10,... | collective-permute-start | bytes 442376 | tf_op jit(solution)/shard_map/ppermute | solution.py:370
  36.3 3.4 %collective-permute-done.14.one_ref = bf16[288,256]{1,0:T(8,128)(2,1)S(1)} collective-permute-done((bf16[288,256]{1,0:T(8,128)(2,1)S(1)}, bf16[288,256]{1,0:T(8,128)(2,1)S(1)}, u32[]{:S(2)}, u32[]{:S(2)}) %collective-permute-start.14) | collective-permute-done | bytes 147488 | tf_op jit(solution)/shard_map/ppermute | solution.py:370
  39.9 0.8 %totals.1 = (f32[256,256]{1,0:T(8,128)}, bf16[32,256]{1,0:T(8,128)(2,1)}, f32[256,256]{1,0:T(8,128)}, f32[32,256]{1,0:T(8,128)}) custom-call(f32[288,256]{1,0:T(8,128)S(1)} %row_shares.2.refs_0_, bf16[288,256]{1,0:T(8,128)(2,1)S(1)} %collective-permute-done.12.refs_1_, f32[2,288,256]{2,1,0:T(8,128)S(1)} %get-tuple-element.55.own_ref.refs_2_, ...), custom_call_target="tpu_custom_call" | custom-call | tf_op jit(solution)/shard_map/totals/pallas_call | solution.py:75
  (35 shorter events, 3.4 us)
Async XLA Ops:
  0.6 10.1 %collective-permute-start = (bf16[256,256]{1,0:T(8,128)(2,1)}, bf16[256,256]{1,0:T(8,128)(2,1)S(1)}, u32[]{:S(2)}, u32[]{:S(2)}) collective-permute-start(bf16[256,256]{1,0:T(8,128)(2,1)} %dst_ref.1), channel_id=1, source_target_pairs={{0,4},{1,5},{2,6},{3,7},{4,0},{5,1},{6,2},{7,3},{8,12},{9,13},{10,... | collective-permute-start | bytes 393224 | tf_op jit(solution)/shard_map/ppermute | solution.py:370
  3.7 7.0 %collective-permute-start.1 = (bf16[32,256]{1,0:T(8,128)(2,1)}, bf16[32,256]{1,0:T(8,128)(2,1)S(1)}, u32[]{:S(2)}, u32[]{:S(2)}) collective-permute-start(bf16[32,256]{1,0:T(8,128)(2,1)} %grad_ref.1), channel_id=1, source_target_pairs={{0,4},{1,5},{2,6},{3,7},{4,0},{5,1},{6,2},{7,3},{8,12},{9,13},{10,... | collective-permute-start | bytes 49160 | tf_op jit(solution)/shard_map/ppermute | solution.py:370
  6.2 10.0 %collective-permute-start.2 = (bf16[304,256]{1,0:T(8,128)(2,1)}, bf16[304,256]{1,0:T(8,128)(2,1)S(1)}, u32[]{:S(2)}, u32[]{:S(2)}) collective-permute-start(bf16[304,256]{1,0:T(8,128)(2,1)} %get-tuple-element.32.src_ref), channel_id=1, source_target_pairs={{0,8},{1,9},{2,10},{3,11},{4,12},{5,13},{6,14},{7,15},{8,0},{9,1},... | collective-permute-start | bytes 466952 | tf_op jit(solution)/shard_map/ppermute | solution.py:370
  9.2 6.5 %collective-permute-start.4 = (bf16[288,256]{1,0:T(8,128)(2,1)}, bf16[288,256]{1,0:T(8,128)(2,1)S(1)}, u32[]{:S(2)}, u32[]{:S(2)}) collective-permute-start(bf16[288,256]{1,0:T(8,128)(2,1)} %get-tuple-element.33.dst_ref), channel_id=1, source_target_pairs={{0,2},{1,3},{2,0},{3,1},{4,6},{5,7},{6,4},{7,5},{8,10},{9,11},{10,... | collective-permute-start | bytes 442376 | tf_op jit(solution)/shard_map/ppermute | solution.py:370
  10.7 6.6 %collective-permute-start.7 = (bf16[288,256]{1,0:T(8,128)(2,1)S(1)}, bf16[288,256]{1,0:T(8,128)(2,1)S(1)}, u32[]{:S(2)}, u32[]{:S(2)}) collective-permute-start(bf16[288,256]{1,0:T(8,128)(2,1)S(1)} %paired.1.refs_0_), channel_id=1, source_target_pairs={{0,2},{1,3},{2,0},{3,1},{4,6},{5,7},{6,4},{7,5},{8,10},{9,11},{10,... | collective-permute-start | bytes 442376 | tf_op jit(solution)/shard_map/ppermute | solution.py:370
  11.3 0.9 %copy-start = (bf16[304,256]{1,0:T(8,128)(2,1)S(1)}, bf16[304,256]{1,0:T(8,128)(2,1)}, u32[]{:S(2)}) copy-start(bf16[304,256]{1,0:T(8,128)(2,1)} %get-tuple-element.32.src_ref) | copy-start | bytes 466948
  12.2 0.9 %copy-start.1 = (bf16[288,256]{1,0:T(8,128)(2,1)S(1)}, bf16[288,256]{1,0:T(8,128)(2,1)}, u32[]{:S(2)}) copy-start(bf16[288,256]{1,0:T(8,128)(2,1)} %get-tuple-element.33.dst_ref) | copy-start | bytes 442372
  13.2 4.2 %collective-permute-start.6 = (bf16[1,288,256]{2,1,0:T(8,128)(2,1)S(1)}, bf16[1,288,256]{2,1,0:T(8,128)(2,1)S(1)}, u32[]{:S(2)}, u32[]{:S(2)}) collective-permute-start(bf16[1,288,256]{2,1,0:T(8,128)(2,1)S(1)} %stack.6.refs_6_.refs_8_), channel_id=1, source_target_pairs={{0,1},{1,0},{2,3},{3,2},{4,5},{5,4},{6,7},{7,6},{8,9},{9,8},{10,11... | collective-permute-start | bytes 442376 | tf_op jit(solution)/shard_map/ppermute | solution.py:370
  13.2 4.1 %collective-permute-start.3 = (bf16[1,288,256]{2,1,0:T(8,128)(2,1)S(1)}, bf16[1,288,256]{2,1,0:T(8,128)(2,1)S(1)}, u32[]{:S(2)}, u32[]{:S(2)}) collective-permute-start(bf16[1,288,256]{2,1,0:T(8,128)(2,1)S(1)} %stack.4.refs_2_.refs_4_), channel_id=1, source_target_pairs={{0,1},{1,0},{2,3},{3,2},{4,5},{5,4},{6,7},{7,6},{8,9},{9,8},{10,11... | collective-permute-start | bytes 442376 | tf_op jit(solution)/shard_map/ppermute | solution.py:370
  15.7 1.7 %collective-permute-start.5 = (bf16[1,288,256]{2,1,0:T(8,128)(2,1)S(1)}, bf16[1,288,256]{2,1,0:T(8,128)(2,1)S(1)}, u32[]{:S(2)}, u32[]{:S(2)}) collective-permute-start(bf16[1,288,256]{2,1,0:T(8,128)(2,1)S(1)} %stack.5.refs_4_.refs_6_), channel_id=1, source_target_pairs={{0,1},{1,0},{2,3},{3,2},{4,5},{5,4},{6,7},{7,6},{8,9},{9,8},{10,11... | collective-permute-start | bytes 442376 | tf_op jit(solution)/shard_map/ppermute | solution.py:370
  17.3 1.7 %collective-permute-start.8 = (bf16[1,288,256]{2,1,0:T(8,128)(2,1)S(1)}, bf16[1,288,256]{2,1,0:T(8,128)(2,1)S(1)}, u32[]{:S(2)}, u32[]{:S(2)}) collective-permute-start(bf16[1,288,256]{2,1,0:T(8,128)(2,1)S(1)} %stack.7.refs_2_.refs_8_.refs_10_), channel_id=1, source_target_pairs={{0,1},{1,0},{2,3},{3,2},{4,5},{5,4},{6,7},{7,6},{8,9},{9,8},{10,11... | collective-permute-start | bytes 442376 | tf_op jit(solution)/shard_map/ppermute | solution.py:370
  19.7 4.6 %collective-permute-start.9 = (f32[8,256]{1,0:T(8,128)S(1)}, f32[8,256]{1,0:T(8,128)S(1)}, u32[]{:S(2)}, u32[]{:S(2)}) collective-permute-start(f32[8,256]{1,0:T(8,128)S(1)} %join.1.refs_4_), channel_id=1, source_target_pairs={{0,8},{1,9},{2,10},{3,11},{4,12},{5,13},{6,14},{7,15},{8,0},{9,1},... | collective-permute-start | bytes 24584 | tf_op jit(solution)/shard_map/ppermute | solution.py:370
  24.8 1.6 %collective-permute-start.10 = (bf16[2,288,256]{2,1,0:T(8,128)(2,1)S(1)}, bf16[2,288,256]{2,1,0:T(8,128)(2,1)S(1)}, u32[]{:S(2)}, u32[]{:S(2)}) collective-permute-start(bf16[2,288,256]{2,1,0:T(8,128)(2,1)S(1)} %get-tuple-element.48.refs_6_), channel_id=1, source_target_pairs={{0,1},{1,0},{2,3},{3,2},{4,5},{5,4},{6,7},{7,6},{8,9},{9,8},{10,11... | collective-permute-start | bytes 884744 | tf_op jit(solution)/shard_map/ppermute | solution.py:370
  25.8 8.9 %collective-permute-start.13 = (bf16[2,288,256]{2,1,0:T(8,128)(2,1)S(1)}, bf16[2,288,256]{2,1,0:T(8,128)(2,1)S(1)}, u32[]{:S(2)}, u32[]{:S(2)}) collective-permute-start(bf16[2,288,256]{2,1,0:T(8,128)(2,1)S(1)} %get-tuple-element.52.refs_6_.refs_0_), channel_id=1, source_target_pairs={{0,1},{1,0},{2,3},{3,2},{4,5},{5,4},{6,7},{7,6},{8,9},{9,8},{10,11... | collective-permute-start | bytes 884744 | tf_op jit(solution)/shard_map/ppermute | solution.py:370
  26.5 6.0 %collective-permute-start.11 = (bf16[288,256]{1,0:T(8,128)(2,1)S(1)}, bf16[288,256]{1,0:T(8,128)(2,1)S(1)}, u32[]{:S(2)}, u32[]{:S(2)}) collective-permute-start(bf16[288,256]{1,0:T(8,128)(2,1)S(1)} %fold.3.refs_1_.refs_13_), channel_id=1, source_target_pairs={{0,2},{1,3},{2,0},{3,1},{4,6},{5,7},{6,4},{7,5},{8,10},{9,11},{10,... | collective-permute-start | bytes 442376 | tf_op jit(solution)/shard_map/ppermute | solution.py:370
  29.0 10.7 %collective-permute-start.12 = (bf16[288,256]{1,0:T(8,128)(2,1)S(1)}, bf16[288,256]{1,0:T(8,128)(2,1)S(1)}, u32[]{:S(2)}, u32[]{:S(2)}) collective-permute-start(bf16[288,256]{1,0:T(8,128)(2,1)S(1)} %row_shares.3), channel_id=1, source_target_pairs={{0,8},{1,9},{2,10},{3,11},{4,12},{5,13},{6,14},{7,15},{8,0},{9,1},... | collective-permute-start | bytes 442376 | tf_op jit(solution)/shard_map/ppermute | solution.py:370
  32.5 7.2 %collective-permute-start.14 = (bf16[288,256]{1,0:T(8,128)(2,1)S(1)}, bf16[288,256]{1,0:T(8,128)(2,1)S(1)}, u32[]{:S(2)}, u32[]{:S(2)}) collective-permute-start(bf16[288,256]{1,0:T(8,128)(2,1)S(1)} %fold.4.refs_13_), channel_id=1, source_target_pairs={{0,4},{1,5},{2,6},{3,7},{4,0},{5,1},{6,2},{7,3},{8,12},{9,13},{10,... | collective-permute-start | bytes 442376 | tf_op jit(solution)/shard_map/ppermute | solution.py:370
  34.7 5.2 %collective-permute-start.15 = (bf16[288,256]{1,0:T(8,128)(2,1)S(1)}, bf16[288,256]{1,0:T(8,128)(2,1)S(1)}, u32[]{:S(2)}, u32[]{:S(2)}) collective-permute-start(bf16[288,256]{1,0:T(8,128)(2,1)S(1)} %fold.5), channel_id=1, source_target_pairs={{0,2},{1,3},{2,0},{3,1},{4,6},{5,7},{6,4},{7,5},{8,10},{9,11},{10,... | collective-permute-start | bytes 442376 | tf_op jit(solution)/shard_map/ppermute | solution.py:370
where the time goes:
time: 40.9 us; the launch traced here: 40.7 us
  starting transfers between devices  15.1 us (37%)
  waiting for transfers between devices  13.8 us (34%)
  Pallas kernels  8.54 us (21%)
  local copies, waits for them, and re-layouts  1.82 us (4%)
  between operations  1.49 us (4%)
    ppermute x16, starting transfers between devices, swap(): return lax.ppermute(array, 'src', [(i, i ^ flip) for i in range(n)])  15.1 us
    ppermute x16, waiting for transfers between devices, swap(): return lax.ppermute(array, 'src', [(i, i ^ flip) for i in range(n)])  13.8 us
    pallas_call x22, Pallas kernels, call(): pl.pallas_call(kernel, out_shape=out_shape, in_specs=[in_vmem()] * len(op...  6.79 us
    unnamed x4, local copies, waits for them, and re-layouts  1.82 us
    pallas_call x1, Pallas kernels, pack(): pl.pallas_call(functools.partial(pack_kernel, g), out_shape=(shape((g.row...  1.75 us
  transfers between devices with their start and end apart: 16, of which 8 were waited for; matrix products, arithmetic and copies ran while one was open for 0% of the time, Pallas kernels for 16%

commit v1 on v0

--- a/solution.py
+++ b/solution.py
@@ -70,7 +70,7 @@
 shape = jax.ShapeDtypeStruct
 
 
-def call(name, kernel, out_shape, operands, after=(), scratch=(), limit=8 * mib):
+def call(name, kernel, out_shape, operands, after=(), scratch=(), limit=8 * mib, cost=None):
     many = isinstance(out_shape, tuple)
     return pl.pallas_call(
         kernel,
@@ -79,11 +79,12 @@
         out_specs=(in_vmem(),) * len(out_shape) if many else in_vmem(),
         scratch_shapes=list(scratch),
         compiler_params=pltpu.CompilerParams(vmem_limit_bytes=limit),
+        cost_estimate=cost,
         name=name,
     )(*operands, *after)
 
 
-def pack_kernel(g, tile_ref, count_ref, src_ref, bel_ref, dst_ref, grad_ref, src_pack, dst_pack, flags):
+def pack_kernel(g, tile_ref, count_ref, src_ref, bel_ref, dst_ref, grad_ref, src_pack, dst_pack, src_small, flags):
     rows, batch = g.rows, g.batch
     me = lax.axis_index("src")
     count = jnp.broadcast_to(count_ref[...], (1, g.width))
@@ -94,6 +95,8 @@
     src_pack[rows + batch :] = flags[...].astype(bf16)
     dst_pack[:rows] = dst_ref[...]
     dst_pack[rows:] = grad_ref[...]
+    src_small[:batch] = bel_ref[...]
+    src_small[batch:] = flags[...].astype(bf16)
 
 
 def pack(g, tile_dst, tile_count, src_emb, beliefs, dst_emb, grad_next):
@@ -102,9 +105,10 @@
         out_shape=(
             shape((g.rows + g.batch + g.n, g.width), bf16),
             shape((g.rows + g.batch, g.width), bf16),
+            shape((g.batch + g.n, g.width), bf16),
         ),
         in_specs=[in_smem()] + [in_vmem()] * 5,
-        out_specs=(in_vmem(),) * 2,
+        out_specs=(in_vmem(),) * 3,
         scratch_shapes=[pltpu.VMEM((g.n, g.width), f32)],
         compiler_params=pltpu.CompilerParams(vmem_limit_bytes=60 * mib),
         name="pack",
@@ -127,13 +131,13 @@
     return call("hand", kernel, shape(one.shape, one.dtype), [one], after, limit=2 * mib)
 
 
-def paired(block, small, *after):
+def paired(block, small, cost=None):
     def kernel(block_ref, small_ref, *refs):
         refs[-1][: block.shape[0]] = block_ref[...]
         refs[-1][block.shape[0] :] = small_ref[...]
 
     out = shape((block.shape[0] + small.shape[0], block.shape[1]), bf16)
-    return call("paired", kernel, out, [block, small], after, limit=2 * mib)
+    return call("paired", kernel, out, [block, small], limit=2 * mib, cost=cost)
 
 
 def stack(packs, *after):
@@ -188,7 +192,10 @@
     scratch = [pltpu.VMEM((span, g.width), bf16), pltpu.VMEM((g.batch, span), bf16)]
     kernel = functools.partial(score_kernel, g, row_slots, slots)
     operands = [*[src_packs[s] for s in row_slots], *stacks]
-    return call("scores", kernel, outs, operands, after, scratch, tall * span * 8 + 6 * mib)
+    cost = pl.CostEstimate(
+        flops=2 * tall * span * (g.width + g.batch), bytes_accessed=8 * tall * span, transcendentals=tall * span
+    )
+    return call("scores", kernel, outs, operands, after, scratch, tall * span * 8 + 6 * mib, cost)
 
 
 def flat(parts):
@@ -369,13 +376,14 @@
     def swap(array, flip):
         return lax.ppermute(array, "src", [(i, i ^ flip) for i in range(n)])
 
-    raw = {t: (swap(dst_emb, t), swap(grad_next, t)) for t in g.early[2:]}
-    src_pack, dst_pack = pack(g, tile_dst, tile_count, src_emb, beliefs, dst_emb, grad_next)
-    src_others = [swap(src_pack, g.row_flip(s)) for s in range(1, g.n_row)]
-    packets = {2: swap(dst_pack, 2)}
-    for t, (block, small) in raw.items():
-        packets[t] = paired(block, small)
-    src_kept, packets[0] = keep(src_pack, dst_pack, *[packets[t] for t in raw])
+    raw = {t: (swap(dst_emb, t), swap(grad_next, t)) for t in reversed(g.early[1:])}
+    raw_src = [swap(src_emb, g.row_flip(s)) for s in range(1, g.n_row)]
+    src_pack, dst_pack, src_small = pack(g, tile_dst, tile_count, src_emb, beliefs, dst_emb, grad_next)
+    small = [swap(src_small, g.row_flip(s)) for s in range(1, g.n_row)]
+    moved = pl.CostEstimate(flops=2 << 30, bytes_accessed=1 << 20, transcendentals=0)
+    src_others = [paired(*pair, moved) for pair in zip(raw_src, small)]
+    packets = {t: paired(*pair) for t, pair in raw.items()}
+    src_kept, packets[0] = keep(src_pack, dst_pack, *[packets[t] for t in g.early[2:]])
     src_packs = [src_kept] + src_others
     for t in sorted(g.late, key=lambda t: bin(t).count("1")):
         packets[t] = swap(packets[t ^ low_bit(t)], low_bit(t))

time: 40.9 us -> 41.5 us (1.015)
  starting transfers between devices: 15.1 us -> 20.3 us
  waiting for transfers between devices: 13.8 us -> 9.07 us
    ppermute x16 -> x18, starting transfers between devices: 15.1 us -> 20.3 us  [swap(): return lax.ppermute(array, 'src', [(i, i ^ flip) for i in range(n)])]
    ppermute x16 -> x18, waiting for transfers between devices: 13.8 us -> 9.07 us  [swap(): return lax.ppermute(array, 'src', [(i, i ^ flip) for i in range(n)])]
    pallas_call x22 -> x24, Pallas kernels: 6.79 us -> 6.82 us  [call(): pl.pallas_call(kernel, out_shape=out_shape, in_specs=[in_vmem()] * len(op...]
  transfers between devices with their start and end apart: 16 -> 18, of which waited for: 8 -> 7; matrix products, arithmetic and copies ran while one was open for 0% -> 0% of each run, Pallas kernels for 16% -> 16%
where the time goes in v1:
time: 41.5 us; the launch traced here: 41.3 us
  starting transfers between devices  20.3 us (49%)
  waiting for transfers between devices  9.07 us (22%)
  Pallas kernels  8.58 us (21%)
  local copies, waits for them, and re-layouts  1.82 us (4%)
  between operations  1.51 us (4%)
    ppermute x18, starting transfers between devices, swap(): return lax.ppermute(array, 'src', [(i, i ^ flip) for i in range(n)])  20.3 us
    ppermute x18, waiting for transfers between devices, swap(): return lax.ppermute(array, 'src', [(i, i ^ flip) for i in range(n)])  9.07 us
    pallas_call x24, Pallas kernels, call(): pl.pallas_call(kernel, out_shape=out_shape, in_specs=[in_vmem()] * len(op...  6.82 us
    unnamed x4, local copies, waits for them, and re-layouts  1.82 us
    pallas_call x1, Pallas kernels, pack(): pl.pallas_call(functools.partial(pack_kernel, g), out_shape=(shape((g.row...  1.75 us
  transfers between devices with their start and end apart: 18, of which 7 were waited for; matrix products, arithmetic and copies ran while one was open for 0% of the time, Pallas kernels for 16%

profile of v1, /device:TPU:0, one launch (start us, length us, event | category | flops | bytes accessed | tf_op | source)
XLA Modules:
  0.0 41.3 jit_solution(17600864722402346094)
XLA Ops:
  0.6 3.1 %collective-permute-start = (bf16[256,256]{1,0:T(8,128)(2,1)}, bf16[256,256]{1,0:T(8,128)(2,1)S(1)}, u32[]{:S(2)}, u32[]{:S(2)}) collective-permute-start(bf16[256,256]{1,0:T(8,128)(2,1)} %dst_ref.1), channel_id=1, source_target_pairs={{0,4},{1,5},{2,6},{3,7},{4,0},{5,1},{6,2},{7,3},{8,12},{9,13},{10,... | collective-permute-start | bytes 393224 | tf_op jit(solution)/shard_map/ppermute | solution.py:377
  3.7 1.5 %collective-permute-start.5 = (bf16[256,256]{1,0:T(8,128)(2,1)}, bf16[256,256]{1,0:T(8,128)(2,1)S(1)}, u32[]{:S(2)}, u32[]{:S(2)}) collective-permute-start(bf16[256,256]{1,0:T(8,128)(2,1)} %dst_ref.1), channel_id=1, source_target_pairs={{0,2},{1,3},{2,0},{3,1},{4,6},{5,7},{6,4},{7,5},{8,10},{9,11},{10,... | collective-permute-start | bytes 393224 | tf_op jit(solution)/shard_map/ppermute | solution.py:377
  5.2 2.6 %collective-permute-start.2 = (bf16[256,256]{1,0:T(8,128)(2,1)}, bf16[256,256]{1,0:T(8,128)(2,1)S(1)}, u32[]{:S(2)}, u32[]{:S(2)}) collective-permute-start(bf16[256,256]{1,0:T(8,128)(2,1)} %src_ref.1), channel_id=1, source_target_pairs={{0,8},{1,9},{2,10},{3,11},{4,12},{5,13},{6,14},{7,15},{8,0},{9,1},... | collective-permute-start | bytes 393224 | tf_op jit(solution)/shard_map/ppermute | solution.py:377
  8.9 1.8 %pack.1 = (bf16[304,256]{1,0:T(8,128)(2,1)}, bf16[288,256]{1,0:T(8,128)(2,1)}, bf16[48,256]{1,0:T(8,128)(2,1)}) custom-call(s32[1,16]{1,0:T(1,128)} %tile_ref.1, s32[1,1]{1,0:T(1,128)} %bitcast.1.count_ref, bf16[256,256]{1,0:T(8,128)(2,1)} %src_ref.1, bf16[32,256]{1,0:T(8,128)(2,1)} %bel_ref.1, bf16[256,256]{1,0:T(8,128)(2,1)} %dst_ref.1, ...), custom_call_target="tpu_custom_call" | custom-call | tf_op jit(solution)/shard_map/pack/pallas_call | solution.py:103
  11.0 0.8 %collective-permute-done.1.small_ref = bf16[32,256]{1,0:T(8,128)(2,1)S(1)} collective-permute-done((bf16[32,256]{1,0:T(8,128)(2,1)}, bf16[32,256]{1,0:T(8,128)(2,1)S(1)}, u32[]{:S(2)}, u32[]{:S(2)}) %collective-permute-start.1) | collective-permute-done | bytes 16416 | tf_op jit(solution)/shard_map/ppermute | solution.py:377
  11.8 0.7 %collective-permute-start.6 = (bf16[32,256]{1,0:T(8,128)(2,1)}, bf16[32,256]{1,0:T(8,128)(2,1)S(1)}, u32[]{:S(2)}, u32[]{:S(2)}) collective-permute-start(bf16[32,256]{1,0:T(8,128)(2,1)} %grad_ref.1), channel_id=1, source_target_pairs={{0,2},{1,3},{2,0},{3,1},{4,6},{5,7},{6,4},{7,5},{8,10},{9,11},{10,... | collective-permute-start | bytes 49160 | tf_op jit(solution)/shard_map/ppermute | solution.py:377
  12.5 1.4 %collective-permute-start.9 = (bf16[288,256]{1,0:T(8,128)(2,1)S(1)}, bf16[288,256]{1,0:T(8,128)(2,1)S(1)}, u32[]{:S(2)}, u32[]{:S(2)}) collective-permute-start(bf16[288,256]{1,0:T(8,128)(2,1)S(1)} %paired.3.refs_0_), channel_id=1, source_target_pairs={{0,2},{1,3},{2,0},{3,1},{4,6},{5,7},{6,4},{7,5},{8,10},{9,11},{10,... | collective-permute-start | bytes 442376 | tf_op jit(solution)/shard_map/ppermute | solution.py:377
  13.9 0.9 %copy-done = bf16[304,256]{1,0:T(8,128)(2,1)S(1)} copy-done((bf16[304,256]{1,0:T(8,128)(2,1)S(1)}, bf16[304,256]{1,0:T(8,128)(2,1)}, u32[]{:S(2)}) %copy-start) | copy-done | bytes 155672
  14.8 0.9 %copy-done.1 = bf16[288,256]{1,0:T(8,128)(2,1)S(1)} copy-done((bf16[288,256]{1,0:T(8,128)(2,1)S(1)}, bf16[288,256]{1,0:T(8,128)(2,1)}, u32[]{:S(2)}) %copy-start.1) | copy-done | bytes 147480
  15.9 0.5 %collective-permute-start.4 = (bf16[1,288,256]{2,1,0:T(8,128)(2,1)S(1)}, bf16[1,288,256]{2,1,0:T(8,128)(2,1)S(1)}, u32[]{:S(2)}, u32[]{:S(2)}) collective-permute-start(bf16[1,288,256]{2,1,0:T(8,128)(2,1)S(1)} %stack.4.refs_2_.refs_4_), channel_id=1, source_target_pairs={{0,1},{1,0},{2,3},{3,2},{4,5},{5,4},{6,7},{7,6},{8,9},{9,8},{10,11... | collective-permute-start | bytes 442376 | tf_op jit(solution)/shard_map/ppermute | solution.py:377
  16.6 1.1 %collective-permute-done.9.refs_0_ = bf16[288,256]{1,0:T(8,128)(2,1)S(1)} collective-permute-done((bf16[288,256]{1,0:T(8,128)(2,1)S(1)}, bf16[288,256]{1,0:T(8,128)(2,1)S(1)}, u32[]{:S(2)}, u32[]{:S(2)}) %collective-permute-start.9) | collective-permute-done | bytes 147488 | tf_op jit(solution)/shard_map/ppermute | solution.py:377
  17.9 1.6 %scores.2 = (f32[1536,512]{1,0:T(8,128)S(1)}, f32[32,512]{1,0:T(8,128)S(1)}, f32[3,512]{1,0:T(4,128)S(1)}) custom-call(bf16[304,256]{1,0:T(8,128)(2,1)S(1)} %get-tuple-element.35.refs_0_, bf16[304,256]{1,0:T(8,128)(2,1)S(1)} %paired.4.refs_1_, bf16[1,288,256]{2,1,0:T(8,128)(2,1)S(1)} %stack.4.refs_2_.refs_4_, ...), custom_call_target="tpu_custom_call" | custom-call | flops 452984832 | bytes 6291456 | tf_op jit(solution)/shard_map/scores/pallas_call | solution.py:75
  19.5 0.7 %scores.3 = (f32[512,512]{1,0:T(8,128)S(1)}, f32[32,512]{1,0:T(8,128)S(1)}, f32[3,512]{1,0:T(4,128)S(1)}) custom-call(bf16[304,256]{1,0:T(8,128)(2,1)S(1)} %get-tuple-element.35.refs_0_, bf16[304,256]{1,0:T(8,128)(2,1)S(1)} %paired.4.refs_1_, bf16[1,288,256]{2,1,0:T(8,128)(2,1)S(1)} %stack.7.refs_2_.refs_8_.refs_10_, ...), custom_call_target="tpu_custom_call" | custom-call | flops 150994944 | bytes 2097152 | tf_op jit(solution)/shard_map/scores/pallas_call | solution.py:75
  20.2 2.4 %collective-permute-start.11 = (f32[8,256]{1,0:T(8,128)S(1)}, f32[8,256]{1,0:T(8,128)S(1)}, u32[]{:S(2)}, u32[]{:S(2)}) collective-permute-start(f32[8,256]{1,0:T(8,128)S(1)} %join.1.refs_4_), channel_id=1, source_target_pairs={{0,8},{1,9},{2,10},{3,11},{4,12},{5,13},{6,14},{7,15},{8,0},{9,1},... | collective-permute-start | bytes 24584 | tf_op jit(solution)/shard_map/ppermute | solution.py:377
  22.6 0.7 %stage.1 = (bf16[512,256]{1,0:T(8,128)(2,1)S(1)}, bf16[32,512]{1,0:T(8,128)(2,1)S(1)}, f32[1536,512]{1,0:T(8,128)S(1)}, f32[512,512]{1,0:T(8,128)S(1)}) custom-call(bf16[304,256]{1,0:T(8,128)(2,1)S(1)} %get-tuple-element.35.refs_0_, bf16[304,256]{1,0:T(8,128)(2,1)S(1)} %paired.4.refs_1_, bf16[1,288,256]{2,1,0:T(8,128)(2,1)S(1)} %stack.4.refs_2_.refs_4_, ...), custom_call_target="tpu_custom_call" | custom-call | tf_op jit(solution)/shard_map/stage/pallas_call | solution.py:75
  23.4 1.4 %collective-permute-done.11.refs_5_ = f32[8,256]{1,0:T(8,128)S(1)} collective-permute-done((f32[8,256]{1,0:T(8,128)S(1)}, f32[8,256]{1,0:T(8,128)S(1)}, u32[]{:S(2)}, u32[]{:S(2)}) %collective-permute-start.11) | collective-permute-done | bytes 8224 | tf_op jit(solution)/shard_map/ppermute | solution.py:377
  26.3 0.6 %collective-permute-start.15 = (bf16[2,288,256]{2,1,0:T(8,128)(2,1)S(1)}, bf16[2,288,256]{2,1,0:T(8,128)(2,1)S(1)}, u32[]{:S(2)}, u32[]{:S(2)}) collective-permute-start(bf16[2,288,256]{2,1,0:T(8,128)(2,1)S(1)} %get-tuple-element.54.refs_6_.refs_0_), channel_id=1, source_target_pairs={{0,1},{1,0},{2,3},{3,2},{4,5},{5,4},{6,7},{7,6},{8,9},{9,8},{10,11... | collective-permute-start | bytes 884744 | tf_op jit(solution)/shard_map/ppermute | solution.py:377
  27.0 1.4 %collective-permute-start.13 = (bf16[288,256]{1,0:T(8,128)(2,1)S(1)}, bf16[288,256]{1,0:T(8,128)(2,1)S(1)}, u32[]{:S(2)}, u32[]{:S(2)}) collective-permute-start(bf16[288,256]{1,0:T(8,128)(2,1)S(1)} %fold.3.refs_1_.refs_13_), channel_id=1, source_target_pairs={{0,2},{1,3},{2,0},{3,1},{4,6},{5,7},{6,4},{7,5},{8,10},{9,11},{10,... | collective-permute-start | bytes 442376 | tf_op jit(solution)/shard_map/ppermute | solution.py:377
  29.3 1.9 %collective-permute-start.14 = (bf16[288,256]{1,0:T(8,128)(2,1)S(1)}, bf16[288,256]{1,0:T(8,128)(2,1)S(1)}, u32[]{:S(2)}, u32[]{:S(2)}) collective-permute-start(bf16[288,256]{1,0:T(8,128)(2,1)S(1)} %row_shares.3), channel_id=1, source_target_pairs={{0,8},{1,9},{2,10},{3,11},{4,12},{5,13},{6,14},{7,15},{8,0},{9,1},... | collective-permute-start | bytes 442376 | tf_op jit(solution)/shard_map/ppermute | solution.py:377
  31.2 1.7 %collective-permute-done.13.refs_0_ = bf16[288,256]{1,0:T(8,128)(2,1)S(1)} collective-permute-done((bf16[288,256]{1,0:T(8,128)(2,1)S(1)}, bf16[288,256]{1,0:T(8,128)(2,1)S(1)}, u32[]{:S(2)}, u32[]{:S(2)}) %collective-permute-start.13) | collective-permute-done | bytes 147488 | tf_op jit(solution)/shard_map/ppermute | solution.py:377
  33.0 1.7 %collective-permute-start.16 = (bf16[288,256]{1,0:T(8,128)(2,1)S(1)}, bf16[288,256]{1,0:T(8,128)(2,1)S(1)}, u32[]{:S(2)}, u32[]{:S(2)}) collective-permute-start(bf16[288,256]{1,0:T(8,128)(2,1)S(1)} %fold.4.refs_13_), channel_id=1, source_target_pairs={{0,4},{1,5},{2,6},{3,7},{4,0},{5,1},{6,2},{7,3},{8,12},{9,13},{10,... | collective-permute-start | bytes 442376 | tf_op jit(solution)/shard_map/ppermute | solution.py:377
  35.3 1.4 %collective-permute-start.17 = (bf16[288,256]{1,0:T(8,128)(2,1)S(1)}, bf16[288,256]{1,0:T(8,128)(2,1)S(1)}, u32[]{:S(2)}, u32[]{:S(2)}) collective-permute-start(bf16[288,256]{1,0:T(8,128)(2,1)S(1)} %fold.5), channel_id=1, source_target_pairs={{0,2},{1,3},{2,0},{3,1},{4,6},{5,7},{6,4},{7,5},{8,10},{9,11},{10,... | collective-permute-start | bytes 442376 | tf_op jit(solution)/shard_map/ppermute | solution.py:377
  36.6 3.5 %collective-permute-done.16.one_ref = bf16[288,256]{1,0:T(8,128)(2,1)S(1)} collective-permute-done((bf16[288,256]{1,0:T(8,128)(2,1)S(1)}, bf16[288,256]{1,0:T(8,128)(2,1)S(1)}, u32[]{:S(2)}, u32[]{:S(2)}) %collective-permute-start.16) | collective-permute-done | bytes 147488 | tf_op jit(solution)/shard_map/ppermute | solution.py:377
  40.5 0.8 %totals.1 = (f32[256,256]{1,0:T(8,128)}, bf16[32,256]{1,0:T(8,128)(2,1)}, f32[256,256]{1,0:T(8,128)}, f32[32,256]{1,0:T(8,128)}) custom-call(f32[288,256]{1,0:T(8,128)S(1)} %row_shares.2.refs_0_, bf16[288,256]{1,0:T(8,128)(2,1)S(1)} %collective-permute-done.14.refs_1_, f32[2,288,256]{2,1,0:T(8,128)S(1)} %get-tuple-element.57.own_ref.refs_2_, ...), custom_call_target="tpu_custom_call" | custom-call | tf_op jit(solution)/shard_map/totals/pallas_call | solution.py:75
  (41 shorter events, 4.6 us)
Async XLA Ops:
  0.6 11.8 %collective-permute-start = (bf16[256,256]{1,0:T(8,128)(2,1)}, bf16[256,256]{1,0:T(8,128)(2,1)S(1)}, u32[]{:S(2)}, u32[]{:S(2)}) collective-permute-start(bf16[256,256]{1,0:T(8,128)(2,1)} %dst_ref.1), channel_id=1, source_target_pairs={{0,4},{1,5},{2,6},{3,7},{4,0},{5,1},{6,2},{7,3},{8,12},{9,13},{10,... | collective-permute-start | bytes 393224 | tf_op jit(solution)/shard_map/ppermute | solution.py:377
  3.7 12.2 %collective-permute-start.5 = (bf16[256,256]{1,0:T(8,128)(2,1)}, bf16[256,256]{1,0:T(8,128)(2,1)S(1)}, u32[]{:S(2)}, u32[]{:S(2)}) collective-permute-start(bf16[256,256]{1,0:T(8,128)(2,1)} %dst_ref.1), channel_id=1, source_target_pairs={{0,2},{1,3},{2,0},{3,1},{4,6},{5,7},{6,4},{7,5},{8,10},{9,11},{10,... | collective-permute-start | bytes 393224 | tf_op jit(solution)/shard_map/ppermute | solution.py:377
  5.2 11.3 %collective-permute-start.2 = (bf16[256,256]{1,0:T(8,128)(2,1)}, bf16[256,256]{1,0:T(8,128)(2,1)S(1)}, u32[]{:S(2)}, u32[]{:S(2)}) collective-permute-start(bf16[256,256]{1,0:T(8,128)(2,1)} %src_ref.1), channel_id=1, source_target_pairs={{0,8},{1,9},{2,10},{3,11},{4,12},{5,13},{6,14},{7,15},{8,0},{9,1},... | collective-permute-start | bytes 393224 | tf_op jit(solution)/shard_map/ppermute | solution.py:377
  7.8 4.0 %collective-permute-start.1 = (bf16[32,256]{1,0:T(8,128)(2,1)}, bf16[32,256]{1,0:T(8,128)(2,1)S(1)}, u32[]{:S(2)}, u32[]{:S(2)}) collective-permute-start(bf16[32,256]{1,0:T(8,128)(2,1)} %grad_ref.1), channel_id=1, source_target_pairs={{0,4},{1,5},{2,6},{3,7},{4,0},{5,1},{6,2},{7,3},{8,12},{9,13},{10,... | collective-permute-start | bytes 49160 | tf_op jit(solution)/shard_map/ppermute | solution.py:377
  10.7 5.7 %collective-permute-start.3 = (bf16[48,256]{1,0:T(8,128)(2,1)}, bf16[48,256]{1,0:T(8,128)(2,1)S(1)}, u32[]{:S(2)}, u32[]{:S(2)}) collective-permute-start(bf16[48,256]{1,0:T(8,128)(2,1)} %get-tuple-element.36), channel_id=1, source_target_pairs={{0,8},{1,9},{2,10},{3,11},{4,12},{5,13},{6,14},{7,15},{8,0},{9,1},... | collective-permute-start | bytes 73736 | tf_op jit(solution)/shard_map/ppermute | solution.py:377
  11.8 4.0 %collective-permute-start.6 = (bf16[32,256]{1,0:T(8,128)(2,1)}, bf16[32,256]{1,0:T(8,128)(2,1)S(1)}, u32[]{:S(2)}, u32[]{:S(2)}) collective-permute-start(bf16[32,256]{1,0:T(8,128)(2,1)} %grad_ref.1), channel_id=1, source_target_pairs={{0,2},{1,3},{2,0},{3,1},{4,6},{5,7},{6,4},{7,5},{8,10},{9,11},{10,... | collective-permute-start | bytes 49160 | tf_op jit(solution)/shard_map/ppermute | solution.py:377
  12.5 5.2 %collective-permute-start.9 = (bf16[288,256]{1,0:T(8,128)(2,1)S(1)}, bf16[288,256]{1,0:T(8,128)(2,1)S(1)}, u32[]{:S(2)}, u32[]{:S(2)}) collective-permute-start(bf16[288,256]{1,0:T(8,128)(2,1)S(1)} %paired.3.refs_0_), channel_id=1, source_target_pairs={{0,2},{1,3},{2,0},{3,1},{4,6},{5,7},{6,4},{7,5},{8,10},{9,11},{10,... | collective-permute-start | bytes 442376 | tf_op jit(solution)/shard_map/ppermute | solution.py:377
  13.9 0.9 %copy-start = (bf16[304,256]{1,0:T(8,128)(2,1)S(1)}, bf16[304,256]{1,0:T(8,128)(2,1)}, u32[]{:S(2)}) copy-start(bf16[304,256]{1,0:T(8,128)(2,1)} %get-tuple-element.33.src_ref) | copy-start | bytes 466948
  14.8 0.9 %copy-start.1 = (bf16[288,256]{1,0:T(8,128)(2,1)S(1)}, bf16[288,256]{1,0:T(8,128)(2,1)}, u32[]{:S(2)}) copy-start(bf16[288,256]{1,0:T(8,128)(2,1)} %get-tuple-element.34.dst_ref) | copy-start | bytes 442372
  15.8 2.0 %collective-permute-start.8 = (bf16[1,288,256]{2,1,0:T(8,128)(2,1)S(1)}, bf16[1,288,256]{2,1,0:T(8,128)(2,1)S(1)}, u32[]{:S(2)}, u32[]{:S(2)}) collective-permute-start(bf16[1,288,256]{2,1,0:T(8,128)(2,1)S(1)} %stack.6.refs_6_.refs_8_), channel_id=1, source_target_pairs={{0,1},{1,0},{2,3},{3,2},{4,5},{5,4},{6,7},{7,6},{8,9},{9,8},{10,11... | collective-permute-start | bytes 442376 | tf_op jit(solution)/shard_map/ppermute | solution.py:377
  15.9 1.9 %collective-permute-start.4 = (bf16[1,288,256]{2,1,0:T(8,128)(2,1)S(1)}, bf16[1,288,256]{2,1,0:T(8,128)(2,1)S(1)}, u32[]{:S(2)}, u32[]{:S(2)}) collective-permute-start(bf16[1,288,256]{2,1,0:T(8,128)(2,1)S(1)} %stack.4.refs_2_.refs_4_), channel_id=1, source_target_pairs={{0,1},{1,0},{2,3},{3,2},{4,5},{5,4},{6,7},{7,6},{8,9},{9,8},{10,11... | collective-permute-start | bytes 442376 | tf_op jit(solution)/shard_map/ppermute | solution.py:377
  16.4 1.4 %collective-permute-start.7 = (bf16[1,288,256]{2,1,0:T(8,128)(2,1)S(1)}, bf16[1,288,256]{2,1,0:T(8,128)(2,1)S(1)}, u32[]{:S(2)}, u32[]{:S(2)}) collective-permute-start(bf16[1,288,256]{2,1,0:T(8,128)(2,1)S(1)} %stack.5.refs_4_.refs_6_), channel_id=1, source_target_pairs={{0,1},{1,0},{2,3},{3,2},{4,5},{5,4},{6,7},{7,6},{8,9},{9,8},{10,11... | collective-permute-start | bytes 442376 | tf_op jit(solution)/shard_map/ppermute | solution.py:377
  17.7 1.7 %collective-permute-start.10 = (bf16[1,288,256]{2,1,0:T(8,128)(2,1)S(1)}, bf16[1,288,256]{2,1,0:T(8,128)(2,1)S(1)}, u32[]{:S(2)}, u32[]{:S(2)}) collective-permute-start(bf16[1,288,256]{2,1,0:T(8,128)(2,1)S(1)} %stack.7.refs_2_.refs_8_.refs_10_), channel_id=1, source_target_pairs={{0,1},{1,0},{2,3},{3,2},{4,5},{5,4},{6,7},{7,6},{8,9},{9,8},{10,11... | collective-permute-start | bytes 442376 | tf_op jit(solution)/shard_map/ppermute | solution.py:377
  20.2 4.6 %collective-permute-start.11 = (f32[8,256]{1,0:T(8,128)S(1)}, f32[8,256]{1,0:T(8,128)S(1)}, u32[]{:S(2)}, u32[]{:S(2)}) collective-permute-start(f32[8,256]{1,0:T(8,128)S(1)} %join.1.refs_4_), channel_id=1, source_target_pairs={{0,8},{1,9},{2,10},{3,11},{4,12},{5,13},{6,14},{7,15},{8,0},{9,1},... | collective-permute-start | bytes 24584 | tf_op jit(solution)/shard_map/ppermute | solution.py:377
  25.3 1.6 %collective-permute-start.12 = (bf16[2,288,256]{2,1,0:T(8,128)(2,1)S(1)}, bf16[2,288,256]{2,1,0:T(8,128)(2,1)S(1)}, u32[]{:S(2)}, u32[]{:S(2)}) collective-permute-start(bf16[2,288,256]{2,1,0:T(8,128)(2,1)S(1)} %get-tuple-element.50.refs_6_), channel_id=1, source_target_pairs={{0,1},{1,0},{2,3},{3,2},{4,5},{5,4},{6,7},{7,6},{8,9},{9,8},{10,11... | collective-permute-start | bytes 884744 | tf_op jit(solution)/shard_map/ppermute | solution.py:377
  26.3 9.0 %collective-permute-start.15 = (bf16[2,288,256]{2,1,0:T(8,128)(2,1)S(1)}, bf16[2,288,256]{2,1,0:T(8,128)(2,1)S(1)}, u32[]{:S(2)}, u32[]{:S(2)}) collective-permute-start(bf16[2,288,256]{2,1,0:T(8,128)(2,1)S(1)} %get-tuple-element.54.refs_6_.refs_0_), channel_id=1, source_target_pairs={{0,1},{1,0},{2,3},{3,2},{4,5},{5,4},{6,7},{7,6},{8,9},{9,8},{10,11... | collective-permute-start | bytes 884744 | tf_op jit(solution)/shard_map/ppermute | solution.py:377
  27.0 6.0 %collective-permute-start.13 = (bf16[288,256]{1,0:T(8,128)(2,1)S(1)}, bf16[288,256]{1,0:T(8,128)(2,1)S(1)}, u32[]{:S(2)}, u32[]{:S(2)}) collective-permute-start(bf16[288,256]{1,0:T(8,128)(2,1)S(1)} %fold.3.refs_1_.refs_13_), channel_id=1, source_target_pairs={{0,2},{1,3},{2,0},{3,1},{4,6},{5,7},{6,4},{7,5},{8,10},{9,11},{10,... | collective-permute-start | bytes 442376 | tf_op jit(solution)/shard_map/ppermute | solution.py:377
  29.3 10.9 %collective-permute-start.14 = (bf16[288,256]{1,0:T(8,128)(2,1)S(1)}, bf16[288,256]{1,0:T(8,128)(2,1)S(1)}, u32[]{:S(2)}, u32[]{:S(2)}) collective-permute-start(bf16[288,256]{1,0:T(8,128)(2,1)S(1)} %row_shares.3), channel_id=1, source_target_pairs={{0,8},{1,9},{2,10},{3,11},{4,12},{5,13},{6,14},{7,15},{8,0},{9,1},... | collective-permute-start | bytes 442376 | tf_op jit(solution)/shard_map/ppermute | solution.py:377
  33.0 7.2 %collective-permute-start.16 = (bf16[288,256]{1,0:T(8,128)(2,1)S(1)}, bf16[288,256]{1,0:T(8,128)(2,1)S(1)}, u32[]{:S(2)}, u32[]{:S(2)}) collective-permute-start(bf16[288,256]{1,0:T(8,128)(2,1)S(1)} %fold.4.refs_13_), channel_id=1, source_target_pairs={{0,4},{1,5},{2,6},{3,7},{4,0},{5,1},{6,2},{7,3},{8,12},{9,13},{10,... | collective-permute-start | bytes 442376 | tf_op jit(solution)/shard_map/ppermute | solution.py:377
  35.3 5.2 %collective-permute-start.17 = (bf16[288,256]{1,0:T(8,128)(2,1)S(1)}, bf16[288,256]{1,0:T(8,128)(2,1)S(1)}, u32[]{:S(2)}, u32[]{:S(2)}) collective-permute-start(bf16[288,256]{1,0:T(8,128)(2,1)S(1)} %fold.5), channel_id=1, source_target_pairs={{0,2},{1,3},{2,0},{3,1},{4,6},{5,7},{6,4},{7,5},{8,10},{9,11},{10,... | collective-permute-start | bytes 442376 | tf_op jit(solution)/shard_map/ppermute | solution.py:377

commit v2 on v0

--- a/solution.py
+++ b/solution.py
@@ -23,6 +23,8 @@
         self.span = self.n_row * rows
         self.packet = rows + batch
         self.head = (3 * self.n_row + 7) // 8 * 8
+        cut = self.packet // 32 * 16 + 16
+        self.pieces = [(0, cut), (cut, self.packet)]
         even = range(0, self.n_col, 2)
         self.early = [t for t in even if t & (t - 1) == 0]
         self.late = [t for t in even if t & (t - 1)]
@@ -70,7 +72,7 @@
 shape = jax.ShapeDtypeStruct
 
 
-def call(name, kernel, out_shape, operands, after=(), scratch=(), limit=8 * mib):
+def call(name, kernel, out_shape, operands, after=(), scratch=(), limit=8 * mib, cost=None):
     many = isinstance(out_shape, tuple)
     return pl.pallas_call(
         kernel,
@@ -79,6 +81,7 @@
         out_specs=(in_vmem(),) * len(out_shape) if many else in_vmem(),
         scratch_shapes=list(scratch),
         compiler_params=pltpu.CompilerParams(vmem_limit_bytes=limit),
+        cost_estimate=cost,
         name=name,
     )(*operands, *after)
 
@@ -120,11 +123,11 @@
     return call("keep", kernel, outs, [src_pack, dst_pack], after, limit=2 * mib)
 
 
-def hand(one, *after):
+def hand(one, *after, cost=None):
     def kernel(one_ref, *refs):
         refs[-1][...] = one_ref[...]
 
-    return call("hand", kernel, shape(one.shape, one.dtype), [one], after, limit=2 * mib)
+    return call("hand", kernel, shape(one.shape, one.dtype), [one], after, limit=2 * mib, cost=cost)
 
 
 def paired(block, small, *after):
@@ -327,31 +330,39 @@
     return call("row_shares", kernel, outs, operands, after, limit=g.n * rows * rows * 4 + 6 * mib)
 
 
-def fold(own, near, i, others, *after):
+def fold(own, near, i, piece, others, cost, *after):
+    start, stop = piece
+
     def kernel(own_ref, near_ref, *refs):
-        total = own_ref[i] + near_ref[i].astype(f32)
+        total = own_ref[i, start:stop] + near_ref[i, start:stop].astype(f32)
         for one in refs[: len(others)]:
             total = total + one[...].astype(f32)
         refs[-1][...] = total.astype(bf16)
 
-    return call("fold", kernel, shape(own.shape[1:], bf16), [own, near, *others], after)
+    out = shape((stop - start, own.shape[2]), bf16)
+    return call("fold", kernel, out, [own, near, *others], after, cost=cost)
 
 
 def totals(g, src_own, src_others, dst_own, dst_near, dst_others):
     def kernel(*refs):
         src_out, belief_out, dst_out, next_out = refs[-4:]
-        src_refs, dst_refs = refs[: 1 + len(src_others)], refs[1 + len(src_others) : -4]
-
-        def added(out, here, own, others):
-            total = own[here] + sum(one[here].astype(f32) for one in others)
-            out[...] = total.astype(out.dtype)
-
-        big, small = slice(0, g.rows), slice(g.rows, g.packet)
-        dst_refs = [dst_refs[0].at[0], dst_refs[1].at[0], *dst_refs[2:]]
-        added(src_out, big, src_refs[0], src_refs[1:])
-        added(belief_out, small, src_refs[0], src_refs[1:])
-        added(dst_out, big, dst_refs[0], dst_refs[1:])
-        added(next_out, small, dst_refs[0], dst_refs[1:])
+        src_refs, refs = refs[: 1 + len(src_others)], refs[1 + len(src_others) : -4]
+        own, near, parts = refs[0], refs[1], refs[2:]
+
+        def src_total(here):
+            return src_refs[0][here] + sum(one[here].astype(f32) for one in src_refs[1:])
+
+        src_out[...] = src_total(slice(0, g.rows))
+        belief_out[...] = src_total(slice(g.rows, g.packet)).astype(bf16)
+        for start, stop in g.pieces:
+            total = own[0, start:stop] + near[0, start:stop].astype(f32)
+            for ((first, last), _), part in zip(dst_others, parts):
+                if first <= start and stop <= last:
+                    total = total + part[start - first : stop - first].astype(f32)
+            edge = min(stop, g.rows)
+            dst_out[start:edge] = total[: edge - start]
+            if stop > g.rows:
+                next_out[...] = total[g.rows - start :]
 
     outs = (
         shape((g.rows, g.width), f32),
@@ -359,7 +370,7 @@
         shape((g.rows, g.width), f32),
         shape((g.batch, g.rows), f32),
     )
-    operands = [src_own, *src_others, dst_own, dst_near, *dst_others]
+    operands = [src_own, *src_others, dst_own, dst_near, *[part for _, part in dst_others]]
     return call("totals", kernel, outs, operands, limit=12 * mib)
 
 
@@ -408,21 +419,25 @@
 
     got = {t: [] for t in range(0, g.n_col, 2)}
     last = near_send
+    early = pl.CostEstimate(flops=1000000000, bytes_accessed=1 << 20, transcendentals=0)
+    slow = pl.CostEstimate(flops=3000000000, bytes_accessed=1 << 20, transcendentals=0)
     for t in reversed(range(2, g.n_col, 2)):
         own, near, slots = (far_own, far_got, g.far) if t in g.far else (near_own, near_got, g.near)
-        send = fold(own, near, slots.index(t), got[t], last)
-        one = swap(send, low_bit(t))
-        got[t ^ low_bit(t)].append(hand(one) if low_bit(t) > 2 else one)
+        for piece in g.pieces if t in g.far else [(0, g.packet)]:
+            others = [one for at, one in got[t] if at == piece]
+            cost = slow if low_bit(t) > 2 and piece[0] else None
+            last = fold(own, near, slots.index(t), piece, others, cost, last)
+            one = swap(last, low_bit(t))
+            got[t ^ low_bit(t)].append((piece, hand(one, cost=early) if low_bit(t) > 2 else one))
         if t == g.n_col - 2:
             rest = list(range(1, g.n_row))
-            src_send = row_shares(g, rest, bf16, changes, order, stacks, belief_sum, send)
-            src_got = [swap(one, g.row_flip(s)) for one, s in zip(src_send, rest)]
+            src_send = row_shares(g, rest, bf16, changes, order, stacks, belief_sum, last)
+            src_got = [hand(swap(one, g.row_flip(s)), cost=early) for one, s in zip(src_send, rest)]
         elif t == 4:
-            (src_own,) = row_shares(g, [0], f32, changes, order, stacks, belief_sum, send)
-            send = src_own
-        last = send
+            (src_own,) = row_shares(g, [0], f32, changes, order, stacks, belief_sum, last)
+            last = src_own
     grad_src, grad_belief, grad_dst, next_belief = totals(
-        g, src_own, src_got, near_own, near_got, got[0]
+        g, src_own, src_got, near_own, near_got, got[0][1::-1] + got[0][2:]
     )
     return (next_belief, grad_belief, grad_src, grad_dst)
 

time: 40.9 us -> 41.1 us (level)
  starting transfers between devices: 15.1 us -> 16 us
  waiting for transfers between devices: 13.8 us -> 13 us
    ppermute x16 -> x18, starting transfers between devices: 15.1 us -> 16 us  [swap(): return lax.ppermute(array, 'src', [(i, i ^ flip) for i in range(n)])]
    ppermute x16 -> x18, waiting for transfers between devices: 13.8 us -> 13 us  [swap(): return lax.ppermute(array, 'src', [(i, i ^ flip) for i in range(n)])]
    pallas_call x22 -> x26, Pallas kernels: 6.79 us -> 6.81 us  [call(): pl.pallas_call(kernel, out_shape=out_shape, in_specs=[in_vmem()] * len(op...]
  transfers between devices with their start and end apart: 16 -> 18, of which waited for: 8 -> 7; matrix products, arithmetic and copies ran while one was open for 0% -> 0% of each run, Pallas kernels for 16% -> 16%
where the time goes in v2:
time: 41.1 us; the launch traced here: 40.9 us
  starting transfers between devices  16 us (39%)
  waiting for transfers between devices  13 us (32%)
  Pallas kernels  8.56 us (21%)
  local copies, waits for them, and re-layouts  1.82 us (4%)
  between operations  1.53 us (4%)
    ppermute x18, starting transfers between devices, swap(): return lax.ppermute(array, 'src', [(i, i ^ flip) for i in range(n)])  16 us
    ppermute x18, waiting for transfers between devices, swap(): return lax.ppermute(array, 'src', [(i, i ^ flip) for i in range(n)])  13 us
    pallas_call x26, Pallas kernels, call(): pl.pallas_call(kernel, out_shape=out_shape, in_specs=[in_vmem()] * len(op...  6.81 us
    unnamed x4, local copies, waits for them, and re-layouts  1.82 us
    pallas_call x1, Pallas kernels, pack(): pl.pallas_call(functools.partial(pack_kernel, g), out_shape=(shape((g.row...  1.75 us
  transfers between devices with their start and end apart: 18, of which 7 were waited for; matrix products, arithmetic and copies ran while one was open for 0% of the time, Pallas kernels for 16%

profile of v2, /device:TPU:0, one launch (start us, length us, event | category | flops | bytes accessed | tf_op | source)
XLA Modules:
  0.0 40.9 jit_solution(17612706289448324018)
XLA Ops:
  0.6 3.1 %collective-permute-start = (bf16[256,256]{1,0:T(8,128)(2,1)}, bf16[256,256]{1,0:T(8,128)(2,1)S(1)}, u32[]{:S(2)}, u32[]{:S(2)}) collective-permute-start(bf16[256,256]{1,0:T(8,128)(2,1)} %dst_ref.1), channel_id=1, source_target_pairs={{0,4},{1,5},{2,6},{3,7},{4,0},{5,1},{6,2},{7,3},{8,12},{9,13},{10,... | collective-permute-start | bytes 393224 | tf_op jit(solution)/shard_map/ppermute | solution.py:381
  4.5 1.8 %pack.1 = (bf16[304,256]{1,0:T(8,128)(2,1)}, bf16[288,256]{1,0:T(8,128)(2,1)}) custom-call(s32[1,16]{1,0:T(1,128)} %tile_ref.1, s32[1,1]{1,0:T(1,128)} %bitcast.1.count_ref, bf16[256,256]{1,0:T(8,128)(2,1)} %src_ref.1, bf16[32,256]{1,0:T(8,128)(2,1)} %bel_ref.1, bf16[256,256]{1,0:T(8,128)(2,1)} %dst_ref.1, bf16[32,256]{1,0:T(8,128)(2,1)} %grad_ref.1), custom_call_target="tpu_custom_call" | custom-call | tf_op jit(solution)/shard_map/pack/pallas_call | solution.py:103
  6.2 3.0 %collective-permute-start.2 = (bf16[304,256]{1,0:T(8,128)(2,1)}, bf16[304,256]{1,0:T(8,128)(2,1)S(1)}, u32[]{:S(2)}, u32[]{:S(2)}) collective-permute-start(bf16[304,256]{1,0:T(8,128)(2,1)} %get-tuple-element.32.src_ref), channel_id=1, source_target_pairs={{0,8},{1,9},{2,10},{3,11},{4,12},{5,13},{6,14},{7,15},{8,0},{9,1},... | collective-permute-start | bytes 466952 | tf_op jit(solution)/shard_map/ppermute | solution.py:381
  9.2 1.5 %collective-permute-start.4 = (bf16[288,256]{1,0:T(8,128)(2,1)}, bf16[288,256]{1,0:T(8,128)(2,1)S(1)}, u32[]{:S(2)}, u32[]{:S(2)}) collective-permute-start(bf16[288,256]{1,0:T(8,128)(2,1)} %get-tuple-element.33.dst_ref), channel_id=1, source_target_pairs={{0,2},{1,3},{2,0},{3,1},{4,6},{5,7},{6,4},{7,5},{8,10},{9,11},{10,... | collective-permute-start | bytes 442376 | tf_op jit(solution)/shard_map/ppermute | solution.py:381
  10.7 0.6 %collective-permute-start.7 = (bf16[288,256]{1,0:T(8,128)(2,1)S(1)}, bf16[288,256]{1,0:T(8,128)(2,1)S(1)}, u32[]{:S(2)}, u32[]{:S(2)}) collective-permute-start(bf16[288,256]{1,0:T(8,128)(2,1)S(1)} %paired.1.refs_0_), channel_id=1, source_target_pairs={{0,2},{1,3},{2,0},{3,1},{4,6},{5,7},{6,4},{7,5},{8,10},{9,11},{10,... | collective-permute-start | bytes 442376 | tf_op jit(solution)/shard_map/ppermute | solution.py:381
  11.3 0.9 %copy-done = bf16[304,256]{1,0:T(8,128)(2,1)S(1)} copy-done((bf16[304,256]{1,0:T(8,128)(2,1)S(1)}, bf16[304,256]{1,0:T(8,128)(2,1)}, u32[]{:S(2)}) %copy-start) | copy-done | bytes 155672
  12.2 0.9 %copy-done.1 = bf16[288,256]{1,0:T(8,128)(2,1)S(1)} copy-done((bf16[288,256]{1,0:T(8,128)(2,1)S(1)}, bf16[288,256]{1,0:T(8,128)(2,1)}, u32[]{:S(2)}) %copy-start.1) | copy-done | bytes 147480
  13.2 0.5 %collective-permute-start.3 = (bf16[1,288,256]{2,1,0:T(8,128)(2,1)S(1)}, bf16[1,288,256]{2,1,0:T(8,128)(2,1)S(1)}, u32[]{:S(2)}, u32[]{:S(2)}) collective-permute-start(bf16[1,288,256]{2,1,0:T(8,128)(2,1)S(1)} %stack.4.refs_2_.refs_4_), channel_id=1, source_target_pairs={{0,1},{1,0},{2,3},{3,2},{4,5},{5,4},{6,7},{7,6},{8,9},{9,8},{10,11... | collective-permute-start | bytes 442376 | tf_op jit(solution)/shard_map/ppermute | solution.py:381
  13.7 2.0 %collective-permute-done.4.refs_0_ = bf16[288,256]{1,0:T(8,128)(2,1)S(1)} collective-permute-done((bf16[288,256]{1,0:T(8,128)(2,1)}, bf16[288,256]{1,0:T(8,128)(2,1)S(1)}, u32[]{:S(2)}, u32[]{:S(2)}) %collective-permute-start.4) | collective-permute-done | bytes 147488 | tf_op jit(solution)/shard_map/ppermute | solution.py:381
  16.2 1.1 %collective-permute-done.7.refs_0_ = bf16[288,256]{1,0:T(8,128)(2,1)S(1)} collective-permute-done((bf16[288,256]{1,0:T(8,128)(2,1)S(1)}, bf16[288,256]{1,0:T(8,128)(2,1)S(1)}, u32[]{:S(2)}, u32[]{:S(2)}) %collective-permute-start.7) | collective-permute-done | bytes 147488 | tf_op jit(solution)/shard_map/ppermute | solution.py:381
  17.4 1.6 %scores.2 = (f32[1536,512]{1,0:T(8,128)S(1)}, f32[32,512]{1,0:T(8,128)S(1)}, f32[3,512]{1,0:T(4,128)S(1)}) custom-call(bf16[304,256]{1,0:T(8,128)(2,1)S(1)} %get-tuple-element.34.refs_0_, bf16[304,256]{1,0:T(8,128)(2,1)S(1)} %collective-permute-done.2.refs_1_, bf16[1,288,256]{2,1,0:T(8,128)(2,1)S(1)} %stack.4.refs_2_.refs_4_, ...), custom_call_target="tpu_custom_call" | custom-call | tf_op jit(solution)/shard_map/scores/pallas_call | solution.py:77
  19.0 0.7 %scores.3 = (f32[512,512]{1,0:T(8,128)S(1)}, f32[32,512]{1,0:T(8,128)S(1)}, f32[3,512]{1,0:T(4,128)S(1)}) custom-call(bf16[304,256]{1,0:T(8,128)(2,1)S(1)} %get-tuple-element.34.refs_0_, bf16[304,256]{1,0:T(8,128)(2,1)S(1)} %collective-permute-done.2.refs_1_, bf16[1,288,256]{2,1,0:T(8,128)(2,1)S(1)} %stack.7.refs_2_.refs_8_.refs_10_, ...), custom_call_target="tpu_custom_call" | custom-call | tf_op jit(solution)/shard_map/scores/pallas_call | solution.py:77
  20.1 0.7 %stage.1 = (bf16[512,256]{1,0:T(8,128)(2,1)S(1)}, bf16[32,512]{1,0:T(8,128)(2,1)S(1)}, f32[1536,512]{1,0:T(8,128)S(1)}, f32[512,512]{1,0:T(8,128)S(1)}) custom-call(bf16[304,256]{1,0:T(8,128)(2,1)S(1)} %get-tuple-element.34.refs_0_, bf16[304,256]{1,0:T(8,128)(2,1)S(1)} %collective-permute-done.2.refs_1_, bf16[1,288,256]{2,1,0:T(8,128)(2,1)S(1)} %stack.4.refs_2_.refs_4_, ...), custom_call_target="tpu_custom_call" | custom-call | tf_op jit(solution)/shard_map/stage/pallas_call | solution.py:77
  20.8 3.5 %collective-permute-done.9.refs_5_ = f32[8,256]{1,0:T(8,128)S(1)} collective-permute-done((f32[8,256]{1,0:T(8,128)S(1)}, f32[8,256]{1,0:T(8,128)S(1)}, u32[]{:S(2)}, u32[]{:S(2)}) %collective-permute-start.9) | collective-permute-done | bytes 8224 | tf_op jit(solution)/shard_map/ppermute | solution.py:381
  25.8 0.7 %collective-permute-done.10.near_ref = bf16[2,288,256]{2,1,0:T(8,128)(2,1)S(1)} collective-permute-done((bf16[2,288,256]{2,1,0:T(8,128)(2,1)S(1)}, bf16[2,288,256]{2,1,0:T(8,128)(2,1)S(1)}, u32[]{:S(2)}, u32[]{:S(2)}) %collective-permute-start.10) | collective-permute-done | bytes 294944 | tf_op jit(solution)/shard_map/ppermute | solution.py:381
  26.5 1.6 %collective-permute-start.12 = (bf16[160,256]{1,0:T(8,128)(2,1)S(1)}, bf16[160,256]{1,0:T(8,128)(2,1)S(1)}, u32[]{:S(2)}, u32[]{:S(2)}) collective-permute-start(bf16[160,256]{1,0:T(8,128)(2,1)S(1)} %fold.5.refs_0_), channel_id=1, source_target_pairs={{0,2},{1,3},{2,0},{3,1},{4,6},{5,7},{6,4},{7,5},{8,10},{9,11},{10,... | collective-permute-start | bytes 245768 | tf_op jit(solution)/shard_map/ppermute | solution.py:381
  28.1 0.6 %collective-permute-start.11 = (bf16[128,256]{1,0:T(8,128)(2,1)S(1)}, bf16[128,256]{1,0:T(8,128)(2,1)S(1)}, u32[]{:S(2)}, u32[]{:S(2)}) collective-permute-start(bf16[128,256]{1,0:T(8,128)(2,1)S(1)} %fold.6.refs_1_.refs_13_), channel_id=1, source_target_pairs={{0,2},{1,3},{2,0},{3,1},{4,6},{5,7},{6,4},{7,5},{8,10},{9,11},{10,... | collective-permute-start | bytes 196616 | tf_op jit(solution)/shard_map/ppermute | solution.py:381
  29.1 0.5 %row_shares.3 = bf16[288,256]{1,0:T(8,128)(2,1)S(1)} custom-call(bf16[512,512]{1,0:T(8,128)(2,1)S(1)} %get-tuple-element.47.refs_0_, bf16[512,512]{1,0:T(8,128)(2,1)S(1)} %get-tuple-element.49.refs_1_, bf16[512,512]{1,0:T(8,128)(2,1)S(1)} %get-tuple-element.51.refs_2_, bf16[512,512]{1,0:T(8,128)(2,1)S(1)} %get-tuple-element.53.refs_3_, ...), custom_call_target="tpu_custom_call" | custom-call | tf_op jit(solution)/shard_map/row_shares/pallas_call | solution.py:77
  30.0 1.6 %collective-permute-done.12.refs_0_ = bf16[160,256]{1,0:T(8,128)(2,1)S(1)} collective-permute-done((bf16[160,256]{1,0:T(8,128)(2,1)S(1)}, bf16[160,256]{1,0:T(8,128)(2,1)S(1)}, u32[]{:S(2)}, u32[]{:S(2)}) %collective-permute-start.12) | collective-permute-done | bytes 81952 | tf_op jit(solution)/shard_map/ppermute | solution.py:381
  31.6 1.6 %collective-permute-start.16 = (bf16[160,256]{1,0:T(8,128)(2,1)S(1)}, bf16[160,256]{1,0:T(8,128)(2,1)S(1)}, u32[]{:S(2)}, u32[]{:S(2)}) collective-permute-start(bf16[160,256]{1,0:T(8,128)(2,1)S(1)} %fold.7.refs_1_), channel_id=1, source_target_pairs={{0,4},{1,5},{2,6},{3,7},{4,0},{5,1},{6,2},{7,3},{8,12},{9,13},{10,... | collective-permute-start | bytes 245768 | tf_op jit(solution)/shard_map/ppermute | solution.py:381
  33.3 0.9 %collective-permute-start.15 = (bf16[128,256]{1,0:T(8,128)(2,1)S(1)}, bf16[128,256]{1,0:T(8,128)(2,1)S(1)}, u32[]{:S(2)}, u32[]{:S(2)}) collective-permute-start(bf16[128,256]{1,0:T(8,128)(2,1)S(1)} %fold.8.refs_13_), channel_id=1, source_target_pairs={{0,4},{1,5},{2,6},{3,7},{4,0},{5,1},{6,2},{7,3},{8,12},{9,13},{10,... | collective-permute-start | bytes 196616 | tf_op jit(solution)/shard_map/ppermute | solution.py:381
  34.7 1.6 %collective-permute-start.17 = (bf16[288,256]{1,0:T(8,128)(2,1)S(1)}, bf16[288,256]{1,0:T(8,128)(2,1)S(1)}, u32[]{:S(2)}, u32[]{:S(2)}) collective-permute-start(bf16[288,256]{1,0:T(8,128)(2,1)S(1)} %fold.9), channel_id=1, source_target_pairs={{0,2},{1,3},{2,0},{3,1},{4,6},{5,7},{6,4},{7,5},{8,10},{9,11},{10,... | collective-permute-start | bytes 442376 | tf_op jit(solution)/shard_map/ppermute | solution.py:381
  36.3 3.7 %collective-permute-done.13.one_ref = bf16[288,256]{1,0:T(8,128)(2,1)S(1)} collective-permute-done((bf16[288,256]{1,0:T(8,128)(2,1)S(1)}, bf16[288,256]{1,0:T(8,128)(2,1)S(1)}, u32[]{:S(2)}, u32[]{:S(2)}) %collective-permute-start.13) | collective-permute-done | bytes 147488 | tf_op jit(solution)/shard_map/ppermute | solution.py:381
  40.1 0.8 %totals.1 = (f32[256,256]{1,0:T(8,128)}, bf16[32,256]{1,0:T(8,128)(2,1)}, f32[256,256]{1,0:T(8,128)}, f32[32,256]{1,0:T(8,128)}) custom-call(f32[288,256]{1,0:T(8,128)S(1)} %row_shares.2.refs_0_, bf16[288,256]{1,0:T(8,128)(2,1)S(1)} %hand.3.refs_1_, f32[2,288,256]{2,1,0:T(8,128)S(1)} %get-tuple-element.55.own_ref.refs_2_, ...), custom_call_target="tpu_custom_call" | custom-call | tf_op jit(solution)/shard_map/totals/pallas_call | solution.py:77
  (43 shorter events, 3.9 us)
Async XLA Ops:
  0.6 10.1 %collective-permute-start = (bf16[256,256]{1,0:T(8,128)(2,1)}, bf16[256,256]{1,0:T(8,128)(2,1)S(1)}, u32[]{:S(2)}, u32[]{:S(2)}) collective-permute-start(bf16[256,256]{1,0:T(8,128)(2,1)} %dst_ref.1), channel_id=1, source_target_pairs={{0,4},{1,5},{2,6},{3,7},{4,0},{5,1},{6,2},{7,3},{8,12},{9,13},{10,... | collective-permute-start | bytes 393224 | tf_op jit(solution)/shard_map/ppermute | solution.py:381
  3.7 7.0 %collective-permute-start.1 = (bf16[32,256]{1,0:T(8,128)(2,1)}, bf16[32,256]{1,0:T(8,128)(2,1)S(1)}, u32[]{:S(2)}, u32[]{:S(2)}) collective-permute-start(bf16[32,256]{1,0:T(8,128)(2,1)} %grad_ref.1), channel_id=1, source_target_pairs={{0,4},{1,5},{2,6},{3,7},{4,0},{5,1},{6,2},{7,3},{8,12},{9,13},{10,... | collective-permute-start | bytes 49160 | tf_op jit(solution)/shard_map/ppermute | solution.py:381
  6.2 10.0 %collective-permute-start.2 = (bf16[304,256]{1,0:T(8,128)(2,1)}, bf16[304,256]{1,0:T(8,128)(2,1)S(1)}, u32[]{:S(2)}, u32[]{:S(2)}) collective-permute-start(bf16[304,256]{1,0:T(8,128)(2,1)} %get-tuple-element.32.src_ref), channel_id=1, source_target_pairs={{0,8},{1,9},{2,10},{3,11},{4,12},{5,13},{6,14},{7,15},{8,0},{9,1},... | collective-permute-start | bytes 466952 | tf_op jit(solution)/shard_map/ppermute | solution.py:381
  9.2 6.5 %collective-permute-start.4 = (bf16[288,256]{1,0:T(8,128)(2,1)}, bf16[288,256]{1,0:T(8,128)(2,1)S(1)}, u32[]{:S(2)}, u32[]{:S(2)}) collective-permute-start(bf16[288,256]{1,0:T(8,128)(2,1)} %get-tuple-element.33.dst_ref), channel_id=1, source_target_pairs={{0,2},{1,3},{2,0},{3,1},{4,6},{5,7},{6,4},{7,5},{8,10},{9,11},{10,... | collective-permute-start | bytes 442376 | tf_op jit(solution)/shard_map/ppermute | solution.py:381
  10.7 6.6 %collective-permute-start.7 = (bf16[288,256]{1,0:T(8,128)(2,1)S(1)}, bf16[288,256]{1,0:T(8,128)(2,1)S(1)}, u32[]{:S(2)}, u32[]{:S(2)}) collective-permute-start(bf16[288,256]{1,0:T(8,128)(2,1)S(1)} %paired.1.refs_0_), channel_id=1, source_target_pairs={{0,2},{1,3},{2,0},{3,1},{4,6},{5,7},{6,4},{7,5},{8,10},{9,11},{10,... | collective-permute-start | bytes 442376 | tf_op jit(solution)/shard_map/ppermute | solution.py:381
  11.3 0.9 %copy-start = (bf16[304,256]{1,0:T(8,128)(2,1)S(1)}, bf16[304,256]{1,0:T(8,128)(2,1)}, u32[]{:S(2)}) copy-start(bf16[304,256]{1,0:T(8,128)(2,1)} %get-tuple-element.32.src_ref) | copy-start | bytes 466948
  12.2 0.9 %copy-start.1 = (bf16[288,256]{1,0:T(8,128)(2,1)S(1)}, bf16[288,256]{1,0:T(8,128)(2,1)}, u32[]{:S(2)}) copy-start(bf16[288,256]{1,0:T(8,128)(2,1)} %get-tuple-element.33.dst_ref) | copy-start | bytes 442372
  13.2 4.2 %collective-permute-start.6 = (bf16[1,288,256]{2,1,0:T(8,128)(2,1)S(1)}, bf16[1,288,256]{2,1,0:T(8,128)(2,1)S(1)}, u32[]{:S(2)}, u32[]{:S(2)}) collective-permute-start(bf16[1,288,256]{2,1,0:T(8,128)(2,1)S(1)} %stack.6.refs_6_.refs_8_), channel_id=1, source_target_pairs={{0,1},{1,0},{2,3},{3,2},{4,5},{5,4},{6,7},{7,6},{8,9},{9,8},{10,11... | collective-permute-start | bytes 442376 | tf_op jit(solution)/shard_map/ppermute | solution.py:381
  13.2 4.1 %collective-permute-start.3 = (bf16[1,288,256]{2,1,0:T(8,128)(2,1)S(1)}, bf16[1,288,256]{2,1,0:T(8,128)(2,1)S(1)}, u32[]{:S(2)}, u32[]{:S(2)}) collective-permute-start(bf16[1,288,256]{2,1,0:T(8,128)(2,1)S(1)} %stack.4.refs_2_.refs_4_), channel_id=1, source_target_pairs={{0,1},{1,0},{2,3},{3,2},{4,5},{5,4},{6,7},{7,6},{8,9},{9,8},{10,11... | collective-permute-start | bytes 442376 | tf_op jit(solution)/shard_map/ppermute | solution.py:381
  15.7 1.7 %collective-permute-start.5 = (bf16[1,288,256]{2,1,0:T(8,128)(2,1)S(1)}, bf16[1,288,256]{2,1,0:T(8,128)(2,1)S(1)}, u32[]{:S(2)}, u32[]{:S(2)}) collective-permute-start(bf16[1,288,256]{2,1,0:T(8,128)(2,1)S(1)} %stack.5.refs_4_.refs_6_), channel_id=1, source_target_pairs={{0,1},{1,0},{2,3},{3,2},{4,5},{5,4},{6,7},{7,6},{8,9},{9,8},{10,11... | collective-permute-start | bytes 442376 | tf_op jit(solution)/shard_map/ppermute | solution.py:381
  17.3 1.7 %collective-permute-start.8 = (bf16[1,288,256]{2,1,0:T(8,128)(2,1)S(1)}, bf16[1,288,256]{2,1,0:T(8,128)(2,1)S(1)}, u32[]{:S(2)}, u32[]{:S(2)}) collective-permute-start(bf16[1,288,256]{2,1,0:T(8,128)(2,1)S(1)} %stack.7.refs_2_.refs_8_.refs_10_), channel_id=1, source_target_pairs={{0,1},{1,0},{2,3},{3,2},{4,5},{5,4},{6,7},{7,6},{8,9},{9,8},{10,11... | collective-permute-start | bytes 442376 | tf_op jit(solution)/shard_map/ppermute | solution.py:381
  19.7 4.6 %collective-permute-start.9 = (f32[8,256]{1,0:T(8,128)S(1)}, f32[8,256]{1,0:T(8,128)S(1)}, u32[]{:S(2)}, u32[]{:S(2)}) collective-permute-start(f32[8,256]{1,0:T(8,128)S(1)} %join.1.refs_4_), channel_id=1, source_target_pairs={{0,8},{1,9},{2,10},{3,11},{4,12},{5,13},{6,14},{7,15},{8,0},{9,1},... | collective-permute-start | bytes 24584 | tf_op jit(solution)/shard_map/ppermute | solution.py:381
  24.8 1.6 %collective-permute-start.10 = (bf16[2,288,256]{2,1,0:T(8,128)(2,1)S(1)}, bf16[2,288,256]{2,1,0:T(8,128)(2,1)S(1)}, u32[]{:S(2)}, u32[]{:S(2)}) collective-permute-start(bf16[2,288,256]{2,1,0:T(8,128)(2,1)S(1)} %get-tuple-element.48.refs_6_), channel_id=1, source_target_pairs={{0,1},{1,0},{2,3},{3,2},{4,5},{5,4},{6,7},{7,6},{8,9},{9,8},{10,11... | collective-permute-start | bytes 884744 | tf_op jit(solution)/shard_map/ppermute | solution.py:381
  26.5 5.0 %collective-permute-start.12 = (bf16[160,256]{1,0:T(8,128)(2,1)S(1)}, bf16[160,256]{1,0:T(8,128)(2,1)S(1)}, u32[]{:S(2)}, u32[]{:S(2)}) collective-permute-start(bf16[160,256]{1,0:T(8,128)(2,1)S(1)} %fold.5.refs_0_), channel_id=1, source_target_pairs={{0,2},{1,3},{2,0},{3,1},{4,6},{5,7},{6,4},{7,5},{8,10},{9,11},{10,... | collective-permute-start | bytes 245768 | tf_op jit(solution)/shard_map/ppermute | solution.py:381
  28.1 5.1 %collective-permute-start.11 = (bf16[128,256]{1,0:T(8,128)(2,1)S(1)}, bf16[128,256]{1,0:T(8,128)(2,1)S(1)}, u32[]{:S(2)}, u32[]{:S(2)}) collective-permute-start(bf16[128,256]{1,0:T(8,128)(2,1)S(1)} %fold.6.refs_1_.refs_13_), channel_id=1, source_target_pairs={{0,2},{1,3},{2,0},{3,1},{4,6},{5,7},{6,4},{7,5},{8,10},{9,11},{10,... | collective-permute-start | bytes 196616 | tf_op jit(solution)/shard_map/ppermute | solution.py:381
  28.7 5.9 %collective-permute-start.14 = (bf16[2,288,256]{2,1,0:T(8,128)(2,1)S(1)}, bf16[2,288,256]{2,1,0:T(8,128)(2,1)S(1)}, u32[]{:S(2)}, u32[]{:S(2)}) collective-permute-start(bf16[2,288,256]{2,1,0:T(8,128)(2,1)S(1)} %get-tuple-element.52.refs_6_.refs_0_), channel_id=1, source_target_pairs={{0,1},{1,0},{2,3},{3,2},{4,5},{5,4},{6,7},{7,6},{8,9},{9,8},{10,11... | collective-permute-start | bytes 884744 | tf_op jit(solution)/shard_map/ppermute | solution.py:381
  29.6 10.4 %collective-permute-start.13 = (bf16[288,256]{1,0:T(8,128)(2,1)S(1)}, bf16[288,256]{1,0:T(8,128)(2,1)S(1)}, u32[]{:S(2)}, u32[]{:S(2)}) collective-permute-start(bf16[288,256]{1,0:T(8,128)(2,1)S(1)} %row_shares.3), channel_id=1, source_target_pairs={{0,8},{1,9},{2,10},{3,11},{4,12},{5,13},{6,14},{7,15},{8,0},{9,1},... | collective-permute-start | bytes 442376 | tf_op jit(solution)/shard_map/ppermute | solution.py:381
  31.6 8.5 %collective-permute-start.16 = (bf16[160,256]{1,0:T(8,128)(2,1)S(1)}, bf16[160,256]{1,0:T(8,128)(2,1)S(1)}, u32[]{:S(2)}, u32[]{:S(2)}) collective-permute-start(bf16[160,256]{1,0:T(8,128)(2,1)S(1)} %fold.7.refs_1_), channel_id=1, source_target_pairs={{0,4},{1,5},{2,6},{3,7},{4,0},{5,1},{6,2},{7,3},{8,12},{9,13},{10,... | collective-permute-start | bytes 245768 | tf_op jit(solution)/shard_map/ppermute | solution.py:381
  33.3 6.8 %collective-permute-start.15 = (bf16[128,256]{1,0:T(8,128)(2,1)S(1)}, bf16[128,256]{1,0:T(8,128)(2,1)S(1)}, u32[]{:S(2)}, u32[]{:S(2)}) collective-permute-start(bf16[128,256]{1,0:T(8,128)(2,1)S(1)} %fold.8.refs_13_), channel_id=1, source_target_pairs={{0,4},{1,5},{2,6},{3,7},{4,0},{5,1},{6,2},{7,3},{8,12},{9,13},{10,... | collective-permute-start | bytes 196616 | tf_op jit(solution)/shard_map/ppermute | solution.py:381
  34.7 5.4 %collective-permute-start.17 = (bf16[288,256]{1,0:T(8,128)(2,1)S(1)}, bf16[288,256]{1,0:T(8,128)(2,1)S(1)}, u32[]{:S(2)}, u32[]{:S(2)}) collective-permute-start(bf16[288,256]{1,0:T(8,128)(2,1)S(1)} %fold.9), channel_id=1, source_target_pairs={{0,2},{1,3},{2,0},{3,1},{4,6},{5,7},{6,4},{7,5},{8,10},{9,11},{10,... | collective-permute-start | bytes 442376 | tf_op jit(solution)/shard_map/ppermute | solution.py:381

commit v3 on v2

--- a/solution.py
+++ b/solution.py
@@ -417,8 +417,11 @@
     changes = [change_of_far_odd, change_of_far, change_of_near_odd, change_of_near]
     order = [odd_far, g.far, odd_near, g.near]
 
+    rest = list(range(1, g.n_row))
+    src_send = row_shares(g, rest, bf16, changes, order, stacks, belief_sum)
+
     got = {t: [] for t in range(0, g.n_col, 2)}
-    last = near_send
+    last = src_send[0]
     early = pl.CostEstimate(flops=1000000000, bytes_accessed=1 << 20, transcendentals=0)
     slow = pl.CostEstimate(flops=3000000000, bytes_accessed=1 << 20, transcendentals=0)
     for t in reversed(range(2, g.n_col, 2)):
@@ -430,9 +433,9 @@
             one = swap(last, low_bit(t))
             got[t ^ low_bit(t)].append((piece, hand(one, cost=early) if low_bit(t) > 2 else one))
         if t == g.n_col - 2:
-            rest = list(range(1, g.n_row))
-            src_send = row_shares(g, rest, bf16, changes, order, stacks, belief_sum, last)
-            src_got = [hand(swap(one, g.row_flip(s)), cost=early) for one, s in zip(src_send, rest)]
+            src_got = [
+                hand(swap(hand(one, last), g.row_flip(s)), cost=early) for one, s in zip(src_send, rest)
+            ]
         elif t == 4:
             (src_own,) = row_shares(g, [0], f32, changes, order, stacks, belief_sum, last)
             last = src_own

time: 41.1 us -> 41.5 us (level)
    pallas_call x26 -> x27, Pallas kernels: 6.81 us -> 6.81 us  [call(): pl.pallas_call(kernel, out_shape=out_shape, in_specs=[in_vmem()] * len(op...]
  transfers between devices with their start and end apart: 18 -> 18, of which waited for: 7 -> 8; matrix products, arithmetic and copies ran while one was open for 0% -> 0% of each run, Pallas kernels for 16% -> 16%
where the time goes in v3:
time: 41.5 us; the launch traced here: 41.4 us
  starting transfers between devices  16.1 us (39%)
  waiting for transfers between devices  13.3 us (32%)
  Pallas kernels  8.56 us (21%)
  local copies, waits for them, and re-layouts  1.82 us (4%)
  between operations  1.52 us (4%)
    ppermute x18, starting transfers between devices, swap(): return lax.ppermute(array, 'src', [(i, i ^ flip) for i in range(n)])  16.1 us
    ppermute x18, waiting for transfers between devices, swap(): return lax.ppermute(array, 'src', [(i, i ^ flip) for i in range(n)])  13.3 us
    pallas_call x27, Pallas kernels, call(): pl.pallas_call(kernel, out_shape=out_shape, in_specs=[in_vmem()] * len(op...  6.81 us
    unnamed x4, local copies, waits for them, and re-layouts  1.82 us
    pallas_call x1, Pallas kernels, pack(): pl.pallas_call(functools.partial(pack_kernel, g), out_shape=(shape((g.row...  1.75 us
  transfers between devices with their start and end apart: 18, of which 8 were waited for; matrix products, arithmetic and copies ran while one was open for 0% of the time, Pallas kernels for 16%

profile of v3, /device:TPU:0, one launch (start us, length us, event | category | flops | bytes accessed | tf_op | source)
XLA Modules:
  0.0 41.4 jit_solution(13763523304926003889)
XLA Ops:
  0.6 3.1 %collective-permute-start = (bf16[256,256]{1,0:T(8,128)(2,1)}, bf16[256,256]{1,0:T(8,128)(2,1)S(1)}, u32[]{:S(2)}, u32[]{:S(2)}) collective-permute-start(bf16[256,256]{1,0:T(8,128)(2,1)} %dst_ref.1), channel_id=1, source_target_pairs={{0,4},{1,5},{2,6},{3,7},{4,0},{5,1},{6,2},{7,3},{8,12},{9,13},{10,... | collective-permute-start | bytes 393224 | tf_op jit(solution)/shard_map/ppermute | solution.py:381
  4.5 1.8 %pack.1 = (bf16[304,256]{1,0:T(8,128)(2,1)}, bf16[288,256]{1,0:T(8,128)(2,1)}) custom-call(s32[1,16]{1,0:T(1,128)} %tile_ref.1, s32[1,1]{1,0:T(1,128)} %bitcast.1.count_ref, bf16[256,256]{1,0:T(8,128)(2,1)} %src_ref.1, bf16[32,256]{1,0:T(8,128)(2,1)} %bel_ref.1, bf16[256,256]{1,0:T(8,128)(2,1)} %dst_ref.1, bf16[32,256]{1,0:T(8,128)(2,1)} %grad_ref.1), custom_call_target="tpu_custom_call" | custom-call | tf_op jit(solution)/shard_map/pack/pallas_call | solution.py:103
  6.2 3.0 %collective-permute-start.2 = (bf16[304,256]{1,0:T(8,128)(2,1)}, bf16[304,256]{1,0:T(8,128)(2,1)S(1)}, u32[]{:S(2)}, u32[]{:S(2)}) collective-permute-start(bf16[304,256]{1,0:T(8,128)(2,1)} %get-tuple-element.32.src_ref), channel_id=1, source_target_pairs={{0,8},{1,9},{2,10},{3,11},{4,12},{5,13},{6,14},{7,15},{8,0},{9,1},... | collective-permute-start | bytes 466952 | tf_op jit(solution)/shard_map/ppermute | solution.py:381
  9.2 1.5 %collective-permute-start.4 = (bf16[288,256]{1,0:T(8,128)(2,1)}, bf16[288,256]{1,0:T(8,128)(2,1)S(1)}, u32[]{:S(2)}, u32[]{:S(2)}) collective-permute-start(bf16[288,256]{1,0:T(8,128)(2,1)} %get-tuple-element.33.dst_ref), channel_id=1, source_target_pairs={{0,2},{1,3},{2,0},{3,1},{4,6},{5,7},{6,4},{7,5},{8,10},{9,11},{10,... | collective-permute-start | bytes 442376 | tf_op jit(solution)/shard_map/ppermute | solution.py:381
  10.7 0.6 %collective-permute-start.7 = (bf16[288,256]{1,0:T(8,128)(2,1)S(1)}, bf16[288,256]{1,0:T(8,128)(2,1)S(1)}, u32[]{:S(2)}, u32[]{:S(2)}) collective-permute-start(bf16[288,256]{1,0:T(8,128)(2,1)S(1)} %paired.1.refs_0_), channel_id=1, source_target_pairs={{0,2},{1,3},{2,0},{3,1},{4,6},{5,7},{6,4},{7,5},{8,10},{9,11},{10,... | collective-permute-start | bytes 442376 | tf_op jit(solution)/shard_map/ppermute | solution.py:381
  11.3 0.9 %copy-done = bf16[304,256]{1,0:T(8,128)(2,1)S(1)} copy-done((bf16[304,256]{1,0:T(8,128)(2,1)S(1)}, bf16[304,256]{1,0:T(8,128)(2,1)}, u32[]{:S(2)}) %copy-start) | copy-done | bytes 155672
  12.2 0.9 %copy-done.1 = bf16[288,256]{1,0:T(8,128)(2,1)S(1)} copy-done((bf16[288,256]{1,0:T(8,128)(2,1)S(1)}, bf16[288,256]{1,0:T(8,128)(2,1)}, u32[]{:S(2)}) %copy-start.1) | copy-done | bytes 147480
  13.2 0.6 %collective-permute-start.6 = (bf16[1,288,256]{2,1,0:T(8,128)(2,1)S(1)}, bf16[1,288,256]{2,1,0:T(8,128)(2,1)S(1)}, u32[]{:S(2)}, u32[]{:S(2)}) collective-permute-start(bf16[1,288,256]{2,1,0:T(8,128)(2,1)S(1)} %stack.6.refs_6_.refs_8_), channel_id=1, source_target_pairs={{0,1},{1,0},{2,3},{3,2},{4,5},{5,4},{6,7},{7,6},{8,9},{9,8},{10,11... | collective-permute-start | bytes 442376 | tf_op jit(solution)/shard_map/ppermute | solution.py:381
  13.8 1.9 %collective-permute-done.4.refs_0_ = bf16[288,256]{1,0:T(8,128)(2,1)S(1)} collective-permute-done((bf16[288,256]{1,0:T(8,128)(2,1)}, bf16[288,256]{1,0:T(8,128)(2,1)S(1)}, u32[]{:S(2)}, u32[]{:S(2)}) %collective-permute-start.4) | collective-permute-done | bytes 147488 | tf_op jit(solution)/shard_map/ppermute | solution.py:381
  16.2 1.1 %collective-permute-done.7.refs_0_ = bf16[288,256]{1,0:T(8,128)(2,1)S(1)} collective-permute-done((bf16[288,256]{1,0:T(8,128)(2,1)S(1)}, bf16[288,256]{1,0:T(8,128)(2,1)S(1)}, u32[]{:S(2)}, u32[]{:S(2)}) %collective-permute-start.7) | collective-permute-done | bytes 147488 | tf_op jit(solution)/shard_map/ppermute | solution.py:381
  17.4 1.6 %scores.2 = (f32[1536,512]{1,0:T(8,128)S(1)}, f32[32,512]{1,0:T(8,128)S(1)}, f32[3,512]{1,0:T(4,128)S(1)}) custom-call(bf16[304,256]{1,0:T(8,128)(2,1)S(1)} %get-tuple-element.34.refs_0_, bf16[304,256]{1,0:T(8,128)(2,1)S(1)} %collective-permute-done.2.refs_1_, bf16[1,288,256]{2,1,0:T(8,128)(2,1)S(1)} %stack.4.refs_2_.refs_4_, ...), custom_call_target="tpu_custom_call" | custom-call | tf_op jit(solution)/shard_map/scores/pallas_call | solution.py:77
  19.0 0.7 %scores.3 = (f32[512,512]{1,0:T(8,128)S(1)}, f32[32,512]{1,0:T(8,128)S(1)}, f32[3,512]{1,0:T(4,128)S(1)}) custom-call(bf16[304,256]{1,0:T(8,128)(2,1)S(1)} %get-tuple-element.34.refs_0_, bf16[304,256]{1,0:T(8,128)(2,1)S(1)} %collective-permute-done.2.refs_1_, bf16[1,288,256]{2,1,0:T(8,128)(2,1)S(1)} %stack.7.refs_2_.refs_8_.refs_10_, ...), custom_call_target="tpu_custom_call" | custom-call | tf_op jit(solution)/shard_map/scores/pallas_call | solution.py:77
  20.1 0.7 %stage.1 = (bf16[512,256]{1,0:T(8,128)(2,1)S(1)}, bf16[32,512]{1,0:T(8,128)(2,1)S(1)}, f32[1536,512]{1,0:T(8,128)S(1)}, f32[512,512]{1,0:T(8,128)S(1)}) custom-call(bf16[304,256]{1,0:T(8,128)(2,1)S(1)} %get-tuple-element.34.refs_0_, bf16[304,256]{1,0:T(8,128)(2,1)S(1)} %collective-permute-done.2.refs_1_, bf16[1,288,256]{2,1,0:T(8,128)(2,1)S(1)} %stack.4.refs_2_.refs_4_, ...), custom_call_target="tpu_custom_call" | custom-call | tf_op jit(solution)/shard_map/stage/pallas_call | solution.py:77
  20.8 3.5 %collective-permute-done.9.refs_5_ = f32[8,256]{1,0:T(8,128)S(1)} collective-permute-done((f32[8,256]{1,0:T(8,128)S(1)}, f32[8,256]{1,0:T(8,128)S(1)}, u32[]{:S(2)}, u32[]{:S(2)}) %collective-permute-start.9) | collective-permute-done | bytes 8224 | tf_op jit(solution)/shard_map/ppermute | solution.py:381
  26.2 0.5 %row_shares.2.refs_0_.one_ref = bf16[288,256]{1,0:T(8,128)(2,1)S(1)} custom-call(bf16[512,512]{1,0:T(8,128)(2,1)S(1)} %get-tuple-element.47.refs_0_, bf16[512,512]{1,0:T(8,128)(2,1)S(1)} %get-tuple-element.49.refs_1_, bf16[512,512]{1,0:T(8,128)(2,1)S(1)} %get-tuple-element.51.refs_2_, bf16[512,512]{1,0:T(8,128)(2,1)S(1)} %get-tuple-element.53.refs_3_, ...), custom_call_target="tpu_custom_call" | custom-call | tf_op jit(solution)/shard_map/row_shares/pallas_call | solution.py:77
  26.8 1.6 %collective-permute-start.12 = (bf16[160,256]{1,0:T(8,128)(2,1)S(1)}, bf16[160,256]{1,0:T(8,128)(2,1)S(1)}, u32[]{:S(2)}, u32[]{:S(2)}) collective-permute-start(bf16[160,256]{1,0:T(8,128)(2,1)S(1)} %fold.5.refs_0_), channel_id=1, source_target_pairs={{0,2},{1,3},{2,0},{3,1},{4,6},{5,7},{6,4},{7,5},{8,10},{9,11},{10,... | collective-permute-start | bytes 245768 | tf_op jit(solution)/shard_map/ppermute | solution.py:381
  28.4 0.6 %collective-permute-start.11 = (bf16[128,256]{1,0:T(8,128)(2,1)S(1)}, bf16[128,256]{1,0:T(8,128)(2,1)S(1)}, u32[]{:S(2)}, u32[]{:S(2)}) collective-permute-start(bf16[128,256]{1,0:T(8,128)(2,1)S(1)} %fold.6.refs_1_.refs_0_), channel_id=1, source_target_pairs={{0,2},{1,3},{2,0},{3,1},{4,6},{5,7},{6,4},{7,5},{8,10},{9,11},{10,... | collective-permute-start | bytes 196616 | tf_op jit(solution)/shard_map/ppermute | solution.py:381
  29.3 2.8 %collective-permute-done.12.refs_0_ = bf16[160,256]{1,0:T(8,128)(2,1)S(1)} collective-permute-done((bf16[160,256]{1,0:T(8,128)(2,1)S(1)}, bf16[160,256]{1,0:T(8,128)(2,1)S(1)}, u32[]{:S(2)}, u32[]{:S(2)}) %collective-permute-start.12) | collective-permute-done | bytes 81952 | tf_op jit(solution)/shard_map/ppermute | solution.py:381
  32.1 1.6 %collective-permute-start.16 = (bf16[160,256]{1,0:T(8,128)(2,1)S(1)}, bf16[160,256]{1,0:T(8,128)(2,1)S(1)}, u32[]{:S(2)}, u32[]{:S(2)}) collective-permute-start(bf16[160,256]{1,0:T(8,128)(2,1)S(1)} %fold.7.refs_1_), channel_id=1, source_target_pairs={{0,4},{1,5},{2,6},{3,7},{4,0},{5,1},{6,2},{7,3},{8,12},{9,13},{10,... | collective-permute-start | bytes 245768 | tf_op jit(solution)/shard_map/ppermute | solution.py:381
  33.8 1.0 %collective-permute-start.15 = (bf16[128,256]{1,0:T(8,128)(2,1)S(1)}, bf16[128,256]{1,0:T(8,128)(2,1)S(1)}, u32[]{:S(2)}, u32[]{:S(2)}) collective-permute-start(bf16[128,256]{1,0:T(8,128)(2,1)S(1)} %fold.8.refs_13_), channel_id=1, source_target_pairs={{0,4},{1,5},{2,6},{3,7},{4,0},{5,1},{6,2},{7,3},{8,12},{9,13},{10,... | collective-permute-start | bytes 196616 | tf_op jit(solution)/shard_map/ppermute | solution.py:381
  35.3 1.6 %collective-permute-start.17 = (bf16[288,256]{1,0:T(8,128)(2,1)S(1)}, bf16[288,256]{1,0:T(8,128)(2,1)S(1)}, u32[]{:S(2)}, u32[]{:S(2)}) collective-permute-start(bf16[288,256]{1,0:T(8,128)(2,1)S(1)} %fold.9), channel_id=1, source_target_pairs={{0,2},{1,3},{2,0},{3,1},{4,6},{5,7},{6,4},{7,5},{8,10},{9,11},{10,... | collective-permute-start | bytes 442376 | tf_op jit(solution)/shard_map/ppermute | solution.py:381
  36.9 2.6 %collective-permute-done.13.one_ref = bf16[288,256]{1,0:T(8,128)(2,1)S(1)} collective-permute-done((bf16[288,256]{1,0:T(8,128)(2,1)S(1)}, bf16[288,256]{1,0:T(8,128)(2,1)S(1)}, u32[]{:S(2)}, u32[]{:S(2)}) %collective-permute-start.13) | collective-permute-done | bytes 147488 | tf_op jit(solution)/shard_map/ppermute | solution.py:381
  39.9 0.6 %collective-permute-done.17.refs_6_ = bf16[288,256]{1,0:T(8,128)(2,1)S(1)} collective-permute-done((bf16[288,256]{1,0:T(8,128)(2,1)S(1)}, bf16[288,256]{1,0:T(8,128)(2,1)S(1)}, u32[]{:S(2)}, u32[]{:S(2)}) %collective-permute-start.17) | collective-permute-done | bytes 147488 | tf_op jit(solution)/shard_map/ppermute | solution.py:381
  40.5 0.8 %totals.1 = (f32[256,256]{1,0:T(8,128)}, bf16[32,256]{1,0:T(8,128)(2,1)}, f32[256,256]{1,0:T(8,128)}, f32[32,256]{1,0:T(8,128)}) custom-call(f32[288,256]{1,0:T(8,128)S(1)} %row_shares.3.refs_0_, bf16[288,256]{1,0:T(8,128)(2,1)S(1)} %hand.5.refs_1_, f32[2,288,256]{2,1,0:T(8,128)S(1)} %get-tuple-element.55.own_ref.refs_2_, ...), custom_call_target="tpu_custom_call" | custom-call | tf_op jit(solution)/shard_map/totals/pallas_call | solution.py:77
  (44 shorter events, 4.4 us)
Async XLA Ops:
  0.6 10.1 %collective-permute-start = (bf16[256,256]{1,0:T(8,128)(2,1)}, bf16[256,256]{1,0:T(8,128)(2,1)S(1)}, u32[]{:S(2)}, u32[]{:S(2)}) collective-permute-start(bf16[256,256]{1,0:T(8,128)(2,1)} %dst_ref.1), channel_id=1, source_target_pairs={{0,4},{1,5},{2,6},{3,7},{4,0},{5,1},{6,2},{7,3},{8,12},{9,13},{10,... | collective-permute-start | bytes 393224 | tf_op jit(solution)/shard_map/ppermute | solution.py:381
  3.7 7.0 %collective-permute-start.1 = (bf16[32,256]{1,0:T(8,128)(2,1)}, bf16[32,256]{1,0:T(8,128)(2,1)S(1)}, u32[]{:S(2)}, u32[]{:S(2)}) collective-permute-start(bf16[32,256]{1,0:T(8,128)(2,1)} %grad_ref.1), channel_id=1, source_target_pairs={{0,4},{1,5},{2,6},{3,7},{4,0},{5,1},{6,2},{7,3},{8,12},{9,13},{10,... | collective-permute-start | bytes 49160 | tf_op jit(solution)/shard_map/ppermute | solution.py:381
  6.2 10.0 %collective-permute-start.2 = (bf16[304,256]{1,0:T(8,128)(2,1)}, bf16[304,256]{1,0:T(8,128)(2,1)S(1)}, u32[]{:S(2)}, u32[]{:S(2)}) collective-permute-start(bf16[304,256]{1,0:T(8,128)(2,1)} %get-tuple-element.32.src_ref), channel_id=1, source_target_pairs={{0,8},{1,9},{2,10},{3,11},{4,12},{5,13},{6,14},{7,15},{8,0},{9,1},... | collective-permute-start | bytes 466952 | tf_op jit(solution)/shard_map/ppermute | solution.py:381
  9.2 6.5 %collective-permute-start.4 = (bf16[288,256]{1,0:T(8,128)(2,1)}, bf16[288,256]{1,0:T(8,128)(2,1)S(1)}, u32[]{:S(2)}, u32[]{:S(2)}) collective-permute-start(bf16[288,256]{1,0:T(8,128)(2,1)} %get-tuple-element.33.dst_ref), channel_id=1, source_target_pairs={{0,2},{1,3},{2,0},{3,1},{4,6},{5,7},{6,4},{7,5},{8,10},{9,11},{10,... | collective-permute-start | bytes 442376 | tf_op jit(solution)/shard_map/ppermute | solution.py:381
  10.7 6.6 %collective-permute-start.7 = (bf16[288,256]{1,0:T(8,128)(2,1)S(1)}, bf16[288,256]{1,0:T(8,128)(2,1)S(1)}, u32[]{:S(2)}, u32[]{:S(2)}) collective-permute-start(bf16[288,256]{1,0:T(8,128)(2,1)S(1)} %paired.1.refs_0_), channel_id=1, source_target_pairs={{0,2},{1,3},{2,0},{3,1},{4,6},{5,7},{6,4},{7,5},{8,10},{9,11},{10,... | collective-permute-start | bytes 442376 | tf_op jit(solution)/shard_map/ppermute | solution.py:381
  11.3 0.9 %copy-start = (bf16[304,256]{1,0:T(8,128)(2,1)S(1)}, bf16[304,256]{1,0:T(8,128)(2,1)}, u32[]{:S(2)}) copy-start(bf16[304,256]{1,0:T(8,128)(2,1)} %get-tuple-element.32.src_ref) | copy-start | bytes 466948
  12.2 0.9 %copy-start.1 = (bf16[288,256]{1,0:T(8,128)(2,1)S(1)}, bf16[288,256]{1,0:T(8,128)(2,1)}, u32[]{:S(2)}) copy-start(bf16[288,256]{1,0:T(8,128)(2,1)} %get-tuple-element.33.dst_ref) | copy-start | bytes 442372
  13.1 4.2 %collective-permute-start.3 = (bf16[1,288,256]{2,1,0:T(8,128)(2,1)S(1)}, bf16[1,288,256]{2,1,0:T(8,128)(2,1)S(1)}, u32[]{:S(2)}, u32[]{:S(2)}) collective-permute-start(bf16[1,288,256]{2,1,0:T(8,128)(2,1)S(1)} %stack.4.refs_2_.refs_4_), channel_id=1, source_target_pairs={{0,1},{1,0},{2,3},{3,2},{4,5},{5,4},{6,7},{7,6},{8,9},{9,8},{10,11... | collective-permute-start | bytes 442376 | tf_op jit(solution)/shard_map/ppermute | solution.py:381
  13.2 4.1 %collective-permute-start.6 = (bf16[1,288,256]{2,1,0:T(8,128)(2,1)S(1)}, bf16[1,288,256]{2,1,0:T(8,128)(2,1)S(1)}, u32[]{:S(2)}, u32[]{:S(2)}) collective-permute-start(bf16[1,288,256]{2,1,0:T(8,128)(2,1)S(1)} %stack.6.refs_6_.refs_8_), channel_id=1, source_target_pairs={{0,1},{1,0},{2,3},{3,2},{4,5},{5,4},{6,7},{7,6},{8,9},{9,8},{10,11... | collective-permute-start | bytes 442376 | tf_op jit(solution)/shard_map/ppermute | solution.py:381
  15.7 1.7 %collective-permute-start.5 = (bf16[1,288,256]{2,1,0:T(8,128)(2,1)S(1)}, bf16[1,288,256]{2,1,0:T(8,128)(2,1)S(1)}, u32[]{:S(2)}, u32[]{:S(2)}) collective-permute-start(bf16[1,288,256]{2,1,0:T(8,128)(2,1)S(1)} %stack.5.refs_4_.refs_6_), channel_id=1, source_target_pairs={{0,1},{1,0},{2,3},{3,2},{4,5},{5,4},{6,7},{7,6},{8,9},{9,8},{10,11... | collective-permute-start | bytes 442376 | tf_op jit(solution)/shard_map/ppermute | solution.py:381
  17.3 1.7 %collective-permute-start.8 = (bf16[1,288,256]{2,1,0:T(8,128)(2,1)S(1)}, bf16[1,288,256]{2,1,0:T(8,128)(2,1)S(1)}, u32[]{:S(2)}, u32[]{:S(2)}) collective-permute-start(bf16[1,288,256]{2,1,0:T(8,128)(2,1)S(1)} %stack.7.refs_2_.refs_8_.refs_10_), channel_id=1, source_target_pairs={{0,1},{1,0},{2,3},{3,2},{4,5},{5,4},{6,7},{7,6},{8,9},{9,8},{10,11... | collective-permute-start | bytes 442376 | tf_op jit(solution)/shard_map/ppermute | solution.py:381
  19.7 4.6 %collective-permute-start.9 = (f32[8,256]{1,0:T(8,128)S(1)}, f32[8,256]{1,0:T(8,128)S(1)}, u32[]{:S(2)}, u32[]{:S(2)}) collective-permute-start(f32[8,256]{1,0:T(8,128)S(1)} %join.1.refs_4_), channel_id=1, source_target_pairs={{0,8},{1,9},{2,10},{3,11},{4,12},{5,13},{6,14},{7,15},{8,0},{9,1},... | collective-permute-start | bytes 24584 | tf_op jit(solution)/shard_map/ppermute | solution.py:381
  24.8 1.9 %collective-permute-start.10 = (bf16[2,288,256]{2,1,0:T(8,128)(2,1)S(1)}, bf16[2,288,256]{2,1,0:T(8,128)(2,1)S(1)}, u32[]{:S(2)}, u32[]{:S(2)}) collective-permute-start(bf16[2,288,256]{2,1,0:T(8,128)(2,1)S(1)} %get-tuple-element.48.refs_6_), channel_id=1, source_target_pairs={{0,1},{1,0},{2,3},{3,2},{4,5},{5,4},{6,7},{7,6},{8,9},{9,8},{10,11... | collective-permute-start | bytes 884744 | tf_op jit(solution)/shard_map/ppermute | solution.py:381
  26.8 5.3 %collective-permute-start.12 = (bf16[160,256]{1,0:T(8,128)(2,1)S(1)}, bf16[160,256]{1,0:T(8,128)(2,1)S(1)}, u32[]{:S(2)}, u32[]{:S(2)}) collective-permute-start(bf16[160,256]{1,0:T(8,128)(2,1)S(1)} %fold.5.refs_0_), channel_id=1, source_target_pairs={{0,2},{1,3},{2,0},{3,1},{4,6},{5,7},{6,4},{7,5},{8,10},{9,11},{10,... | collective-permute-start | bytes 245768 | tf_op jit(solution)/shard_map/ppermute | solution.py:381
  28.4 5.4 %collective-permute-start.11 = (bf16[128,256]{1,0:T(8,128)(2,1)S(1)}, bf16[128,256]{1,0:T(8,128)(2,1)S(1)}, u32[]{:S(2)}, u32[]{:S(2)}) collective-permute-start(bf16[128,256]{1,0:T(8,128)(2,1)S(1)} %fold.6.refs_1_.refs_0_), channel_id=1, source_target_pairs={{0,2},{1,3},{2,0},{3,1},{4,6},{5,7},{6,4},{7,5},{8,10},{9,11},{10,... | collective-permute-start | bytes 196616 | tf_op jit(solution)/shard_map/ppermute | solution.py:381
  28.9 6.3 %collective-permute-start.14 = (bf16[2,288,256]{2,1,0:T(8,128)(2,1)S(1)}, bf16[2,288,256]{2,1,0:T(8,128)(2,1)S(1)}, u32[]{:S(2)}, u32[]{:S(2)}) collective-permute-start(bf16[2,288,256]{2,1,0:T(8,128)(2,1)S(1)} %get-tuple-element.52.refs_6_), channel_id=1, source_target_pairs={{0,1},{1,0},{2,3},{3,2},{4,5},{5,4},{6,7},{7,6},{8,9},{9,8},{10,11... | collective-permute-start | bytes 884744 | tf_op jit(solution)/shard_map/ppermute | solution.py:381
  28.9 10.5 %collective-permute-start.13 = (bf16[288,256]{1,0:T(8,128)(2,1)S(1)}, bf16[288,256]{1,0:T(8,128)(2,1)S(1)}, u32[]{:S(2)}, u32[]{:S(2)}) collective-permute-start(bf16[288,256]{1,0:T(8,128)(2,1)S(1)} %hand.4), channel_id=1, source_target_pairs={{0,8},{1,9},{2,10},{3,11},{4,12},{5,13},{6,14},{7,15},{8,0},{9,1},... | collective-permute-start | bytes 442376 | tf_op jit(solution)/shard_map/ppermute | solution.py:381
  32.1 7.8 %collective-permute-start.16 = (bf16[160,256]{1,0:T(8,128)(2,1)S(1)}, bf16[160,256]{1,0:T(8,128)(2,1)S(1)}, u32[]{:S(2)}, u32[]{:S(2)}) collective-permute-start(bf16[160,256]{1,0:T(8,128)(2,1)S(1)} %fold.7.refs_1_), channel_id=1, source_target_pairs={{0,4},{1,5},{2,6},{3,7},{4,0},{5,1},{6,2},{7,3},{8,12},{9,13},{10,... | collective-permute-start | bytes 245768 | tf_op jit(solution)/shard_map/ppermute | solution.py:381
  33.8 6.2 %collective-permute-start.15 = (bf16[128,256]{1,0:T(8,128)(2,1)S(1)}, bf16[128,256]{1,0:T(8,128)(2,1)S(1)}, u32[]{:S(2)}, u32[]{:S(2)}) collective-permute-start(bf16[128,256]{1,0:T(8,128)(2,1)S(1)} %fold.8.refs_13_), channel_id=1, source_target_pairs={{0,4},{1,5},{2,6},{3,7},{4,0},{5,1},{6,2},{7,3},{8,12},{9,13},{10,... | collective-permute-start | bytes 196616 | tf_op jit(solution)/shard_map/ppermute | solution.py:381
  35.3 5.3 %collective-permute-start.17 = (bf16[288,256]{1,0:T(8,128)(2,1)S(1)}, bf16[288,256]{1,0:T(8,128)(2,1)S(1)}, u32[]{:S(2)}, u32[]{:S(2)}) collective-permute-start(bf16[288,256]{1,0:T(8,128)(2,1)S(1)} %fold.9), channel_id=1, source_target_pairs={{0,2},{1,3},{2,0},{3,1},{4,6},{5,7},{6,4},{7,5},{8,10},{9,11},{10,... | collective-permute-start | bytes 442376 | tf_op jit(solution)/shard_map/ppermute | solution.py:381

commit v4 on v3

--- a/solution.py
+++ b/solution.py
@@ -438,7 +438,6 @@
             ]
         elif t == 4:
             (src_own,) = row_shares(g, [0], f32, changes, order, stacks, belief_sum, last)
-            last = src_own
     grad_src, grad_belief, grad_dst, next_belief = totals(
         g, src_own, src_got, near_own, near_got, got[0][1::-1] + got[0][2:]
     )

time: 41.5 us -> 41 us (0.988)
    ppermute x18, waiting for transfers between devices: 13.3 us -> 12.9 us  [swap(): return lax.ppermute(array, 'src', [(i, i ^ flip) for i in range(n)])]
where the time goes in v4:
time: 41 us; the launch traced here: 40.9 us
  starting transfers between devices  16.1 us (39%)
  waiting for transfers between devices  12.9 us (31%)
  Pallas kernels  8.56 us (21%)
  local copies, waits for them, and re-layouts  1.82 us (4%)
  between operations  1.51 us (4%)
    ppermute x18, starting transfers between devices, swap(): return lax.ppermute(array, 'src', [(i, i ^ flip) for i in range(n)])  16.1 us
    ppermute x18, waiting for transfers between devices, swap(): return lax.ppermute(array, 'src', [(i, i ^ flip) for i in range(n)])  12.9 us
    pallas_call x27, Pallas kernels, call(): pl.pallas_call(kernel, out_shape=out_shape, in_specs=[in_vmem()] * len(op...  6.81 us
    unnamed x4, local copies, waits for them, and re-layouts  1.82 us
    pallas_call x1, Pallas kernels, pack(): pl.pallas_call(functools.partial(pack_kernel, g), out_shape=(shape((g.row...  1.75 us
  transfers between devices with their start and end apart: 18, of which 8 were waited for; matrix products, arithmetic and copies ran while one was open for 0% of the time, Pallas kernels for 16%

profile of v4, /device:TPU:0, one launch (start us, length us, event | category | flops | bytes accessed | tf_op | source)
XLA Modules:
  0.0 40.9 jit_solution(17289986568511163789)
XLA Ops:
  0.6 3.1 %collective-permute-start = (bf16[256,256]{1,0:T(8,128)(2,1)}, bf16[256,256]{1,0:T(8,128)(2,1)S(1)}, u32[]{:S(2)}, u32[]{:S(2)}) collective-permute-start(bf16[256,256]{1,0:T(8,128)(2,1)} %dst_ref.1), channel_id=1, source_target_pairs={{0,4},{1,5},{2,6},{3,7},{4,0},{5,1},{6,2},{7,3},{8,12},{9,13},{10,... | collective-permute-start | bytes 393224 | tf_op jit(solution)/shard_map/ppermute | solution.py:381
  4.5 1.8 %pack.1 = (bf16[304,256]{1,0:T(8,128)(2,1)}, bf16[288,256]{1,0:T(8,128)(2,1)}) custom-call(s32[1,16]{1,0:T(1,128)} %tile_ref.1, s32[1,1]{1,0:T(1,128)} %bitcast.1.count_ref, bf16[256,256]{1,0:T(8,128)(2,1)} %src_ref.1, bf16[32,256]{1,0:T(8,128)(2,1)} %bel_ref.1, bf16[256,256]{1,0:T(8,128)(2,1)} %dst_ref.1, bf16[32,256]{1,0:T(8,128)(2,1)} %grad_ref.1), custom_call_target="tpu_custom_call" | custom-call | tf_op jit(solution)/shard_map/pack/pallas_call | solution.py:103
  6.2 3.0 %collective-permute-start.2 = (bf16[304,256]{1,0:T(8,128)(2,1)}, bf16[304,256]{1,0:T(8,128)(2,1)S(1)}, u32[]{:S(2)}, u32[]{:S(2)}) collective-permute-start(bf16[304,256]{1,0:T(8,128)(2,1)} %get-tuple-element.32.src_ref), channel_id=1, source_target_pairs={{0,8},{1,9},{2,10},{3,11},{4,12},{5,13},{6,14},{7,15},{8,0},{9,1},... | collective-permute-start | bytes 466952 | tf_op jit(solution)/shard_map/ppermute | solution.py:381
  9.2 1.5 %collective-permute-start.4 = (bf16[288,256]{1,0:T(8,128)(2,1)}, bf16[288,256]{1,0:T(8,128)(2,1)S(1)}, u32[]{:S(2)}, u32[]{:S(2)}) collective-permute-start(bf16[288,256]{1,0:T(8,128)(2,1)} %get-tuple-element.33.dst_ref), channel_id=1, source_target_pairs={{0,2},{1,3},{2,0},{3,1},{4,6},{5,7},{6,4},{7,5},{8,10},{9,11},{10,... | collective-permute-start | bytes 442376 | tf_op jit(solution)/shard_map/ppermute | solution.py:381
  10.7 0.6 %collective-permute-start.7 = (bf16[288,256]{1,0:T(8,128)(2,1)S(1)}, bf16[288,256]{1,0:T(8,128)(2,1)S(1)}, u32[]{:S(2)}, u32[]{:S(2)}) collective-permute-start(bf16[288,256]{1,0:T(8,128)(2,1)S(1)} %paired.1.refs_0_), channel_id=1, source_target_pairs={{0,2},{1,3},{2,0},{3,1},{4,6},{5,7},{6,4},{7,5},{8,10},{9,11},{10,... | collective-permute-start | bytes 442376 | tf_op jit(solution)/shard_map/ppermute | solution.py:381
  11.3 0.9 %copy-done = bf16[304,256]{1,0:T(8,128)(2,1)S(1)} copy-done((bf16[304,256]{1,0:T(8,128)(2,1)S(1)}, bf16[304,256]{1,0:T(8,128)(2,1)}, u32[]{:S(2)}) %copy-start) | copy-done | bytes 155672
  12.2 0.9 %copy-done.1 = bf16[288,256]{1,0:T(8,128)(2,1)S(1)} copy-done((bf16[288,256]{1,0:T(8,128)(2,1)S(1)}, bf16[288,256]{1,0:T(8,128)(2,1)}, u32[]{:S(2)}) %copy-start.1) | copy-done | bytes 147480
  13.2 0.6 %collective-permute-start.6 = (bf16[1,288,256]{2,1,0:T(8,128)(2,1)S(1)}, bf16[1,288,256]{2,1,0:T(8,128)(2,1)S(1)}, u32[]{:S(2)}, u32[]{:S(2)}) collective-permute-start(bf16[1,288,256]{2,1,0:T(8,128)(2,1)S(1)} %stack.6.refs_6_.refs_8_), channel_id=1, source_target_pairs={{0,1},{1,0},{2,3},{3,2},{4,5},{5,4},{6,7},{7,6},{8,9},{9,8},{10,11... | collective-permute-start | bytes 442376 | tf_op jit(solution)/shard_map/ppermute | solution.py:381
  13.8 1.9 %collective-permute-done.4.refs_0_ = bf16[288,256]{1,0:T(8,128)(2,1)S(1)} collective-permute-done((bf16[288,256]{1,0:T(8,128)(2,1)}, bf16[288,256]{1,0:T(8,128)(2,1)S(1)}, u32[]{:S(2)}, u32[]{:S(2)}) %collective-permute-start.4) | collective-permute-done | bytes 147488 | tf_op jit(solution)/shard_map/ppermute | solution.py:381
  16.2 1.1 %collective-permute-done.7.refs_0_ = bf16[288,256]{1,0:T(8,128)(2,1)S(1)} collective-permute-done((bf16[288,256]{1,0:T(8,128)(2,1)S(1)}, bf16[288,256]{1,0:T(8,128)(2,1)S(1)}, u32[]{:S(2)}, u32[]{:S(2)}) %collective-permute-start.7) | collective-permute-done | bytes 147488 | tf_op jit(solution)/shard_map/ppermute | solution.py:381
  17.4 1.6 %scores.2 = (f32[1536,512]{1,0:T(8,128)S(1)}, f32[32,512]{1,0:T(8,128)S(1)}, f32[3,512]{1,0:T(4,128)S(1)}) custom-call(bf16[304,256]{1,0:T(8,128)(2,1)S(1)} %get-tuple-element.34.refs_0_, bf16[304,256]{1,0:T(8,128)(2,1)S(1)} %collective-permute-done.2.refs_1_, bf16[1,288,256]{2,1,0:T(8,128)(2,1)S(1)} %stack.4.refs_2_.refs_4_, ...), custom_call_target="tpu_custom_call" | custom-call | tf_op jit(solution)/shard_map/scores/pallas_call | solution.py:77
  19.0 0.7 %scores.3 = (f32[512,512]{1,0:T(8,128)S(1)}, f32[32,512]{1,0:T(8,128)S(1)}, f32[3,512]{1,0:T(4,128)S(1)}) custom-call(bf16[304,256]{1,0:T(8,128)(2,1)S(1)} %get-tuple-element.34.refs_0_, bf16[304,256]{1,0:T(8,128)(2,1)S(1)} %collective-permute-done.2.refs_1_, bf16[1,288,256]{2,1,0:T(8,128)(2,1)S(1)} %stack.7.refs_2_.refs_8_.refs_10_, ...), custom_call_target="tpu_custom_call" | custom-call | tf_op jit(solution)/shard_map/scores/pallas_call | solution.py:77
  20.1 0.7 %stage.1 = (bf16[512,256]{1,0:T(8,128)(2,1)S(1)}, bf16[32,512]{1,0:T(8,128)(2,1)S(1)}, f32[1536,512]{1,0:T(8,128)S(1)}, f32[512,512]{1,0:T(8,128)S(1)}) custom-call(bf16[304,256]{1,0:T(8,128)(2,1)S(1)} %get-tuple-element.34.refs_0_, bf16[304,256]{1,0:T(8,128)(2,1)S(1)} %collective-permute-done.2.refs_1_, bf16[1,288,256]{2,1,0:T(8,128)(2,1)S(1)} %stack.4.refs_2_.refs_4_, ...), custom_call_target="tpu_custom_call" | custom-call | tf_op jit(solution)/shard_map/stage/pallas_call | solution.py:77
  20.8 3.5 %collective-permute-done.9.refs_5_ = f32[8,256]{1,0:T(8,128)S(1)} collective-permute-done((f32[8,256]{1,0:T(8,128)S(1)}, f32[8,256]{1,0:T(8,128)S(1)}, u32[]{:S(2)}, u32[]{:S(2)}) %collective-permute-start.9) | collective-permute-done | bytes 8224 | tf_op jit(solution)/shard_map/ppermute | solution.py:381
  26.2 0.5 %row_shares.2.refs_0_.one_ref = bf16[288,256]{1,0:T(8,128)(2,1)S(1)} custom-call(bf16[512,512]{1,0:T(8,128)(2,1)S(1)} %get-tuple-element.47.refs_0_, bf16[512,512]{1,0:T(8,128)(2,1)S(1)} %get-tuple-element.49.refs_1_, bf16[512,512]{1,0:T(8,128)(2,1)S(1)} %get-tuple-element.51.refs_2_, bf16[512,512]{1,0:T(8,128)(2,1)S(1)} %get-tuple-element.53.refs_3_, ...), custom_call_target="tpu_custom_call" | custom-call | tf_op jit(solution)/shard_map/row_shares/pallas_call | solution.py:77
  26.8 1.6 %collective-permute-start.12 = (bf16[160,256]{1,0:T(8,128)(2,1)S(1)}, bf16[160,256]{1,0:T(8,128)(2,1)S(1)}, u32[]{:S(2)}, u32[]{:S(2)}) collective-permute-start(bf16[160,256]{1,0:T(8,128)(2,1)S(1)} %fold.5.refs_0_), channel_id=1, source_target_pairs={{0,2},{1,3},{2,0},{3,1},{4,6},{5,7},{6,4},{7,5},{8,10},{9,11},{10,... | collective-permute-start | bytes 245768 | tf_op jit(solution)/shard_map/ppermute | solution.py:381
  28.4 0.6 %collective-permute-start.11 = (bf16[128,256]{1,0:T(8,128)(2,1)S(1)}, bf16[128,256]{1,0:T(8,128)(2,1)S(1)}, u32[]{:S(2)}, u32[]{:S(2)}) collective-permute-start(bf16[128,256]{1,0:T(8,128)(2,1)S(1)} %fold.6.refs_1_.refs_0_), channel_id=1, source_target_pairs={{0,2},{1,3},{2,0},{3,1},{4,6},{5,7},{6,4},{7,5},{8,10},{9,11},{10,... | collective-permute-start | bytes 196616 | tf_op jit(solution)/shard_map/ppermute | solution.py:381
  29.3 2.8 %collective-permute-done.12.refs_0_ = bf16[160,256]{1,0:T(8,128)(2,1)S(1)} collective-permute-done((bf16[160,256]{1,0:T(8,128)(2,1)S(1)}, bf16[160,256]{1,0:T(8,128)(2,1)S(1)}, u32[]{:S(2)}, u32[]{:S(2)}) %collective-permute-start.12) | collective-permute-done | bytes 81952 | tf_op jit(solution)/shard_map/ppermute | solution.py:381
  32.1 1.6 %collective-permute-start.16 = (bf16[160,256]{1,0:T(8,128)(2,1)S(1)}, bf16[160,256]{1,0:T(8,128)(2,1)S(1)}, u32[]{:S(2)}, u32[]{:S(2)}) collective-permute-start(bf16[160,256]{1,0:T(8,128)(2,1)S(1)} %fold.7.refs_1_), channel_id=1, source_target_pairs={{0,4},{1,5},{2,6},{3,7},{4,0},{5,1},{6,2},{7,3},{8,12},{9,13},{10,... | collective-permute-start | bytes 245768 | tf_op jit(solution)/shard_map/ppermute | solution.py:381
  33.8 1.0 %collective-permute-start.15 = (bf16[128,256]{1,0:T(8,128)(2,1)S(1)}, bf16[128,256]{1,0:T(8,128)(2,1)S(1)}, u32[]{:S(2)}, u32[]{:S(2)}) collective-permute-start(bf16[128,256]{1,0:T(8,128)(2,1)S(1)} %fold.8.refs_13_.refs_0_), channel_id=1, source_target_pairs={{0,4},{1,5},{2,6},{3,7},{4,0},{5,1},{6,2},{7,3},{8,12},{9,13},{10,... | collective-permute-start | bytes 196616 | tf_op jit(solution)/shard_map/ppermute | solution.py:381
  34.8 1.6 %collective-permute-start.17 = (bf16[288,256]{1,0:T(8,128)(2,1)S(1)}, bf16[288,256]{1,0:T(8,128)(2,1)S(1)}, u32[]{:S(2)}, u32[]{:S(2)}) collective-permute-start(bf16[288,256]{1,0:T(8,128)(2,1)S(1)} %fold.9), channel_id=1, source_target_pairs={{0,2},{1,3},{2,0},{3,1},{4,6},{5,7},{6,4},{7,5},{8,10},{9,11},{10,... | collective-permute-start | bytes 442376 | tf_op jit(solution)/shard_map/ppermute | solution.py:381
  36.4 0.5 %row_shares.3.refs_0_ = f32[288,256]{1,0:T(8,128)S(1)} custom-call(bf16[512,512]{1,0:T(8,128)(2,1)S(1)} %get-tuple-element.47.refs_0_, bf16[512,512]{1,0:T(8,128)(2,1)S(1)} %get-tuple-element.49.refs_1_, bf16[512,512]{1,0:T(8,128)(2,1)S(1)} %get-tuple-element.51.refs_2_, bf16[512,512]{1,0:T(8,128)(2,1)S(1)} %get-tuple-element.53.refs_3_, ...), custom_call_target="tpu_custom_call" | custom-call | tf_op jit(solution)/shard_map/row_shares/pallas_call | solution.py:77
  36.8 2.6 %collective-permute-done.13.one_ref = bf16[288,256]{1,0:T(8,128)(2,1)S(1)} collective-permute-done((bf16[288,256]{1,0:T(8,128)(2,1)S(1)}, bf16[288,256]{1,0:T(8,128)(2,1)S(1)}, u32[]{:S(2)}, u32[]{:S(2)}) %collective-permute-start.13) | collective-permute-done | bytes 147488 | tf_op jit(solution)/shard_map/ppermute | solution.py:381
  40.0 0.8 %totals.1 = (f32[256,256]{1,0:T(8,128)}, bf16[32,256]{1,0:T(8,128)(2,1)}, f32[256,256]{1,0:T(8,128)}, f32[32,256]{1,0:T(8,128)}) custom-call(f32[288,256]{1,0:T(8,128)S(1)} %row_shares.3.refs_0_, bf16[288,256]{1,0:T(8,128)(2,1)S(1)} %hand.5.refs_1_, f32[2,288,256]{2,1,0:T(8,128)S(1)} %get-tuple-element.55.own_ref.refs_2_, ...), custom_call_target="tpu_custom_call" | custom-call | tf_op jit(solution)/shard_map/totals/pallas_call | solution.py:77
  (44 shorter events, 4.0 us)
Async XLA Ops:
  0.6 10.1 %collective-permute-start = (bf16[256,256]{1,0:T(8,128)(2,1)}, bf16[256,256]{1,0:T(8,128)(2,1)S(1)}, u32[]{:S(2)}, u32[]{:S(2)}) collective-permute-start(bf16[256,256]{1,0:T(8,128)(2,1)} %dst_ref.1), channel_id=1, source_target_pairs={{0,4},{1,5},{2,6},{3,7},{4,0},{5,1},{6,2},{7,3},{8,12},{9,13},{10,... | collective-permute-start | bytes 393224 | tf_op jit(solution)/shard_map/ppermute | solution.py:381
  3.7 7.0 %collective-permute-start.1 = (bf16[32,256]{1,0:T(8,128)(2,1)}, bf16[32,256]{1,0:T(8,128)(2,1)S(1)}, u32[]{:S(2)}, u32[]{:S(2)}) collective-permute-start(bf16[32,256]{1,0:T(8,128)(2,1)} %grad_ref.1), channel_id=1, source_target_pairs={{0,4},{1,5},{2,6},{3,7},{4,0},{5,1},{6,2},{7,3},{8,12},{9,13},{10,... | collective-permute-start | bytes 49160 | tf_op jit(solution)/shard_map/ppermute | solution.py:381
  6.2 10.0 %collective-permute-start.2 = (bf16[304,256]{1,0:T(8,128)(2,1)}, bf16[304,256]{1,0:T(8,128)(2,1)S(1)}, u32[]{:S(2)}, u32[]{:S(2)}) collective-permute-start(bf16[304,256]{1,0:T(8,128)(2,1)} %get-tuple-element.32.src_ref), channel_id=1, source_target_pairs={{0,8},{1,9},{2,10},{3,11},{4,12},{5,13},{6,14},{7,15},{8,0},{9,1},... | collective-permute-start | bytes 466952 | tf_op jit(solution)/shard_map/ppermute | solution.py:381
  9.2 6.5 %collective-permute-start.4 = (bf16[288,256]{1,0:T(8,128)(2,1)}, bf16[288,256]{1,0:T(8,128)(2,1)S(1)}, u32[]{:S(2)}, u32[]{:S(2)}) collective-permute-start(bf16[288,256]{1,0:T(8,128)(2,1)} %get-tuple-element.33.dst_ref), channel_id=1, source_target_pairs={{0,2},{1,3},{2,0},{3,1},{4,6},{5,7},{6,4},{7,5},{8,10},{9,11},{10,... | collective-permute-start | bytes 442376 | tf_op jit(solution)/shard_map/ppermute | solution.py:381
  10.7 6.6 %collective-permute-start.7 = (bf16[288,256]{1,0:T(8,128)(2,1)S(1)}, bf16[288,256]{1,0:T(8,128)(2,1)S(1)}, u32[]{:S(2)}, u32[]{:S(2)}) collective-permute-start(bf16[288,256]{1,0:T(8,128)(2,1)S(1)} %paired.1.refs_0_), channel_id=1, source_target_pairs={{0,2},{1,3},{2,0},{3,1},{4,6},{5,7},{6,4},{7,5},{8,10},{9,11},{10,... | collective-permute-start | bytes 442376 | tf_op jit(solution)/shard_map/ppermute | solution.py:381
  11.3 0.9 %copy-start = (bf16[304,256]{1,0:T(8,128)(2,1)S(1)}, bf16[304,256]{1,0:T(8,128)(2,1)}, u32[]{:S(2)}) copy-start(bf16[304,256]{1,0:T(8,128)(2,1)} %get-tuple-element.32.src_ref) | copy-start | bytes 466948
  12.2 0.9 %copy-start.1 = (bf16[288,256]{1,0:T(8,128)(2,1)S(1)}, bf16[288,256]{1,0:T(8,128)(2,1)}, u32[]{:S(2)}) copy-start(bf16[288,256]{1,0:T(8,128)(2,1)} %get-tuple-element.33.dst_ref) | copy-start | bytes 442372
  13.1 4.2 %collective-permute-start.3 = (bf16[1,288,256]{2,1,0:T(8,128)(2,1)S(1)}, bf16[1,288,256]{2,1,0:T(8,128)(2,1)S(1)}, u32[]{:S(2)}, u32[]{:S(2)}) collective-permute-start(bf16[1,288,256]{2,1,0:T(8,128)(2,1)S(1)} %stack.4.refs_2_.refs_4_), channel_id=1, source_target_pairs={{0,1},{1,0},{2,3},{3,2},{4,5},{5,4},{6,7},{7,6},{8,9},{9,8},{10,11... | collective-permute-start | bytes 442376 | tf_op jit(solution)/shard_map/ppermute | solution.py:381
  13.2 4.1 %collective-permute-start.6 = (bf16[1,288,256]{2,1,0:T(8,128)(2,1)S(1)}, bf16[1,288,256]{2,1,0:T(8,128)(2,1)S(1)}, u32[]{:S(2)}, u32[]{:S(2)}) collective-permute-start(bf16[1,288,256]{2,1,0:T(8,128)(2,1)S(1)} %stack.6.refs_6_.refs_8_), channel_id=1, source_target_pairs={{0,1},{1,0},{2,3},{3,2},{4,5},{5,4},{6,7},{7,6},{8,9},{9,8},{10,11... | collective-permute-start | bytes 442376 | tf_op jit(solution)/shard_map/ppermute | solution.py:381
  15.7 1.7 %collective-permute-start.5 = (bf16[1,288,256]{2,1,0:T(8,128)(2,1)S(1)}, bf16[1,288,256]{2,1,0:T(8,128)(2,1)S(1)}, u32[]{:S(2)}, u32[]{:S(2)}) collective-permute-start(bf16[1,288,256]{2,1,0:T(8,128)(2,1)S(1)} %stack.5.refs_4_.refs_6_), channel_id=1, source_target_pairs={{0,1},{1,0},{2,3},{3,2},{4,5},{5,4},{6,7},{7,6},{8,9},{9,8},{10,11... | collective-permute-start | bytes 442376 | tf_op jit(solution)/shard_map/ppermute | solution.py:381
  17.3 1.7 %collective-permute-start.8 = (bf16[1,288,256]{2,1,0:T(8,128)(2,1)S(1)}, bf16[1,288,256]{2,1,0:T(8,128)(2,1)S(1)}, u32[]{:S(2)}, u32[]{:S(2)}) collective-permute-start(bf16[1,288,256]{2,1,0:T(8,128)(2,1)S(1)} %stack.7.refs_2_.refs_8_.refs_10_), channel_id=1, source_target_pairs={{0,1},{1,0},{2,3},{3,2},{4,5},{5,4},{6,7},{7,6},{8,9},{9,8},{10,11... | collective-permute-start | bytes 442376 | tf_op jit(solution)/shard_map/ppermute | solution.py:381
  19.7 4.6 %collective-permute-start.9 = (f32[8,256]{1,0:T(8,128)S(1)}, f32[8,256]{1,0:T(8,128)S(1)}, u32[]{:S(2)}, u32[]{:S(2)}) collective-permute-start(f32[8,256]{1,0:T(8,128)S(1)} %join.1.refs_4_), channel_id=1, source_target_pairs={{0,8},{1,9},{2,10},{3,11},{4,12},{5,13},{6,14},{7,15},{8,0},{9,1},... | collective-permute-start | bytes 24584 | tf_op jit(solution)/shard_map/ppermute | solution.py:381
  24.8 1.9 %collective-permute-start.10 = (bf16[2,288,256]{2,1,0:T(8,128)(2,1)S(1)}, bf16[2,288,256]{2,1,0:T(8,128)(2,1)S(1)}, u32[]{:S(2)}, u32[]{:S(2)}) collective-permute-start(bf16[2,288,256]{2,1,0:T(8,128)(2,1)S(1)} %get-tuple-element.48.refs_6_), channel_id=1, source_target_pairs={{0,1},{1,0},{2,3},{3,2},{4,5},{5,4},{6,7},{7,6},{8,9},{9,8},{10,11... | collective-permute-start | bytes 884744 | tf_op jit(solution)/shard_map/ppermute | solution.py:381
  26.8 5.3 %collective-permute-start.12 = (bf16[160,256]{1,0:T(8,128)(2,1)S(1)}, bf16[160,256]{1,0:T(8,128)(2,1)S(1)}, u32[]{:S(2)}, u32[]{:S(2)}) collective-permute-start(bf16[160,256]{1,0:T(8,128)(2,1)S(1)} %fold.5.refs_0_), channel_id=1, source_target_pairs={{0,2},{1,3},{2,0},{3,1},{4,6},{5,7},{6,4},{7,5},{8,10},{9,11},{10,... | collective-permute-start | bytes 245768 | tf_op jit(solution)/shard_map/ppermute | solution.py:381
  28.4 5.4 %collective-permute-start.11 = (bf16[128,256]{1,0:T(8,128)(2,1)S(1)}, bf16[128,256]{1,0:T(8,128)(2,1)S(1)}, u32[]{:S(2)}, u32[]{:S(2)}) collective-permute-start(bf16[128,256]{1,0:T(8,128)(2,1)S(1)} %fold.6.refs_1_.refs_0_), channel_id=1, source_target_pairs={{0,2},{1,3},{2,0},{3,1},{4,6},{5,7},{6,4},{7,5},{8,10},{9,11},{10,... | collective-permute-start | bytes 196616 | tf_op jit(solution)/shard_map/ppermute | solution.py:381
  28.9 5.8 %collective-permute-start.14 = (bf16[2,288,256]{2,1,0:T(8,128)(2,1)S(1)}, bf16[2,288,256]{2,1,0:T(8,128)(2,1)S(1)}, u32[]{:S(2)}, u32[]{:S(2)}) collective-permute-start(bf16[2,288,256]{2,1,0:T(8,128)(2,1)S(1)} %get-tuple-element.52.refs_6_), channel_id=1, source_target_pairs={{0,1},{1,0},{2,3},{3,2},{4,5},{5,4},{6,7},{7,6},{8,9},{9,8},{10,11... | collective-permute-start | bytes 884744 | tf_op jit(solution)/shard_map/ppermute | solution.py:381
  28.9 10.5 %collective-permute-start.13 = (bf16[288,256]{1,0:T(8,128)(2,1)S(1)}, bf16[288,256]{1,0:T(8,128)(2,1)S(1)}, u32[]{:S(2)}, u32[]{:S(2)}) collective-permute-start(bf16[288,256]{1,0:T(8,128)(2,1)S(1)} %hand.4), channel_id=1, source_target_pairs={{0,8},{1,9},{2,10},{3,11},{4,12},{5,13},{6,14},{7,15},{8,0},{9,1},... | collective-permute-start | bytes 442376 | tf_op jit(solution)/shard_map/ppermute | solution.py:381
  32.1 7.8 %collective-permute-start.16 = (bf16[160,256]{1,0:T(8,128)(2,1)S(1)}, bf16[160,256]{1,0:T(8,128)(2,1)S(1)}, u32[]{:S(2)}, u32[]{:S(2)}) collective-permute-start(bf16[160,256]{1,0:T(8,128)(2,1)S(1)} %fold.7.refs_1_), channel_id=1, source_target_pairs={{0,4},{1,5},{2,6},{3,7},{4,0},{5,1},{6,2},{7,3},{8,12},{9,13},{10,... | collective-permute-start | bytes 245768 | tf_op jit(solution)/shard_map/ppermute | solution.py:381
  33.8 6.2 %collective-permute-start.15 = (bf16[128,256]{1,0:T(8,128)(2,1)S(1)}, bf16[128,256]{1,0:T(8,128)(2,1)S(1)}, u32[]{:S(2)}, u32[]{:S(2)}) collective-permute-start(bf16[128,256]{1,0:T(8,128)(2,1)S(1)} %fold.8.refs_13_.refs_0_), channel_id=1, source_target_pairs={{0,4},{1,5},{2,6},{3,7},{4,0},{5,1},{6,2},{7,3},{8,12},{9,13},{10,... | collective-permute-start | bytes 196616 | tf_op jit(solution)/shard_map/ppermute | solution.py:381
  34.8 5.3 %collective-permute-start.17 = (bf16[288,256]{1,0:T(8,128)(2,1)S(1)}, bf16[288,256]{1,0:T(8,128)(2,1)S(1)}, u32[]{:S(2)}, u32[]{:S(2)}) collective-permute-start(bf16[288,256]{1,0:T(8,128)(2,1)S(1)} %fold.9), channel_id=1, source_target_pairs={{0,2},{1,3},{2,0},{3,1},{4,6},{5,7},{6,4},{7,5},{8,10},{9,11},{10,... | collective-permute-start | bytes 442376 | tf_op jit(solution)/shard_map/ppermute | solution.py:381

commit v5 on v0

--- a/solution.py
+++ b/solution.py
@@ -70,7 +70,7 @@
 shape = jax.ShapeDtypeStruct
 
 
-def call(name, kernel, out_shape, operands, after=(), scratch=(), limit=8 * mib):
+def call(name, kernel, out_shape, operands, after=(), scratch=(), limit=8 * mib, cost=None):
     many = isinstance(out_shape, tuple)
     return pl.pallas_call(
         kernel,
@@ -79,6 +79,7 @@
         out_specs=(in_vmem(),) * len(out_shape) if many else in_vmem(),
         scratch_shapes=list(scratch),
         compiler_params=pltpu.CompilerParams(vmem_limit_bytes=limit),
+        cost_estimate=cost,
         name=name,
     )(*operands, *after)
 
@@ -327,14 +328,14 @@
     return call("row_shares", kernel, outs, operands, after, limit=g.n * rows * rows * 4 + 6 * mib)
 
 
-def fold(own, near, i, others, *after):
+def fold(own, near, i, others, cost, *after):
     def kernel(own_ref, near_ref, *refs):
         total = own_ref[i] + near_ref[i].astype(f32)
         for one in refs[: len(others)]:
             total = total + one[...].astype(f32)
         refs[-1][...] = total.astype(bf16)
 
-    return call("fold", kernel, shape(own.shape[1:], bf16), [own, near, *others], after)
+    return call("fold", kernel, shape(own.shape[1:], bf16), [own, near, *others], after, cost=cost)
 
 
 def totals(g, src_own, src_others, dst_own, dst_near, dst_others):
@@ -410,7 +411,8 @@
     last = near_send
     for t in reversed(range(2, g.n_col, 2)):
         own, near, slots = (far_own, far_got, g.far) if t in g.far else (near_own, near_got, g.near)
-        send = fold(own, near, slots.index(t), got[t], last)
+        slow = pl.CostEstimate(flops=3 * 10**9, bytes_accessed=1 << 20, transcendentals=0)
+        send = fold(own, near, slots.index(t), got[t], slow if low_bit(t) > 2 else None, last)
         one = swap(send, low_bit(t))
         got[t ^ low_bit(t)].append(hand(one) if low_bit(t) > 2 else one)
         if t == g.n_col - 2:
@@ -419,7 +421,6 @@
             src_got = [swap(one, g.row_flip(s)) for one, s in zip(src_send, rest)]
         elif t == 4:
             (src_own,) = row_shares(g, [0], f32, changes, order, stacks, belief_sum, send)
-            send = src_own
         last = send
     grad_src, grad_belief, grad_dst, next_belief = totals(
         g, src_own, src_got, near_own, near_got, got[0]

time: 40.9 us -> 40.8 us (level)
  starting transfers between devices: 15.1 us -> 14.6 us
    ppermute x16, starting transfers between devices: 15.1 us -> 14.6 us  [swap(): return lax.ppermute(array, 'src', [(i, i ^ flip) for i in range(n)])]
    ppermute x16, waiting for transfers between devices: 13.8 us -> 14.2 us  [swap(): return lax.ppermute(array, 'src', [(i, i ^ flip) for i in range(n)])]
  transfers between devices with their start and end apart: 16 -> 16, of which waited for: 8 -> 7; matrix products, arithmetic and copies ran while one was open for 0% -> 0% of each run, Pallas kernels for 16% -> 16%
where the time goes in v5:
time: 40.8 us; the launch traced here: 40.7 us
  starting transfers between devices  14.6 us (36%)
  waiting for transfers between devices  14.2 us (35%)
  Pallas kernels  8.56 us (21%)
  local copies, waits for them, and re-layouts  1.82 us (4%)
  between operations  1.49 us (4%)
    ppermute x16, starting transfers between devices, swap(): return lax.ppermute(array, 'src', [(i, i ^ flip) for i in range(n)])  14.6 us
    ppermute x16, waiting for transfers between devices, swap(): return lax.ppermute(array, 'src', [(i, i ^ flip) for i in range(n)])  14.2 us
    pallas_call x22, Pallas kernels, call(): pl.pallas_call(kernel, out_shape=out_shape, in_specs=[in_vmem()] * len(op...  6.81 us
    unnamed x4, local copies, waits for them, and re-layouts  1.82 us
    pallas_call x1, Pallas kernels, pack(): pl.pallas_call(functools.partial(pack_kernel, g), out_shape=(shape((g.row...  1.75 us
  transfers between devices with their start and end apart: 16, of which 7 were waited for; matrix products, arithmetic and copies ran while one was open for 0% of the time, Pallas kernels for 16%

profile of v5, /device:TPU:0, one launch (start us, length us, event | category | flops | bytes accessed | tf_op | source)
XLA Modules:
  0.0 40.7 jit_solution(7469586471522914864)
XLA Ops:
  0.6 3.1 %collective-permute-start = (bf16[256,256]{1,0:T(8,128)(2,1)}, bf16[256,256]{1,0:T(8,128)(2,1)S(1)}, u32[]{:S(2)}, u32[]{:S(2)}) collective-permute-start(bf16[256,256]{1,0:T(8,128)(2,1)} %dst_ref.1), channel_id=1, source_target_pairs={{0,4},{1,5},{2,6},{3,7},{4,0},{5,1},{6,2},{7,3},{8,12},{9,13},{10,... | collective-permute-start | bytes 393224 | tf_op jit(solution)/shard_map/ppermute | solution.py:371
  4.5 1.8 %pack.1 = (bf16[304,256]{1,0:T(8,128)(2,1)}, bf16[288,256]{1,0:T(8,128)(2,1)}) custom-call(s32[1,16]{1,0:T(1,128)} %tile_ref.1, s32[1,1]{1,0:T(1,128)} %bitcast.1.count_ref, bf16[256,256]{1,0:T(8,128)(2,1)} %src_ref.1, bf16[32,256]{1,0:T(8,128)(2,1)} %bel_ref.1, bf16[256,256]{1,0:T(8,128)(2,1)} %dst_ref.1, bf16[32,256]{1,0:T(8,128)(2,1)} %grad_ref.1), custom_call_target="tpu_custom_call" | custom-call | tf_op jit(solution)/shard_map/pack/pallas_call | solution.py:101
  6.2 3.0 %collective-permute-start.2 = (bf16[304,256]{1,0:T(8,128)(2,1)}, bf16[304,256]{1,0:T(8,128)(2,1)S(1)}, u32[]{:S(2)}, u32[]{:S(2)}) collective-permute-start(bf16[304,256]{1,0:T(8,128)(2,1)} %get-tuple-element.32.src_ref), channel_id=1, source_target_pairs={{0,8},{1,9},{2,10},{3,11},{4,12},{5,13},{6,14},{7,15},{8,0},{9,1},... | collective-permute-start | bytes 466952 | tf_op jit(solution)/shard_map/ppermute | solution.py:371
  9.2 1.5 %collective-permute-start.4 = (bf16[288,256]{1,0:T(8,128)(2,1)}, bf16[288,256]{1,0:T(8,128)(2,1)S(1)}, u32[]{:S(2)}, u32[]{:S(2)}) collective-permute-start(bf16[288,256]{1,0:T(8,128)(2,1)} %get-tuple-element.33.dst_ref), channel_id=1, source_target_pairs={{0,2},{1,3},{2,0},{3,1},{4,6},{5,7},{6,4},{7,5},{8,10},{9,11},{10,... | collective-permute-start | bytes 442376 | tf_op jit(solution)/shard_map/ppermute | solution.py:371
  10.7 0.6 %collective-permute-start.7 = (bf16[288,256]{1,0:T(8,128)(2,1)S(1)}, bf16[288,256]{1,0:T(8,128)(2,1)S(1)}, u32[]{:S(2)}, u32[]{:S(2)}) collective-permute-start(bf16[288,256]{1,0:T(8,128)(2,1)S(1)} %paired.1.refs_0_), channel_id=1, source_target_pairs={{0,2},{1,3},{2,0},{3,1},{4,6},{5,7},{6,4},{7,5},{8,10},{9,11},{10,... | collective-permute-start | bytes 442376 | tf_op jit(solution)/shard_map/ppermute | solution.py:371
  11.3 0.9 %copy-done = bf16[304,256]{1,0:T(8,128)(2,1)S(1)} copy-done((bf16[304,256]{1,0:T(8,128)(2,1)S(1)}, bf16[304,256]{1,0:T(8,128)(2,1)}, u32[]{:S(2)}) %copy-start) | copy-done | bytes 155672
  12.2 0.9 %copy-done.1 = bf16[288,256]{1,0:T(8,128)(2,1)S(1)} copy-done((bf16[288,256]{1,0:T(8,128)(2,1)S(1)}, bf16[288,256]{1,0:T(8,128)(2,1)}, u32[]{:S(2)}) %copy-start.1) | copy-done | bytes 147480
  13.2 0.5 %collective-permute-start.3 = (bf16[1,288,256]{2,1,0:T(8,128)(2,1)S(1)}, bf16[1,288,256]{2,1,0:T(8,128)(2,1)S(1)}, u32[]{:S(2)}, u32[]{:S(2)}) collective-permute-start(bf16[1,288,256]{2,1,0:T(8,128)(2,1)S(1)} %stack.4.refs_2_.refs_4_), channel_id=1, source_target_pairs={{0,1},{1,0},{2,3},{3,2},{4,5},{5,4},{6,7},{7,6},{8,9},{9,8},{10,11... | collective-permute-start | bytes 442376 | tf_op jit(solution)/shard_map/ppermute | solution.py:371
  13.7 2.0 %collective-permute-done.4.refs_0_ = bf16[288,256]{1,0:T(8,128)(2,1)S(1)} collective-permute-done((bf16[288,256]{1,0:T(8,128)(2,1)}, bf16[288,256]{1,0:T(8,128)(2,1)S(1)}, u32[]{:S(2)}, u32[]{:S(2)}) %collective-permute-start.4) | collective-permute-done | bytes 147488 | tf_op jit(solution)/shard_map/ppermute | solution.py:371
  16.2 1.1 %collective-permute-done.7.refs_0_ = bf16[288,256]{1,0:T(8,128)(2,1)S(1)} collective-permute-done((bf16[288,256]{1,0:T(8,128)(2,1)S(1)}, bf16[288,256]{1,0:T(8,128)(2,1)S(1)}, u32[]{:S(2)}, u32[]{:S(2)}) %collective-permute-start.7) | collective-permute-done | bytes 147488 | tf_op jit(solution)/shard_map/ppermute | solution.py:371
  17.4 1.6 %scores.2 = (f32[1536,512]{1,0:T(8,128)S(1)}, f32[32,512]{1,0:T(8,128)S(1)}, f32[3,512]{1,0:T(4,128)S(1)}) custom-call(bf16[304,256]{1,0:T(8,128)(2,1)S(1)} %get-tuple-element.34.refs_0_, bf16[304,256]{1,0:T(8,128)(2,1)S(1)} %collective-permute-done.2.refs_1_, bf16[1,288,256]{2,1,0:T(8,128)(2,1)S(1)} %stack.4.refs_2_.refs_4_, ...), custom_call_target="tpu_custom_call" | custom-call | tf_op jit(solution)/shard_map/scores/pallas_call | solution.py:75
  19.0 0.7 %scores.3 = (f32[512,512]{1,0:T(8,128)S(1)}, f32[32,512]{1,0:T(8,128)S(1)}, f32[3,512]{1,0:T(4,128)S(1)}) custom-call(bf16[304,256]{1,0:T(8,128)(2,1)S(1)} %get-tuple-element.34.refs_0_, bf16[304,256]{1,0:T(8,128)(2,1)S(1)} %collective-permute-done.2.refs_1_, bf16[1,288,256]{2,1,0:T(8,128)(2,1)S(1)} %stack.7.refs_2_.refs_8_.refs_10_, ...), custom_call_target="tpu_custom_call" | custom-call | tf_op jit(solution)/shard_map/scores/pallas_call | solution.py:75
  20.1 0.7 %stage.1 = (bf16[512,256]{1,0:T(8,128)(2,1)S(1)}, bf16[32,512]{1,0:T(8,128)(2,1)S(1)}, f32[1536,512]{1,0:T(8,128)S(1)}, f32[512,512]{1,0:T(8,128)S(1)}) custom-call(bf16[304,256]{1,0:T(8,128)(2,1)S(1)} %get-tuple-element.34.refs_0_, bf16[304,256]{1,0:T(8,128)(2,1)S(1)} %collective-permute-done.2.refs_1_, bf16[1,288,256]{2,1,0:T(8,128)(2,1)S(1)} %stack.4.refs_2_.refs_4_, ...), custom_call_target="tpu_custom_call" | custom-call | tf_op jit(solution)/shard_map/stage/pallas_call | solution.py:75
  20.8 3.5 %collective-permute-done.9.refs_5_ = f32[8,256]{1,0:T(8,128)S(1)} collective-permute-done((f32[8,256]{1,0:T(8,128)S(1)}, f32[8,256]{1,0:T(8,128)S(1)}, u32[]{:S(2)}, u32[]{:S(2)}) %collective-permute-start.9) | collective-permute-done | bytes 8224 | tf_op jit(solution)/shard_map/ppermute | solution.py:371
  25.4 0.4 %column_shares.6 = (bf16[512,512]{1,0:T(8,128)(2,1)S(1)}, bf16[2,288,256]{2,1,0:T(8,128)(2,1)S(1)}) custom-call(f32[8,512]{1,0:T(8,128)S(1)} %get-tuple-element.40.factors, f32[1536,512]{1,0:T(8,128)S(1)} %get-tuple-element.41.refs_0_, f32[512,512]{1,0:T(8,128)S(1)} %get-tuple-element.42.refs_1_, f32[1536,512]{1,0:T(8,128)S(1)} %get-tuple-element.43.refs_2_, ...), custom_call_target="tpu_custom_call" | custom-call | tf_op jit(solution)/shard_map/column_shares/pallas_call | solution.py:75
  25.8 0.7 %collective-permute-done.10.near_ref = bf16[2,288,256]{2,1,0:T(8,128)(2,1)S(1)} collective-permute-done((bf16[2,288,256]{2,1,0:T(8,128)(2,1)S(1)}, bf16[2,288,256]{2,1,0:T(8,128)(2,1)S(1)}, u32[]{:S(2)}, u32[]{:S(2)}) %collective-permute-start.10) | collective-permute-done | bytes 294944 | tf_op jit(solution)/shard_map/ppermute | solution.py:371
  26.5 1.6 %collective-permute-start.11 = (bf16[288,256]{1,0:T(8,128)(2,1)S(1)}, bf16[288,256]{1,0:T(8,128)(2,1)S(1)}, u32[]{:S(2)}, u32[]{:S(2)}) collective-permute-start(bf16[288,256]{1,0:T(8,128)(2,1)S(1)} %fold.3.refs_1_.refs_13_), channel_id=1, source_target_pairs={{0,2},{1,3},{2,0},{3,1},{4,6},{5,7},{6,4},{7,5},{8,10},{9,11},{10,... | collective-permute-start | bytes 442376 | tf_op jit(solution)/shard_map/ppermute | solution.py:371
  28.5 0.5 %row_shares.3 = bf16[288,256]{1,0:T(8,128)(2,1)S(1)} custom-call(bf16[512,512]{1,0:T(8,128)(2,1)S(1)} %get-tuple-element.47.refs_0_, bf16[512,512]{1,0:T(8,128)(2,1)S(1)} %get-tuple-element.49.refs_1_, bf16[512,512]{1,0:T(8,128)(2,1)S(1)} %get-tuple-element.51.refs_2_, bf16[512,512]{1,0:T(8,128)(2,1)S(1)} %get-tuple-element.53.refs_3_, ...), custom_call_target="tpu_custom_call" | custom-call | tf_op jit(solution)/shard_map/row_shares/pallas_call | solution.py:75
  29.4 3.0 %collective-permute-done.11.refs_0_ = bf16[288,256]{1,0:T(8,128)(2,1)S(1)} collective-permute-done((bf16[288,256]{1,0:T(8,128)(2,1)S(1)}, bf16[288,256]{1,0:T(8,128)(2,1)S(1)}, u32[]{:S(2)}, u32[]{:S(2)}) %collective-permute-start.11) | collective-permute-done | bytes 147488 | tf_op jit(solution)/shard_map/ppermute | solution.py:371
  32.5 1.6 %collective-permute-start.14 = (bf16[288,256]{1,0:T(8,128)(2,1)S(1)}, bf16[288,256]{1,0:T(8,128)(2,1)S(1)}, u32[]{:S(2)}, u32[]{:S(2)}) collective-permute-start(bf16[288,256]{1,0:T(8,128)(2,1)S(1)} %fold.4.refs_13_.refs_0_), channel_id=1, source_target_pairs={{0,4},{1,5},{2,6},{3,7},{4,0},{5,1},{6,2},{7,3},{8,12},{9,13},{10,... | collective-permute-start | bytes 442376 | tf_op jit(solution)/shard_map/ppermute | solution.py:371
  34.2 1.6 %collective-permute-start.15 = (bf16[288,256]{1,0:T(8,128)(2,1)S(1)}, bf16[288,256]{1,0:T(8,128)(2,1)S(1)}, u32[]{:S(2)}, u32[]{:S(2)}) collective-permute-start(bf16[288,256]{1,0:T(8,128)(2,1)S(1)} %fold.5), channel_id=1, source_target_pairs={{0,2},{1,3},{2,0},{3,1},{4,6},{5,7},{6,4},{7,5},{8,10},{9,11},{10,... | collective-permute-start | bytes 442376 | tf_op jit(solution)/shard_map/ppermute | solution.py:371
  35.8 0.5 %row_shares.2.refs_0_ = f32[288,256]{1,0:T(8,128)S(1)} custom-call(bf16[512,512]{1,0:T(8,128)(2,1)S(1)} %get-tuple-element.47.refs_0_, bf16[512,512]{1,0:T(8,128)(2,1)S(1)} %get-tuple-element.49.refs_1_, bf16[512,512]{1,0:T(8,128)(2,1)S(1)} %get-tuple-element.51.refs_2_, bf16[512,512]{1,0:T(8,128)(2,1)S(1)} %get-tuple-element.53.refs_3_, ...), custom_call_target="tpu_custom_call" | custom-call | tf_op jit(solution)/shard_map/row_shares/pallas_call | solution.py:75
  36.3 3.5 %collective-permute-done.14.one_ref = bf16[288,256]{1,0:T(8,128)(2,1)S(1)} collective-permute-done((bf16[288,256]{1,0:T(8,128)(2,1)S(1)}, bf16[288,256]{1,0:T(8,128)(2,1)S(1)}, u32[]{:S(2)}, u32[]{:S(2)}) %collective-permute-start.14) | collective-permute-done | bytes 147488 | tf_op jit(solution)/shard_map/ppermute | solution.py:371
  39.8 0.8 %totals.1 = (f32[256,256]{1,0:T(8,128)}, bf16[32,256]{1,0:T(8,128)(2,1)}, f32[256,256]{1,0:T(8,128)}, f32[32,256]{1,0:T(8,128)}) custom-call(f32[288,256]{1,0:T(8,128)S(1)} %row_shares.2.refs_0_, bf16[288,256]{1,0:T(8,128)(2,1)S(1)} %collective-permute-done.12.refs_1_, f32[2,288,256]{2,1,0:T(8,128)S(1)} %get-tuple-element.55.own_ref.refs_2_, ...), custom_call_target="tpu_custom_call" | custom-call | tf_op jit(solution)/shard_map/totals/pallas_call | solution.py:75
  (35 shorter events, 3.1 us)
Async XLA Ops:
  0.6 10.1 %collective-permute-start = (bf16[256,256]{1,0:T(8,128)(2,1)}, bf16[256,256]{1,0:T(8,128)(2,1)S(1)}, u32[]{:S(2)}, u32[]{:S(2)}) collective-permute-start(bf16[256,256]{1,0:T(8,128)(2,1)} %dst_ref.1), channel_id=1, source_target_pairs={{0,4},{1,5},{2,6},{3,7},{4,0},{5,1},{6,2},{7,3},{8,12},{9,13},{10,... | collective-permute-start | bytes 393224 | tf_op jit(solution)/shard_map/ppermute | solution.py:371
  3.7 7.0 %collective-permute-start.1 = (bf16[32,256]{1,0:T(8,128)(2,1)}, bf16[32,256]{1,0:T(8,128)(2,1)S(1)}, u32[]{:S(2)}, u32[]{:S(2)}) collective-permute-start(bf16[32,256]{1,0:T(8,128)(2,1)} %grad_ref.1), channel_id=1, source_target_pairs={{0,4},{1,5},{2,6},{3,7},{4,0},{5,1},{6,2},{7,3},{8,12},{9,13},{10,... | collective-permute-start | bytes 49160 | tf_op jit(solution)/shard_map/ppermute | solution.py:371
  6.2 10.0 %collective-permute-start.2 = (bf16[304,256]{1,0:T(8,128)(2,1)}, bf16[304,256]{1,0:T(8,128)(2,1)S(1)}, u32[]{:S(2)}, u32[]{:S(2)}) collective-permute-start(bf16[304,256]{1,0:T(8,128)(2,1)} %get-tuple-element.32.src_ref), channel_id=1, source_target_pairs={{0,8},{1,9},{2,10},{3,11},{4,12},{5,13},{6,14},{7,15},{8,0},{9,1},... | collective-permute-start | bytes 466952 | tf_op jit(solution)/shard_map/ppermute | solution.py:371
  9.2 6.5 %collective-permute-start.4 = (bf16[288,256]{1,0:T(8,128)(2,1)}, bf16[288,256]{1,0:T(8,128)(2,1)S(1)}, u32[]{:S(2)}, u32[]{:S(2)}) collective-permute-start(bf16[288,256]{1,0:T(8,128)(2,1)} %get-tuple-element.33.dst_ref), channel_id=1, source_target_pairs={{0,2},{1,3},{2,0},{3,1},{4,6},{5,7},{6,4},{7,5},{8,10},{9,11},{10,... | collective-permute-start | bytes 442376 | tf_op jit(solution)/shard_map/ppermute | solution.py:371
  10.7 6.6 %collective-permute-start.7 = (bf16[288,256]{1,0:T(8,128)(2,1)S(1)}, bf16[288,256]{1,0:T(8,128)(2,1)S(1)}, u32[]{:S(2)}, u32[]{:S(2)}) collective-permute-start(bf16[288,256]{1,0:T(8,128)(2,1)S(1)} %paired.1.refs_0_), channel_id=1, source_target_pairs={{0,2},{1,3},{2,0},{3,1},{4,6},{5,7},{6,4},{7,5},{8,10},{9,11},{10,... | collective-permute-start | bytes 442376 | tf_op jit(solution)/shard_map/ppermute | solution.py:371
  11.3 0.9 %copy-start = (bf16[304,256]{1,0:T(8,128)(2,1)S(1)}, bf16[304,256]{1,0:T(8,128)(2,1)}, u32[]{:S(2)}) copy-start(bf16[304,256]{1,0:T(8,128)(2,1)} %get-tuple-element.32.src_ref) | copy-start | bytes 466948
  12.2 0.9 %copy-start.1 = (bf16[288,256]{1,0:T(8,128)(2,1)S(1)}, bf16[288,256]{1,0:T(8,128)(2,1)}, u32[]{:S(2)}) copy-start(bf16[288,256]{1,0:T(8,128)(2,1)} %get-tuple-element.33.dst_ref) | copy-start | bytes 442372
  13.2 4.2 %collective-permute-start.6 = (bf16[1,288,256]{2,1,0:T(8,128)(2,1)S(1)}, bf16[1,288,256]{2,1,0:T(8,128)(2,1)S(1)}, u32[]{:S(2)}, u32[]{:S(2)}) collective-permute-start(bf16[1,288,256]{2,1,0:T(8,128)(2,1)S(1)} %stack.6.refs_6_.refs_8_), channel_id=1, source_target_pairs={{0,1},{1,0},{2,3},{3,2},{4,5},{5,4},{6,7},{7,6},{8,9},{9,8},{10,11... | collective-permute-start | bytes 442376 | tf_op jit(solution)/shard_map/ppermute | solution.py:371
  13.2 4.1 %collective-permute-start.3 = (bf16[1,288,256]{2,1,0:T(8,128)(2,1)S(1)}, bf16[1,288,256]{2,1,0:T(8,128)(2,1)S(1)}, u32[]{:S(2)}, u32[]{:S(2)}) collective-permute-start(bf16[1,288,256]{2,1,0:T(8,128)(2,1)S(1)} %stack.4.refs_2_.refs_4_), channel_id=1, source_target_pairs={{0,1},{1,0},{2,3},{3,2},{4,5},{5,4},{6,7},{7,6},{8,9},{9,8},{10,11... | collective-permute-start | bytes 442376 | tf_op jit(solution)/shard_map/ppermute | solution.py:371
  15.7 1.7 %collective-permute-start.5 = (bf16[1,288,256]{2,1,0:T(8,128)(2,1)S(1)}, bf16[1,288,256]{2,1,0:T(8,128)(2,1)S(1)}, u32[]{:S(2)}, u32[]{:S(2)}) collective-permute-start(bf16[1,288,256]{2,1,0:T(8,128)(2,1)S(1)} %stack.5.refs_4_.refs_6_), channel_id=1, source_target_pairs={{0,1},{1,0},{2,3},{3,2},{4,5},{5,4},{6,7},{7,6},{8,9},{9,8},{10,11... | collective-permute-start | bytes 442376 | tf_op jit(solution)/shard_map/ppermute | solution.py:371
  17.3 1.7 %collective-permute-start.8 = (bf16[1,288,256]{2,1,0:T(8,128)(2,1)S(1)}, bf16[1,288,256]{2,1,0:T(8,128)(2,1)S(1)}, u32[]{:S(2)}, u32[]{:S(2)}) collective-permute-start(bf16[1,288,256]{2,1,0:T(8,128)(2,1)S(1)} %stack.7.refs_2_.refs_8_.refs_10_), channel_id=1, source_target_pairs={{0,1},{1,0},{2,3},{3,2},{4,5},{5,4},{6,7},{7,6},{8,9},{9,8},{10,11... | collective-permute-start | bytes 442376 | tf_op jit(solution)/shard_map/ppermute | solution.py:371
  19.7 4.6 %collective-permute-start.9 = (f32[8,256]{1,0:T(8,128)S(1)}, f32[8,256]{1,0:T(8,128)S(1)}, u32[]{:S(2)}, u32[]{:S(2)}) collective-permute-start(f32[8,256]{1,0:T(8,128)S(1)} %join.1.refs_4_), channel_id=1, source_target_pairs={{0,8},{1,9},{2,10},{3,11},{4,12},{5,13},{6,14},{7,15},{8,0},{9,1},... | collective-permute-start | bytes 24584 | tf_op jit(solution)/shard_map/ppermute | solution.py:371
  24.8 1.6 %collective-permute-start.10 = (bf16[2,288,256]{2,1,0:T(8,128)(2,1)S(1)}, bf16[2,288,256]{2,1,0:T(8,128)(2,1)S(1)}, u32[]{:S(2)}, u32[]{:S(2)}) collective-permute-start(bf16[2,288,256]{2,1,0:T(8,128)(2,1)S(1)} %get-tuple-element.48.refs_6_), channel_id=1, source_target_pairs={{0,1},{1,0},{2,3},{3,2},{4,5},{5,4},{6,7},{7,6},{8,9},{9,8},{10,11... | collective-permute-start | bytes 884744 | tf_op jit(solution)/shard_map/ppermute | solution.py:371
  26.5 6.0 %collective-permute-start.11 = (bf16[288,256]{1,0:T(8,128)(2,1)S(1)}, bf16[288,256]{1,0:T(8,128)(2,1)S(1)}, u32[]{:S(2)}, u32[]{:S(2)}) collective-permute-start(bf16[288,256]{1,0:T(8,128)(2,1)S(1)} %fold.3.refs_1_.refs_13_), channel_id=1, source_target_pairs={{0,2},{1,3},{2,0},{3,1},{4,6},{5,7},{6,4},{7,5},{8,10},{9,11},{10,... | collective-permute-start | bytes 442376 | tf_op jit(solution)/shard_map/ppermute | solution.py:371
  28.1 6.1 %collective-permute-start.13 = (bf16[2,288,256]{2,1,0:T(8,128)(2,1)S(1)}, bf16[2,288,256]{2,1,0:T(8,128)(2,1)S(1)}, u32[]{:S(2)}, u32[]{:S(2)}) collective-permute-start(bf16[2,288,256]{2,1,0:T(8,128)(2,1)S(1)} %get-tuple-element.52.refs_6_.refs_0_), channel_id=1, source_target_pairs={{0,1},{1,0},{2,3},{3,2},{4,5},{5,4},{6,7},{7,6},{8,9},{9,8},{10,11... | collective-permute-start | bytes 884744 | tf_op jit(solution)/shard_map/ppermute | solution.py:371
  29.0 10.8 %collective-permute-start.12 = (bf16[288,256]{1,0:T(8,128)(2,1)S(1)}, bf16[288,256]{1,0:T(8,128)(2,1)S(1)}, u32[]{:S(2)}, u32[]{:S(2)}) collective-permute-start(bf16[288,256]{1,0:T(8,128)(2,1)S(1)} %row_shares.3), channel_id=1, source_target_pairs={{0,8},{1,9},{2,10},{3,11},{4,12},{5,13},{6,14},{7,15},{8,0},{9,1},... | collective-permute-start | bytes 442376 | tf_op jit(solution)/shard_map/ppermute | solution.py:371
  32.5 7.3 %collective-permute-start.14 = (bf16[288,256]{1,0:T(8,128)(2,1)S(1)}, bf16[288,256]{1,0:T(8,128)(2,1)S(1)}, u32[]{:S(2)}, u32[]{:S(2)}) collective-permute-start(bf16[288,256]{1,0:T(8,128)(2,1)S(1)} %fold.4.refs_13_.refs_0_), channel_id=1, source_target_pairs={{0,4},{1,5},{2,6},{3,7},{4,0},{5,1},{6,2},{7,3},{8,12},{9,13},{10,... | collective-permute-start | bytes 442376 | tf_op jit(solution)/shard_map/ppermute | solution.py:371
  34.2 5.6 %collective-permute-start.15 = (bf16[288,256]{1,0:T(8,128)(2,1)S(1)}, bf16[288,256]{1,0:T(8,128)(2,1)S(1)}, u32[]{:S(2)}, u32[]{:S(2)}) collective-permute-start(bf16[288,256]{1,0:T(8,128)(2,1)S(1)} %fold.5), channel_id=1, source_target_pairs={{0,2},{1,3},{2,0},{3,1},{4,6},{5,7},{6,4},{7,5},{8,10},{9,11},{10,... | collective-permute-start | bytes 442376 | tf_op jit(solution)/shard_map/ppermute | solution.py:371
